TPU v7x, 256 devices: a whole 4x4x8 slice. The times are simulated.
256 devices in a mesh: view: 16 (over z_lo, x, core), render: 4 (over z_hi), head: 4 (over y).
Axes of the slice: x: 4, y: 4, z: 8 (z_hi: 4, z_lo: 2; z = z_hi * 2 + z_lo), core: 2. Of those that a mesh axis runs over, the one named last changes fastest.
Arguments:
- input_keys: bfloat16 [16384, 4096], P('view', 'head'), may hold values from -6 to 6
- input_values: bfloat16 [16384, 4096], P('view', 'head'), may hold values from -6 to 6
- token_rates: float32 [4, 16384], P('head', 'view'), may hold values from 0.00015625 to 0.0015625
- gate_weight: bfloat16 [4, 1024, 2048], P('head', None, 'render'), may hold values from -1.25 to 1.25
- up_weight: bfloat16 [4, 1024, 2048], P('head', None, 'render'), may hold values from -1.25 to 1.25
- down_weight: bfloat16 [4, 1024, 2048], P('head', None, 'render'), may hold values from -0.8838835 to 0.8838835
- queries: bfloat16 [16384, 4096], P(('view', 'render'), 'head'), may hold values from -6 to 6
Outputs:
- rendered: bfloat16 [16384, 4096], P(('view', 'render'), 'head')
All inputs are finite; a program needn't handle non-finite values.
Results may differ from a plain program's by a relative error of at most 0.04.
Values may be sent and summed in bfloat16 or wider, within the bound.
No kernel may reach another device: no remote copies, remote signals or barrier semaphores. Data moves between devices by JAX's collectives and lax.ppermute only.
A program may use at most 64 MiB of HBM per device.

v0:
```python
import jax
import jax.numpy as jnp
from jax import lax
from jax.sharding import PartitionSpec as P


def renorm(old, delta):
    old_wide = old.astype(jnp.float32)
    summed = old_wide + delta
    factor = jnp.sqrt(jnp.sum(old_wide * old_wide, axis=-2, keepdims=True)) / jnp.sqrt(
        jnp.sum(summed * summed, axis=-2, keepdims=True) + 1e-06
    )
    return (summed * factor).astype(jnp.bfloat16)


def contract_rows(left, right):
    return lax.dot_general(
        left, right, (((0,), (0,)), ((), ())), preferred_element_type=jnp.float32
    )


def render_rows(query_rows, piece_gate, piece_up, piece_down):
    gate_q = jnp.dot(query_rows, piece_gate, preferred_element_type=jnp.float32)
    up_q = jnp.dot(query_rows, piece_up, preferred_element_type=jnp.float32)
    hidden_q = (gate_q * jax.nn.sigmoid(gate_q) * up_q).astype(jnp.bfloat16)
    return lax.dot_general(
        hidden_q, piece_down, (((1,), (1,)), ((), ())), preferred_element_type=jnp.float32
    )


def local(input_keys, input_values, token_rates, gate_weight, up_weight, down_weight, queries):
    rate_col = token_rates[0][:, None]
    gate_out = jnp.dot(input_keys, gate_weight[0], preferred_element_type=jnp.float32)
    up_out = jnp.dot(input_keys, up_weight[0], preferred_element_type=jnp.float32)
    sigmoid_gate = jax.nn.sigmoid(gate_out)
    activated = gate_out * sigmoid_gate
    hidden = (activated * up_out).astype(jnp.bfloat16)
    scaled_values = (rate_col * input_values.astype(jnp.float32)).astype(jnp.bfloat16)
    grad_down = contract_rows(scaled_values, hidden)[None]
    back_grad = jnp.dot(input_values, down_weight[0], preferred_element_type=jnp.float32)
    pre_gate = (
        rate_col * back_grad * up_out * sigmoid_gate * (1.0 + gate_out * (1.0 - sigmoid_gate))
    ).astype(jnp.bfloat16)
    pre_up = (rate_col * back_grad * activated).astype(jnp.bfloat16)
    grad_down = lax.psum(grad_down.astype(jnp.bfloat16), "view").astype(jnp.float32)
    grad_gate = contract_rows(input_keys, pre_gate)[None]
    grad_up = contract_rows(input_keys, pre_up)[None]
    grad_gate, grad_up = (
        lax.psum(grad_gate.astype(jnp.bfloat16), "view").astype(jnp.float32),
        lax.psum(grad_up.astype(jnp.bfloat16), "view").astype(jnp.float32),
    )
    new_gate = renorm(gate_weight, grad_gate)
    new_up = renorm(up_weight, grad_up)
    new_down = renorm(down_weight, grad_down)
    running = render_rows(
        queries,
        lax.all_gather(new_gate, "render", axis=2, tiled=True)[0],
        lax.all_gather(new_up, "render", axis=2, tiled=True)[0],
        lax.all_gather(new_down, "render", axis=2, tiled=True)[0],
    )
    return running.astype(jnp.bfloat16)


def solution(mesh):
    return jax.shard_map(
        local,
        mesh=mesh,
        in_specs=(
            P("view", "head"),
            P("view", "head"),
            P("head", "view"),
            P("head", None, "render"),
            P("head", None, "render"),
            P("head", None, "render"),
            P(("view", "render"), "head"),
        ),
        out_specs=P(("view", "render"), "head"),
        check_vma=False,
    )
```

profile of v0, /device:TPU:1, one launch (start us, length us, event | category | flops | bytes accessed | tf_op | source)
XLA Modules:
  0.0 428.2 jit_solution(297411898883113179)
XLA Ops:
  6.5 0.0 copy-start
  6.5 0.0 copy-start.7
  6.5 0.0 all-reduce.3.cloned.1.call-start
  6.5 1.6 copy-done
  8.1 2.5 fusion.31
  10.6 0.0 copy-done.7
  10.6 0.0 copy-start.2
  10.6 0.0 copy-start.8
  10.6 1.2 fusion.33
  11.9 0.0 copy-done.2
  11.9 0.6 copy-done.8
  12.5 0.0 copy-start.10
  12.5 1.2 fusion.35
  13.8 0.0 copy-done.10
  13.8 2.6 fusion.26
  16.4 2.7 fusion.25
  19.1 2.6 fusion.27
  21.7 0.0 copy-start.6
  21.7 0.0 all-reduce.3.cloned.1.call-update
  21.7 0.0 all-gather.4.cloned.1.call-start
  21.8 1.1 copy-done.6
  22.9 1.3 copy.8
  24.3 1.5 copy.9
  25.7 130.5 %all-reduce.3.cloned.1.call-done = (bf16[1,1024,512]{2,1,0:T(8,128)(2,1)}, bf16[1,1024,512]{1,2,0:T(8,128)(2,1)}, bf16[1,1024,512]{1,2,0:T(8,128)(2,1)}) async-done(((bf16[1,1024,512]{2,1,0:T(8,128)(2,1)}, bf16[1,1024,512]{1,2,0:T(8,128)(2,1)}, bf16[1,1024,512]{1,2,0:T(8,128)(2,1)}), (bf16[1,1024,512]{2,1,0:T(8,128)(2,1)}, bf16[1,1024,512]{1,2,0:T(8,128)(2,1)}, ...) | async-done | bytes 3145744 | tf_op jit(solution)/shard_map/psum | solution.py:45
  156.2 0.0 copy-start.1
  156.3 0.0 copy-start.5
  156.3 3.0 fusion.18
  159.3 0.0 copy-done.1
  159.3 0.0 copy-done.5
  159.3 1.4 multiply_convert_fusion.6
  160.7 0.0 all-gather.4.cloned.1.call-update
  160.7 0.0 all-gather.6.cloned.1.call-start
  160.8 2.5 multiply_convert_fusion.4
  163.3 0.0 copy-start.3
  163.3 0.0 all-gather.6.cloned.1.call-update
  163.4 0.2 all-gather.8.cloned.1.call-start
  163.6 0.0 copy-start.4
  163.6 2.1 fusion.20
  165.8 0.0 copy-done.3
  165.8 0.0 copy-done.4
  165.8 1.3 multiply_convert_fusion.2
  167.1 0.0 all-gather.8.cloned.1.call-update
  167.1 0.0 copy-start.9
  167.1 72.7 %all-gather.4.cloned.1.call-done = bf16[1,1024,2048]{1,2,0:T(8,128)(2,1)} async-done(((bf16[1,1024,512]{1,2,0:T(8,128)(2,1)}), bf16[1,1024,2048]{1,2,0:T(8,128)(2,1)}) %all-gather.4.cloned.1.call-update) | async-done | bytes 4194320 | tf_op jit(solution)/shard_map/all_gather | solution.py:57
  239.8 4.9 %fusion.6 = f32[256,2048]{0,1:T(8,128)} fusion(bf16[256,1024]{1,0:T(8,128)(2,1)} %param.13, bf16[1,1024,2048]{1,2,0:T(8,128)(2,1)} %all-gather.4.cloned.1.call-done), kind=kOutput, calls=%fused_computation.7 | convolution fusion | flops 1073741824 | bytes 6815744 | tf_op jit(solution)/shard_map/dot_general | solution.py:23
  244.8 81.5 %all-gather.6.cloned.1.call-done = bf16[1,1024,2048]{1,2,0:T(8,128)(2,1)} async-done(((bf16[1,1024,512]{1,2,0:T(8,128)(2,1)}), bf16[1,1024,2048]{1,2,0:T(8,128)(2,1)}) %all-gather.6.cloned.1.call-update) | async-done | bytes 4194320 | tf_op jit(solution)/shard_map/all_gather | solution.py:58
  326.3 86.2 %all-gather.8.cloned.1.call-done = bf16[1,1024,2048]{2,1,0:T(8,128)(2,1)} async-done(((bf16[1,1024,512]{2,1,0:T(8,128)(2,1)}), bf16[1,1024,2048]{2,1,0:T(8,128)(2,1)}) %all-gather.8.cloned.1.call-update) | async-done | bytes 4194320 | tf_op jit(solution)/shard_map/all_gather | solution.py:59
  412.5 0.0 copy-done.9
  412.5 9.1 %fusion.28 = bf16[256,1024]{1,0:T(8,128)(2,1)} fusion(bf16[1,1024,2048]{2,1,0:T(8,128)(2,1)} %all-gather.8.cloned.1.call-done, bf16[256,1024]{1,0:T(8,128)(2,1)S(1)} %copy-done.9, bf16[1,1024,2048]{1,2,0:T(8,128)(2,1)} %all-gather.6.cloned.1.call-done, f32[256,2048]{0,1:T(8,128)} %fusion.6), kind=kOutput, calls=%fused_computation.39 | convolution fusion | flops 2150891520 | bytes 11534336 | tf_op jit(solution)/shard_map/dot_general | solution.py:26
  (3 shorter events, 0.0 us)
Async XLA Ops:
  6.5 1.6 copy-start
  6.5 4.1 copy-start.7
  6.5 149.7 %all-reduce.3.cloned.1.call-start = ((), (), s32[]{:S(2)}) async-start(), calls=%async_computation.3 | async-start | bytes 6291456 | tf_op jit(solution)/shard_map/psum | solution.py:45
  10.6 1.3 copy-start.2
  10.6 1.9 copy-start.8
  12.5 1.3 copy-start.10
  21.7 1.2 copy-start.6
  21.7 218.1 %all-gather.4.cloned.1.call-start = ((), (), s32[]{:S(2)}) async-start(), calls=%async_computation | async-start | bytes 5242880 | tf_op jit(solution)/shard_map/all_gather | solution.py:57
  156.2 3.1 copy-start.1
  156.3 3.1 copy-start.5
  160.7 165.5 %all-gather.6.cloned.1.call-start = ((), (), s32[]{:S(2)}) async-start(), calls=%async_computation.1 | async-start | bytes 5242880 | tf_op jit(solution)/shard_map/all_gather | solution.py:58
  163.3 2.4 copy-start.3
  163.4 249.1 %all-gather.8.cloned.1.call-start = ((), (), s32[]{:S(2)}) async-start(), calls=%async_computation.2 | async-start | bytes 5242880 | tf_op jit(solution)/shard_map/all_gather | solution.py:59
  163.6 2.2 copy-start.4
  167.1 245.4 %copy-start.9 = (bf16[256,1024]{1,0:T(8,128)(2,1)S(1)}, bf16[256,1024]{1,0:T(8,128)(2,1)}, u32[]{:S(2)}) copy-start(bf16[256,1024]{1,0:T(8,128)(2,1)} %param.13) | copy-start | bytes 1572868
Sparse Core Ops, SparseCore 0:
  21.8 134.3 all-reduce.2
  160.8 78.9 all-gather.3
  241.7 84.5 all-gather.5
  327.9 84.5 all-gather.7
where the time goes:
time: 436 us; the launch traced here: 428 us
  waiting for transfers between devices  371 us (85%)
  matrix products  26.9 us (6%)
  between operations  13.3 us (3%)
  other arithmetic  10.4 us (2%)
  local copies, waits for them, and re-layouts  6.24 us (1%)
    psum x1, waiting for transfers between devices, local(): lax.psum(grad_down.astype(jnp.bfloat16), 'view').astype(jnp.float32)  130 us
    all_gather x1, waiting for transfers between devices, local(): lax.all_gather(new_down, 'render', axis=2, tiled=True)[0]  86.2 us
    all_gather x1, waiting for transfers between devices, local(): lax.all_gather(new_up, 'render', axis=2, tiled=True)[0]  81.5 us
    all_gather x1, waiting for transfers between devices, local(): lax.all_gather(new_gate, 'render', axis=2, tiled=True)[0]  72.7 us
    dot_general x1, matrix products, render_rows(): lax.dot_general(hidden_q, piece_down, (((1,), (1,)), ((), ())), preferred...  9.14 us
  transfers between devices with their start and end apart: 4, of which 4 were waited for; matrix products, arithmetic and copies ran while one was open for 3% of the time, Pallas kernels for 0%

commit v1 on v0

v1 whole, which is shorter than its diff:
```python
import jax
import jax.numpy as jnp
from jax import lax
from jax.sharding import PartitionSpec as P

AXES = ("view", "render")
LZ, NX, NC, HZ = 2, 4, 2, 4
NZ = LZ * HZ
F32 = jnp.float32
BF16 = jnp.bfloat16


def move(array, target):
    pairs = []
    for zl in range(LZ):
        for x in range(NX):
            for core in range(NC):
                for zh in range(HZ):
                    tl, tx, tc, th = target(zl, x, core, zh)
                    pairs.append(
                        (((zl * NX + x) * NC + core) * HZ + zh, ((tl * NX + tx) * NC + tc) * HZ + th)
                    )
    return lax.ppermute(array, AXES, pairs)


def along_x(array, step):
    return move(array, lambda zl, x, c, zh: (zl, (x + step) % NX, c, zh))


def along_z(array, step):
    def target(zl, x, c, zh):
        z = (zh * LZ + zl + step) % NZ
        return z % LZ, x, c, z // LZ

    return move(array, target)


def swap_core(array):
    return move(array, lambda zl, x, c, zh: (zl, x, 1 - c, zh))


def swap_pair(array):
    return move(array, lambda zl, x, c, zh: (1 - zl, x, c, zh))


def pick(array, index, axis=0):
    return lax.dynamic_index_in_dim(array, index, axis, keepdims=False)


def add(*terms):
    total = terms[0].astype(F32)
    for term in terms[1:]:
        total = total + term.astype(F32)
    return total


def local(input_keys, input_values, token_rates, gate_weight, up_weight, down_weight, queries):
    view = lax.axis_index("view")
    zl, x, core = view // (NX * NC), (view // NC) % NX, view % NC
    tokens, width = input_keys.shape
    units = gate_weight.shape[2]
    own_units = units // (NC * NX * LZ)

    rate_col = token_rates[0][:, None]
    gate_out = jnp.dot(input_keys, gate_weight[0], preferred_element_type=F32)
    up_out = jnp.dot(input_keys, up_weight[0], preferred_element_type=F32)
    sigmoid_gate = jax.nn.sigmoid(gate_out)
    activated = gate_out * sigmoid_gate
    hidden = (activated * up_out).astype(BF16)
    scaled_values = (rate_col * input_values.astype(F32)).astype(BF16)
    back_grad = jnp.dot(input_values, down_weight[0], preferred_element_type=F32)
    pre_gate = (
        rate_col * back_grad * up_out * sigmoid_gate * (1.0 + gate_out * (1.0 - sigmoid_gate))
    ).astype(BF16)
    pre_up = (rate_col * back_grad * activated).astype(BF16)

    def delta(left, right):
        full = lax.dot_general(left, right, (((0,), (0,)), ((), ())), preferred_element_type=F32)
        return full.reshape(NC, NX, LZ, own_units, width).astype(BF16)

    def reduce_x(part):
        mine = pick(part, core)
        chip = add(mine, swap_core(pick(part, 1 - core))).astype(BF16)
        got = [along_x(pick(chip, (x + step) % NX), step) for step in (2, 1, 3)]
        return add(pick(chip, x), *got)

    sums = [
        reduce_x(delta(hidden, scaled_values)),
        reduce_x(delta(pre_gate, input_keys)),
        reduce_x(delta(pre_up, input_keys)),
    ]
    both = jnp.stack([sums[1], sums[2], sums[0]], 1).astype(BF16)
    mine = add(pick(both, zl), swap_pair(pick(both, 1 - zl)))

    offset = ((core * NX + x) * LZ + zl) * own_units
    old = jnp.stack(
        [
            lax.dynamic_slice_in_dim(w[0], offset, own_units, 1).T
            for w in (gate_weight, up_weight, down_weight)
        ]
    ).astype(F32)
    summed = old + mine
    factor = jnp.sqrt(jnp.sum(old * old, axis=-1, keepdims=True)) / jnp.sqrt(
        jnp.sum(summed * summed, axis=-1, keepdims=True) + 1e-06
    )
    new = (summed * factor).astype(BF16)

    pieces = [new]
    up_way, down_way = new, new
    for _ in range(NZ // 2 - 1):
        up_way, down_way = along_z(up_way, 1), along_z(down_way, -1)
        pieces += [up_way, down_way]
    half = own_units // 2
    pieces.append(
        jnp.concatenate([along_z(up_way[:, :half], 1), along_z(down_way[:, half:], -1)], 1)
    )
    here = jnp.concatenate(pieces, 1)
    weights = jnp.concatenate([here, swap_core(here)], 1)

    query_rows = [queries] + [along_x(queries, -step) for step in (2, 1, 3)]
    outs = []
    for rows in query_rows:
        gate_q = lax.dot_general(rows, weights[0], (((1,), (1,)), ((), ())), preferred_element_type=F32)
        up_q = lax.dot_general(rows, weights[1], (((1,), (1,)), ((), ())), preferred_element_type=F32)
        hidden_q = (gate_q * jax.nn.sigmoid(gate_q) * up_q).astype(BF16)
        outs.append(jnp.dot(hidden_q, weights[2], preferred_element_type=F32))
    got = [along_x(out.astype(BF16), step) for out, step in zip(outs[1:], (2, 1, 3))]
    return add(outs[0], *got).astype(BF16)


def solution(mesh):
    return jax.shard_map(
        local,
        mesh=mesh,
        in_specs=(
            P("view", "head"),
            P("view", "head"),
            P("head", "view"),
            P("head", None, "render"),
            P("head", None, "render"),
            P("head", None, "render"),
            P(("view", "render"), "head"),
        ),
        out_specs=P(("view", "render"), "head"),
        check_vma=False,
    )
```

time: 436 us -> 143 us (0.33); the launches traced: 428 us -> 140 us
  waiting for transfers between devices: 371 us -> 44 us
  starting transfers between devices: 0.31 us -> 43.8 us
  between operations: 13.3 us -> 0.34 us
  matrix products: 26.9 us -> 39.6 us
  other arithmetic: 10.4 us -> 4.52 us
    all_gather x3 -> x0, waiting for transfers between devices: 240 us -> none  [the longest x1 86.2 us: local(): lax.all_gather(new_down, 'render', axis=2, tiled=True)[0]]
    psum x1 -> x0, waiting for transfers between devices: 130 us -> none  [local(): lax.psum(grad_down.astype(jnp.bfloat16), 'view').astype(jnp.float32)]
    ppermute x0 -> x28, waiting for transfers between devices: none -> 44 us  [move(): return lax.ppermute(array, AXES, pairs)]
    ppermute x0 -> x28, starting transfers between devices: none -> 43.8 us  [move(): return lax.ppermute(array, AXES, pairs)]
    dot_general x8 -> x14, matrix products: 26.9 us -> 39.6 us  [the longest x4 16.1 us: local(): outs.append(jnp.dot(hidden_q, weights[2], preferred_element_type=F32))]
    reduce_sum x2 -> x1, other arithmetic: 5.18 us -> 0.19 us  [local(): jnp.sum(old * old, axis=-1, keepdims=True)]
  transfers between devices with their start and end apart: 4 -> 28, of which waited for: 4 -> 14; matrix products, arithmetic and copies ran while one was open for 3% -> 24% of each run, Pallas kernels for 0% -> 0%
where the time goes in v1:
time: 143 us; the launch traced here: 140 us
  waiting for transfers between devices  44 us (31%)
  starting transfers between devices  43.8 us (31%)
  matrix products  39.6 us (28%)
  local copies, waits for them, and re-layouts  7.81 us (5%)
  other arithmetic  4.52 us (3%)
    ppermute x28, waiting for transfers between devices, move(): return lax.ppermute(array, AXES, pairs)  44 us
    ppermute x28, starting transfers between devices, move(): return lax.ppermute(array, AXES, pairs)  43.8 us
    dot_general x4, matrix products, local(): outs.append(jnp.dot(hidden_q, weights[2], preferred_element_type=F32))  16.1 us
    dot_general x3, matrix products, local(): lax.dot_general(rows, weights[1], (((1,), (1,)), ((), ())), preferred_ele...  6.53 us
    dot_general x3, matrix products, delta(): lax.dot_general(left, right, (((0,), (0,)), ((), ())), preferred_element_...  4.95 us
    convert_element_type x3, other arithmetic, reduce_x(): chip = add(mine, swap_core(pick(part, 1 - core))).astype(BF16)  3.94 us
    dot_general x1, matrix products, local(): gate_out = jnp.dot(input_keys, gate_weight[0], preferred_element_type=F32)  3.9 us
    dot_general x1, matrix products, local(): jnp.dot(input_values, down_weight[0], preferred_element_type=F32)  2.98 us
  transfers between devices with their start and end apart: 28, of which 14 were waited for; matrix products, arithmetic and copies ran while one was open for 24% of the time, Pallas kernels for 0%

profile of v1, /device:TPU:1, one launch (start us, length us, event | category | flops | bytes accessed | tf_op | source)
XLA Modules:
  0.0 140.1 jit_solution(7530406625523755093)
XLA Ops:
  0.0 1.6 %copy-done = bf16[1024,1024]{1,0:T(8,128)(2,1)S(1)} copy-done((bf16[1024,1024]{1,0:T(8,128)(2,1)S(1)}, bf16[1024,1024]{1,0:T(8,128)(2,1)}, u32[]{:S(2)}) %copy-start) | copy-done | bytes 2097176
  1.6 3.9 %fusion.12 = f32[1024,512]{1,0:T(8,128)} fusion(bf16[1024,1024]{1,0:T(8,128)(2,1)S(1)} %copy-done, bf16[1,1024,512]{2,1,0:T(8,128)(2,1)} %param.10), kind=kOutput, calls=%fused_computation.37 | convolution fusion | flops 1073741824 | bytes 5242880 | tf_op jit(solution)/shard_map/dot_general | solution.py:65
  5.5 2.6 %fusion.14 = f32[1024,512]{1,0:T(8,128)} fusion(bf16[1024,1024]{1,0:T(8,128)(2,1)S(1)} %copy-done, bf16[1,1024,512]{2,1,0:T(8,128)(2,1)S(1)} %copy-done.5), kind=kOutput, calls=%fused_computation.39 | convolution fusion | flops 1073741824 | bytes 5242880 | tf_op jit(solution)/shard_map/dot_general | solution.py:66
  8.1 3.0 %fusion.16 = f32[1024,512]{1,0:T(8,128)S(1)} fusion(bf16[1024,1024]{1,0:T(8,128)(2,1)} %param.8, bf16[1,1024,512]{2,1,0:T(8,128)(2,1)S(1)} %copy-done.4), kind=kOutput, calls=%fused_computation.41 | convolution fusion | flops 1073741824 | bytes 5242880 | tf_op jit(solution)/shard_map/dot_general | solution.py:71
  11.1 1.8 %convolution_convert_fusion.1 = bf16[512,1024]{1,0:T(8,128)(2,1)S(1)} fusion(bf16[1024,1024]{1,0:T(8,128)(2,1)S(1)} %copy-done, f32[1024,512]{1,0:T(8,128)S(1)} %copy-done.10, f32[1024,512]{1,0:T(8,128)S(1)} %copy-done.11, f32[1024,512]{1,0:T(8,128)S(1)} %fusion.16, f32[1024]{0:T(1024)S(1)} %bitcast.173), kind=kOutput, calls=%fused_computation.10 | convolution fusion | flops 1080033280 | bytes 9441280 | tf_op jit(solution)/shard_map/dot_general | solution.py:78
  12.9 0.9 dynamic-slice_bitcast_fusion.2
  13.9 3.3 %collective-permute-start = (bf16[4,2,32,1024]{3,2,1,0:T(8,128)(2,1)}, bf16[4,2,32,1024]{3,2,1,0:T(8,128)(2,1)}, u32[]{:S(2)}, u32[]{:S(2)}) collective-permute-start(bf16[4,2,32,1024]{3,2,1,0:T(8,128)(2,1)} %dynamic-slice_bitcast_fusion.2), channel_id=1, source_target_pairs={{0,16},{4,20},{8,24},{12,28},{16,0},{20,4},{24,8},{28,12},{32,48},... | collective-permute-start | bytes 1572872 | tf_op jit(solution)/shard_map/ppermute | solution.py:23
  17.1 1.6 %convolution_convert_fusion = bf16[512,1024]{1,0:T(8,128)(2,1)S(1)} fusion(bf16[1024,1024]{1,0:T(8,128)(2,1)S(1)} %copy-done, f32[1024,512]{1,0:T(8,128)S(1)} %fusion.16, f32[1024]{0:T(1024)S(1)} %bitcast.174, f32[1024,512]{1,0:T(8,128)S(1)} %copy-done.10), kind=kOutput, calls=%fused_computation.9 | convolution fusion | flops 1077936128 | bytes 7344128 | tf_op jit(solution)/shard_map/dot_general | solution.py:78
  18.7 0.9 dynamic-slice_bitcast_fusion.1
  19.6 0.3 copy-done.1
  19.9 1.6 %fusion.3 = bf16[512,1024]{1,0:T(8,128)(2,1)S(1)} fusion(bf16[1024,1024]{1,0:T(8,128)(2,1)S(1)} %copy-done.7, f32[1024]{0:T(1024)S(1)} %bitcast.175, f32[1024,512]{1,0:T(8,128)S(1)} %copy-done.11, f32[1024,512]{1,0:T(8,128)S(1)} %copy-done.10), kind=kOutput, calls=%fused_computation.8 | convolution fusion | flops 1080557568 | bytes 7344128 | tf_op jit(solution)/shard_map/dot_general | solution.py:78
  21.5 0.9 dynamic-slice_bitcast_fusion
  22.4 0.5 collective-permute-start.8
  22.9 1.5 %fusion.11 = bf16[4,2,32,1024]{3,2,1,0:T(8,128)(2,1)S(1)} fusion(bf16[4,2,32,1024]{3,2,1,0:T(8,128)(2,1)} %collective-permute-done, bf16[2,4,2,32,1024]{4,3,2,1,0:T(8,128)(2,1)} %bitcast.166, s32[]{:T(128)S(6)} %select_n.91), kind=kLoop, calls=%fused_computation.36 | loop fusion | flops 1048576 | bytes 1572868 | tf_op jit(solution)/shard_map/convert_element_type | solution.py:83
  24.4 1.1 collective-permute-start.1
  25.5 0.3 collective-permute-start.2
  25.8 2.4 %collective-permute-start.3 = (bf16[2,32,1024]{2,1,0:T(8,128)(2,1)S(1)}, bf16[2,32,1024]{2,1,0:T(8,128)(2,1)S(1)}, u32[]{:S(2)}, u32[]{:S(2)}) collective-permute-start(bf16[2,32,1024]{2,1,0:T(8,128)(2,1)S(1)} %get-tuple-element.10), channel_id=1, source_target_pairs={{0,96},{4,100},{8,104},{12,108},{16,112},{20,116},{24,120},{28,124... | collective-permute-start | bytes 393224 | tf_op jit(solution)/shard_map/ppermute | solution.py:23
  28.2 1.2 fusion.10
  29.5 0.8 collective-permute-start.5
  30.3 1.2 fusion.9
  31.6 2.8 %collective-permute-start.7 = (bf16[2,32,1024]{2,1,0:T(8,128)(2,1)S(1)}, bf16[2,32,1024]{2,1,0:T(8,128)(2,1)S(1)}, u32[]{:S(2)}, u32[]{:S(2)}) collective-permute-start(bf16[2,32,1024]{2,1,0:T(8,128)(2,1)S(1)} %get-tuple-element.13), channel_id=1, source_target_pairs={{0,96},{4,100},{8,104},{12,108},{16,112},{20,116},{24,120},{28,124... | collective-permute-start | bytes 393224 | tf_op jit(solution)/shard_map/ppermute | solution.py:23
  34.4 0.2 collective-permute-done.2
  34.6 2.7 %collective-permute-start.11 = (bf16[2,32,1024]{2,1,0:T(8,128)(2,1)S(1)}, bf16[2,32,1024]{2,1,0:T(8,128)(2,1)S(1)}, u32[]{:S(2)}, u32[]{:S(2)}) collective-permute-start(bf16[2,32,1024]{2,1,0:T(8,128)(2,1)S(1)} %get-tuple-element.16), channel_id=1, source_target_pairs={{0,96},{4,100},{8,104},{12,108},{16,112},{20,116},{24,120},{28,124... | collective-permute-start | bytes 393224 | tf_op jit(solution)/shard_map/ppermute | solution.py:23
  37.3 0.4 collective-permute-start.9
  37.7 2.1 %collective-permute-done.6 = bf16[2,32,1024]{2,1,0:T(8,128)(2,1)S(1)} collective-permute-done((bf16[2,32,1024]{2,1,0:T(8,128)(2,1)S(1)}, bf16[2,32,1024]{2,1,0:T(8,128)(2,1)S(1)}, u32[]{:S(2)}, u32[]{:S(2)}) %collective-permute-start.6) | collective-permute-done | bytes 131104 | tf_op jit(solution)/shard_map/ppermute | solution.py:23
  39.8 2.5 %collective-permute-done.10 = bf16[2,32,1024]{2,1,0:T(8,128)(2,1)S(1)} collective-permute-done((bf16[2,32,1024]{2,1,0:T(8,128)(2,1)S(1)}, bf16[2,32,1024]{2,1,0:T(8,128)(2,1)S(1)}, u32[]{:S(2)}, u32[]{:S(2)}) %collective-permute-start.10) | collective-permute-done | bytes 131104 | tf_op jit(solution)/shard_map/ppermute | solution.py:23
  42.4 1.9 %collective-permute-done.9 = bf16[2,32,1024]{2,1,0:T(8,128)(2,1)S(1)} collective-permute-done((bf16[2,32,1024]{2,1,0:T(8,128)(2,1)S(1)}, bf16[2,32,1024]{2,1,0:T(8,128)(2,1)S(1)}, u32[]{:S(2)}, u32[]{:S(2)}) %collective-permute-start.9) | collective-permute-done | bytes 131104 | tf_op jit(solution)/shard_map/ppermute | solution.py:23
  44.4 1.3 collective-permute-start.12
  45.7 1.2 constant_dynamic-slice_fusion
  47.0 0.1 copy.12
  47.1 0.1 copy.13
  47.2 1.1 constant_dynamic-slice_fusion.2
  48.4 0.6 collective-permute-done.12
  49.0 0.2 fusion.24
  49.3 1.3 collective-permute-start.13
  50.6 4.0 %collective-permute-start.14 = (bf16[3,32,1024]{2,1,0:T(8,128)(2,1)S(1)}, bf16[3,32,1024]{2,1,0:T(8,128)(2,1)S(1)}, u32[]{:S(2)}, u32[]{:S(2)}) collective-permute-start(bf16[3,32,1024]{2,1,0:T(8,128)(2,1)S(1)} %get-tuple-element.8), channel_id=1, source_target_pairs={{0,140},{4,128},{8,132},{12,136},{16,156},{20,144},{24,148},{28,15... | collective-permute-start | bytes 589832 | tf_op jit(solution)/shard_map/ppermute | solution.py:23
  54.7 3.0 %collective-permute-done.13 = bf16[3,32,1024]{2,1,0:T(8,128)(2,1)S(1)} collective-permute-done((bf16[3,32,1024]{2,1,0:T(8,128)(2,1)S(1)}, bf16[3,32,1024]{2,1,0:T(8,128)(2,1)S(1)}, u32[]{:S(2)}, u32[]{:S(2)}) %collective-permute-start.13) | collective-permute-done | bytes 196640 | tf_op jit(solution)/shard_map/ppermute | solution.py:23
  57.6 2.8 %collective-permute-start.16 = (bf16[3,32,1024]{2,1,0:T(8,128)(2,1)S(1)}, bf16[3,32,1024]{2,1,0:T(8,128)(2,1)S(1)}, u32[]{:S(2)}, u32[]{:S(2)}) collective-permute-start(bf16[3,32,1024]{2,1,0:T(8,128)(2,1)S(1)} %collective-permute-done.14), channel_id=1, source_target_pairs={{0,140},{4,128},{8,132},{12,136},{16,156},{20,144},{24,148},{28,15... | collective-permute-start | bytes 589832 | tf_op jit(solution)/shard_map/ppermute | solution.py:23
  60.5 2.9 %collective-permute-done.15 = bf16[3,32,1024]{2,1,0:T(8,128)(2,1)S(1)} collective-permute-done((bf16[3,32,1024]{2,1,0:T(8,128)(2,1)S(1)}, bf16[3,32,1024]{2,1,0:T(8,128)(2,1)S(1)}, u32[]{:S(2)}, u32[]{:S(2)}) %collective-permute-start.15) | collective-permute-done | bytes 196640 | tf_op jit(solution)/shard_map/ppermute | solution.py:23
  63.4 2.8 %collective-permute-start.18 = (bf16[3,32,1024]{2,1,0:T(8,128)(2,1)S(1)}, bf16[3,32,1024]{2,1,0:T(8,128)(2,1)S(1)}, u32[]{:S(2)}, u32[]{:S(2)}) collective-permute-start(bf16[3,32,1024]{2,1,0:T(8,128)(2,1)S(1)} %collective-permute-done.16), channel_id=1, source_target_pairs={{0,140},{4,128},{8,132},{12,136},{16,156},{20,144},{24,148},{28,15... | collective-permute-start | bytes 589832 | tf_op jit(solution)/shard_map/ppermute | solution.py:23
  66.2 3.4 %collective-permute-done.17 = bf16[3,32,1024]{2,1,0:T(8,128)(2,1)S(1)} collective-permute-done((bf16[3,32,1024]{2,1,0:T(8,128)(2,1)S(1)}, bf16[3,32,1024]{2,1,0:T(8,128)(2,1)S(1)}, u32[]{:S(2)}, u32[]{:S(2)}) %collective-permute-start.17) | collective-permute-done | bytes 196640 | tf_op jit(solution)/shard_map/ppermute | solution.py:23
  69.7 3.0 %collective-permute-start.20 = (bf16[3,16,1024]{2,1,0:T(8,128)(2,1)S(1)}, bf16[3,16,1024]{2,1,0:T(8,128)(2,1)S(1)}, u32[]{:S(2)}, u32[]{:S(2)}) collective-permute-start(bf16[3,16,1024]{2,1,0:T(8,128)(2,1)S(1)} %slice.30), channel_id=1, source_target_pairs={{0,140},{4,128},{8,132},{12,136},{16,156},{20,144},{24,148},{28,15... | collective-permute-start | bytes 294920 | tf_op jit(solution)/shard_map/ppermute | solution.py:23
  72.8 2.9 %collective-permute-done.19 = bf16[3,16,1024]{2,1,0:T(8,128)(2,1)S(1)} collective-permute-done((bf16[3,16,1024]{2,1,0:T(8,128)(2,1)S(1)}, bf16[3,16,1024]{2,1,0:T(8,128)(2,1)S(1)}, u32[]{:S(2)}, u32[]{:S(2)}) %collective-permute-start.19) | collective-permute-done | bytes 98336 | tf_op jit(solution)/shard_map/ppermute | solution.py:23
  75.7 6.9 %collective-permute-start.21 = (bf16[3,256,1024]{2,1,0:T(8,128)(2,1)S(1)}, bf16[3,256,1024]{2,1,0:T(8,128)(2,1)S(1)}, u32[]{:S(2)}, u32[]{:S(2)}) collective-permute-start(bf16[3,256,1024]{2,1,0:T(8,128)(2,1)S(1)} %get-tuple-element.30), channel_id=1, source_target_pairs={{0,16},{4,20},{8,24},{12,28},{16,0},{20,4},{24,8},{28,12},{32,48},... | collective-permute-start | bytes 4718600 | tf_op jit(solution)/shard_map/ppermute | solution.py:23
  82.6 1.3 collective-permute-start.22
  83.9 0.9 collective-permute-start.24
  84.8 0.6 collective-permute-start.26
  85.4 0.2 collective-permute-done.21
  85.6 0.1 constant_dynamic-update-slice_fusion.9
  85.8 11.6 %collective-permute-done.22 = bf16[256,1024]{1,0:T(8,128)(2,1)S(1)} collective-permute-done((bf16[256,1024]{1,0:T(8,128)(2,1)S(1)}, bf16[256,1024]{1,0:T(8,128)(2,1)S(1)}, u32[]{:S(2)}, u32[]{:S(2)}) %collective-permute-start.22) | collective-permute-done | bytes 524320 | tf_op jit(solution)/shard_map/ppermute | solution.py:23
  97.3 1.3 convolution_bitcast_fusion.4
  98.6 3.9 %convolution_convert_fusion.4 = bf16[256,1024]{1,0:T(8,128)(2,1)} fusion(bf16[3,512,1024]{2,1,0:T(8,128)(2,1)} %copy-done.6, f32[256,512]{0,1:T(8,128)} %convolution_bitcast_fusion.4, bf16[256,1024]{1,0:T(8,128)(2,1)S(1)} %collective-permute-done.22), kind=kOutput, calls=%fused_computation.16 | convolution fusion | flops 537919488 | bytes 3670016 | tf_op jit(solution)/shard_map/dot_general | solution.py:126
  102.5 1.3 collective-permute-start.23
  103.8 4.4 %collective-permute-done.24 = bf16[256,1024]{1,0:T(8,128)(2,1)} collective-permute-done((bf16[256,1024]{1,0:T(8,128)(2,1)S(1)}, bf16[256,1024]{1,0:T(8,128)(2,1)}, u32[]{:S(2)}, u32[]{:S(2)}) %collective-permute-start.24) | collective-permute-done | bytes 524320 | tf_op jit(solution)/shard_map/ppermute | solution.py:23
  108.3 2.6 %convolution_bitcast_fusion.2 = f32[256,512]{0,1:T(8,128)} fusion(bf16[256,1024]{1,0:T(8,128)(2,1)} %collective-permute-done.24, bf16[3,512,1024]{2,1,0:T(8,128)(2,1)} %copy-done.6), kind=kOutput, calls=%fused_computation.20 | convolution fusion | flops 268435456 | bytes 2097152 | tf_op jit(solution)/shard_map/dot_general | solution.py:124
  110.9 4.0 %convolution_convert_fusion.3 = bf16[256,1024]{1,0:T(8,128)(2,1)} fusion(bf16[3,512,1024]{2,1,0:T(8,128)(2,1)} %copy-done.6, f32[256,512]{0,1:T(8,128)} %convolution_bitcast_fusion.2, bf16[256,1024]{1,0:T(8,128)(2,1)} %collective-permute-done.24), kind=kOutput, calls=%fused_computation.15 | convolution fusion | flops 537919488 | bytes 3670016 | tf_op jit(solution)/shard_map/dot_general | solution.py:126
  114.9 1.5 %collective-permute-start.25 = (bf16[256,1024]{1,0:T(8,128)(2,1)}, bf16[256,1024]{1,0:T(8,128)(2,1)}, u32[]{:S(2)}, u32[]{:S(2)}) collective-permute-start(bf16[256,1024]{1,0:T(8,128)(2,1)} %convolution_convert_fusion.3), channel_id=1, source_target_pairs={{0,32},{4,36},{8,40},{12,44},{16,48},{20,52},{24,56},{28,60},{32,6... | collective-permute-start | bytes 1572872 | tf_op jit(solution)/shard_map/ppermute | solution.py:23
  116.4 2.6 %convolution_bitcast_fusion = f32[256,512]{0,1:T(8,128)} fusion(bf16[256,1024]{1,0:T(8,128)(2,1)} %collective-permute-done.26, bf16[3,512,1024]{2,1,0:T(8,128)(2,1)} %copy-done.6), kind=kOutput, calls=%fused_computation.18 | convolution fusion | flops 268435456 | bytes 2097152 | tf_op jit(solution)/shard_map/dot_general | solution.py:124
  119.0 4.0 %convolution_convert_fusion.2 = bf16[256,1024]{1,0:T(8,128)(2,1)} fusion(bf16[3,512,1024]{2,1,0:T(8,128)(2,1)} %copy-done.6, f32[256,512]{0,1:T(8,128)} %convolution_bitcast_fusion, bf16[256,1024]{1,0:T(8,128)(2,1)} %collective-permute-done.26), kind=kOutput, calls=%fused_computation.14 | convolution fusion | flops 537919488 | bytes 3670016 | tf_op jit(solution)/shard_map/dot_general | solution.py:126
  123.1 1.9 %collective-permute-start.27 = (bf16[256,1024]{1,0:T(8,128)(2,1)}, bf16[256,1024]{1,0:T(8,128)(2,1)}, u32[]{:S(2)}, u32[]{:S(2)}) collective-permute-start(bf16[256,1024]{1,0:T(8,128)(2,1)} %convolution_convert_fusion.2), channel_id=1, source_target_pairs={{0,96},{4,100},{8,104},{12,108},{16,112},{20,116},{24,120},{28,124... | collective-permute-start | bytes 1572872 | tf_op jit(solution)/shard_map/ppermute | solution.py:23
  125.0 2.5 %convolution_bitcast_fusion.7 = f32[256,512]{0,1:T(8,128)} fusion(bf16[256,1024]{1,0:T(8,128)(2,1)S(1)} %copy-done.8, bf16[3,512,1024]{2,1,0:T(8,128)(2,1)} %copy-done.6), kind=kOutput, calls=%fused_computation.26 | convolution fusion | flops 268435456 | bytes 2097152 | tf_op jit(solution)/shard_map/dot_general | solution.py:123
  127.5 3.5 %collective-permute-done.25 = bf16[256,1024]{1,0:T(8,128)(2,1)} collective-permute-done((bf16[256,1024]{1,0:T(8,128)(2,1)}, bf16[256,1024]{1,0:T(8,128)(2,1)}, u32[]{:S(2)}, u32[]{:S(2)}) %collective-permute-start.25) | collective-permute-done | bytes 524320 | tf_op jit(solution)/shard_map/ppermute | solution.py:23
  131.0 5.0 %collective-permute-done.27 = bf16[256,1024]{1,0:T(8,128)(2,1)} collective-permute-done((bf16[256,1024]{1,0:T(8,128)(2,1)}, bf16[256,1024]{1,0:T(8,128)(2,1)}, u32[]{:S(2)}, u32[]{:S(2)}) %collective-permute-start.27) | collective-permute-done | bytes 524320 | tf_op jit(solution)/shard_map/ppermute | solution.py:23
  135.9 4.1 %fusion.6 = bf16[256,1024]{1,0:T(8,128)(2,1)} fusion(bf16[256,1024]{1,0:T(8,128)(2,1)S(1)} %copy-done.8, bf16[256,1024]{1,0:T(8,128)(2,1)} %collective-permute-done.27, bf16[256,1024]{1,0:T(8,128)(2,1)} %collective-permute-done.25, bf16[256,1024]{1,0:T(8,128)(2,1)S(1)} %collective-permute-done.23, bf16[3,512,1024]{2,1,0:T(8,128)(2,1)} %copy-done.6, ...), kind=kOutput, calls=%fused_computation.17 | convolution fusion | flops 539492352 | bytes 5242880 | tf_op jit(solution)/shard_map/dot_general | solution.py:126
  (64 shorter events, 1.0 us)
Async XLA Ops:
  0.0 1.6 %copy-start = (bf16[1024,1024]{1,0:T(8,128)(2,1)S(1)}, bf16[1024,1024]{1,0:T(8,128)(2,1)}, u32[]{:S(2)}) copy-start(bf16[1024,1024]{1,0:T(8,128)(2,1)} %param.7) | copy-start | bytes 6291460
  1.6 3.9 %copy-start.5 = (bf16[1,1024,512]{2,1,0:T(8,128)(2,1)S(1)}, bf16[1,1024,512]{2,1,0:T(8,128)(2,1)}, u32[]{:S(2)}) copy-start(bf16[1,1024,512]{2,1,0:T(8,128)(2,1)} %param.11) | copy-start | bytes 3145732
  5.5 2.6 %copy-start.4 = (bf16[1,1024,512]{2,1,0:T(8,128)(2,1)S(1)}, bf16[1,1024,512]{2,1,0:T(8,128)(2,1)}, u32[]{:S(2)}) copy-start(bf16[1,1024,512]{2,1,0:T(8,128)(2,1)} %param.12) | copy-start | bytes 3145732
  8.1 3.0 %copy-start.9 = (f32[1,1024]{1,0:T(1,128)S(1)}, f32[1,1024]{1,0:T(1,128)}, u32[]{:S(2)}) copy-start(f32[1,1024]{1,0:T(1,128)} %param.9) | copy-start | bytes 12292
  8.1 3.0 %copy-start.10 = (f32[1024,512]{1,0:T(8,128)S(1)}, f32[1024,512]{1,0:T(8,128)}, u32[]{:S(2)}) copy-start(f32[1024,512]{1,0:T(8,128)} %fusion.12) | copy-start | bytes 6291460
  8.1 3.0 %copy-start.11 = (f32[1024,512]{1,0:T(8,128)S(1)}, f32[1024,512]{1,0:T(8,128)}, u32[]{:S(2)}) copy-start(f32[1024,512]{1,0:T(8,128)} %fusion.14) | copy-start | bytes 6291460
  12.9 5.8 %copy-start.3 = (bf16[512,1024]{1,0:T(8,128)(2,1)}, bf16[512,1024]{1,0:T(8,128)(2,1)S(1)}, u32[]{:S(2)}) copy-start(bf16[512,1024]{1,0:T(8,128)(2,1)S(1)} %convolution_convert_fusion.1) | copy-start | bytes 3145732
  13.8 6.1 %copy-start.7 = (bf16[1024,1024]{1,0:T(8,128)(2,1)S(1)}, bf16[1024,1024]{1,0:T(8,128)(2,1)}, u32[]{:S(2)}) copy-start(bf16[1024,1024]{1,0:T(8,128)(2,1)} %param.8) | copy-start | bytes 6291460
  13.9 9.0 %collective-permute-start = (bf16[4,2,32,1024]{3,2,1,0:T(8,128)(2,1)}, bf16[4,2,32,1024]{3,2,1,0:T(8,128)(2,1)}, u32[]{:S(2)}, u32[]{:S(2)}) collective-permute-start(bf16[4,2,32,1024]{3,2,1,0:T(8,128)(2,1)} %dynamic-slice_bitcast_fusion.2), channel_id=1, source_target_pairs={{0,16},{4,20},{8,24},{12,28},{16,0},{20,4},{24,8},{28,12},{32,48},... | collective-permute-start | bytes 1572872 | tf_op jit(solution)/shard_map/ppermute | solution.py:23
  18.7 1.2 copy-start.1
  19.9 8.3 %collective-permute-start.4 = (bf16[4,2,32,1024]{3,2,1,0:T(8,128)(2,1)}, bf16[4,2,32,1024]{3,2,1,0:T(8,128)(2,1)}, u32[]{:S(2)}, u32[]{:S(2)}) collective-permute-start(bf16[4,2,32,1024]{3,2,1,0:T(8,128)(2,1)} %dynamic-slice_bitcast_fusion.1), channel_id=1, source_target_pairs={{0,16},{4,20},{8,24},{12,28},{16,0},{20,4},{24,8},{28,12},{32,48},... | collective-permute-start | bytes 1572872 | tf_op jit(solution)/shard_map/ppermute | solution.py:23
  22.4 7.9 %collective-permute-start.8 = (bf16[4,2,32,1024]{3,2,1,0:T(8,128)(2,1)}, bf16[4,2,32,1024]{3,2,1,0:T(8,128)(2,1)}, u32[]{:S(2)}, u32[]{:S(2)}) collective-permute-start(bf16[4,2,32,1024]{3,2,1,0:T(8,128)(2,1)} %dynamic-slice_bitcast_fusion), channel_id=1, source_target_pairs={{0,16},{4,20},{8,24},{12,28},{16,0},{20,4},{24,8},{28,12},{32,48},... | collective-permute-start | bytes 1572872 | tf_op jit(solution)/shard_map/ppermute | solution.py:23
  22.9 5.3 %copy-start.2 = (bf16[512,1024]{1,0:T(8,128)(2,1)S(1)}, bf16[512,1024]{1,0:T(8,128)(2,1)}, u32[]{:S(2)}) copy-start(bf16[512,1024]{1,0:T(8,128)(2,1)} %copy-done.1) | copy-start | bytes 3145732
  24.4 7.2 %collective-permute-start.1 = (bf16[2,32,1024]{2,1,0:T(8,128)(2,1)S(1)}, bf16[2,32,1024]{2,1,0:T(8,128)(2,1)S(1)}, u32[]{:S(2)}, u32[]{:S(2)}) collective-permute-start(bf16[2,32,1024]{2,1,0:T(8,128)(2,1)S(1)} %get-tuple-element.9), channel_id=1, source_target_pairs={{0,64},{4,68},{8,72},{12,76},{16,80},{20,84},{24,88},{28,92},{32,9... | collective-permute-start | bytes 393224 | tf_op jit(solution)/shard_map/ppermute | solution.py:23
  25.5 9.1 %collective-permute-start.2 = (bf16[2,32,1024]{2,1,0:T(8,128)(2,1)S(1)}, bf16[2,32,1024]{2,1,0:T(8,128)(2,1)S(1)}, u32[]{:S(2)}, u32[]{:S(2)}) collective-permute-start(bf16[2,32,1024]{2,1,0:T(8,128)(2,1)S(1)} %get-tuple-element.11), channel_id=1, source_target_pairs={{0,32},{4,36},{8,40},{12,44},{16,48},{20,52},{24,56},{28,60},{32,6... | collective-permute-start | bytes 393224 | tf_op jit(solution)/shard_map/ppermute | solution.py:23
  25.8 8.8 %collective-permute-start.3 = (bf16[2,32,1024]{2,1,0:T(8,128)(2,1)S(1)}, bf16[2,32,1024]{2,1,0:T(8,128)(2,1)S(1)}, u32[]{:S(2)}, u32[]{:S(2)}) collective-permute-start(bf16[2,32,1024]{2,1,0:T(8,128)(2,1)S(1)} %get-tuple-element.10), channel_id=1, source_target_pairs={{0,96},{4,100},{8,104},{12,108},{16,112},{20,116},{24,120},{28,124... | collective-permute-start | bytes 393224 | tf_op jit(solution)/shard_map/ppermute | solution.py:23
  29.5 7.8 %collective-permute-start.5 = (bf16[2,32,1024]{2,1,0:T(8,128)(2,1)S(1)}, bf16[2,32,1024]{2,1,0:T(8,128)(2,1)S(1)}, u32[]{:S(2)}, u32[]{:S(2)}) collective-permute-start(bf16[2,32,1024]{2,1,0:T(8,128)(2,1)S(1)} %get-tuple-element.12), channel_id=1, source_target_pairs={{0,64},{4,68},{8,72},{12,76},{16,80},{20,84},{24,88},{28,92},{32,9... | collective-permute-start | bytes 393224 | tf_op jit(solution)/shard_map/ppermute | solution.py:23
  30.3 9.4 %collective-permute-start.6 = (bf16[2,32,1024]{2,1,0:T(8,128)(2,1)S(1)}, bf16[2,32,1024]{2,1,0:T(8,128)(2,1)S(1)}, u32[]{:S(2)}, u32[]{:S(2)}) collective-permute-start(bf16[2,32,1024]{2,1,0:T(8,128)(2,1)S(1)} %get-tuple-element.14), channel_id=1, source_target_pairs={{0,32},{4,36},{8,40},{12,44},{16,48},{20,52},{24,56},{28,60},{32,6... | collective-permute-start | bytes 393224 | tf_op jit(solution)/shard_map/ppermute | solution.py:23
  31.6 8.1 %collective-permute-start.7 = (bf16[2,32,1024]{2,1,0:T(8,128)(2,1)S(1)}, bf16[2,32,1024]{2,1,0:T(8,128)(2,1)S(1)}, u32[]{:S(2)}, u32[]{:S(2)}) collective-permute-start(bf16[2,32,1024]{2,1,0:T(8,128)(2,1)S(1)} %get-tuple-element.13), channel_id=1, source_target_pairs={{0,96},{4,100},{8,104},{12,108},{16,112},{20,116},{24,120},{28,124... | collective-permute-start | bytes 393224 | tf_op jit(solution)/shard_map/ppermute | solution.py:23
  34.6 7.8 %collective-permute-start.10 = (bf16[2,32,1024]{2,1,0:T(8,128)(2,1)S(1)}, bf16[2,32,1024]{2,1,0:T(8,128)(2,1)S(1)}, u32[]{:S(2)}, u32[]{:S(2)}) collective-permute-start(bf16[2,32,1024]{2,1,0:T(8,128)(2,1)S(1)} %get-tuple-element.17), channel_id=1, source_target_pairs={{0,32},{4,36},{8,40},{12,44},{16,48},{20,52},{24,56},{28,60},{32,6... | collective-permute-start | bytes 393224 | tf_op jit(solution)/shard_map/ppermute | solution.py:23
  34.6 7.8 %collective-permute-start.11 = (bf16[2,32,1024]{2,1,0:T(8,128)(2,1)S(1)}, bf16[2,32,1024]{2,1,0:T(8,128)(2,1)S(1)}, u32[]{:S(2)}, u32[]{:S(2)}) collective-permute-start(bf16[2,32,1024]{2,1,0:T(8,128)(2,1)S(1)} %get-tuple-element.16), channel_id=1, source_target_pairs={{0,96},{4,100},{8,104},{12,108},{16,112},{20,116},{24,120},{28,124... | collective-permute-start | bytes 393224 | tf_op jit(solution)/shard_map/ppermute | solution.py:23
  37.3 6.9 %collective-permute-start.9 = (bf16[2,32,1024]{2,1,0:T(8,128)(2,1)S(1)}, bf16[2,32,1024]{2,1,0:T(8,128)(2,1)S(1)}, u32[]{:S(2)}, u32[]{:S(2)}) collective-permute-start(bf16[2,32,1024]{2,1,0:T(8,128)(2,1)S(1)} %get-tuple-element.15), channel_id=1, source_target_pairs={{0,64},{4,68},{8,72},{12,76},{16,80},{20,84},{24,88},{28,92},{32,9... | collective-permute-start | bytes 393224 | tf_op jit(solution)/shard_map/ppermute | solution.py:23
  44.4 4.6 %collective-permute-start.12 = (bf16[3,32,1024]{2,1,0:T(8,128)(2,1)S(1)}, bf16[3,32,1024]{2,1,0:T(8,128)(2,1)S(1)}, u32[]{:S(2)}, u32[]{:S(2)}) collective-permute-start(bf16[3,32,1024]{2,1,0:T(8,128)(2,1)S(1)} %dynamic-slice_bitcast_fusion.3), channel_id=1, source_target_pairs={{0,128},{4,132},{8,136},{12,140},{16,144},{20,148},{24,152},{28,15... | collective-permute-start | bytes 589832 | tf_op jit(solution)/shard_map/ppermute | solution.py:23
  49.3 8.3 %collective-permute-start.13 = (bf16[3,32,1024]{2,1,0:T(8,128)(2,1)S(1)}, bf16[3,32,1024]{2,1,0:T(8,128)(2,1)S(1)}, u32[]{:S(2)}, u32[]{:S(2)}) collective-permute-start(bf16[3,32,1024]{2,1,0:T(8,128)(2,1)S(1)} %get-tuple-element.8), channel_id=1, source_target_pairs={{0,128},{4,132},{8,136},{12,140},{16,144},{20,148},{24,152},{28,15... | collective-permute-start | bytes 589832 | tf_op jit(solution)/shard_map/ppermute | solution.py:23
  50.6 7.0 %collective-permute-start.14 = (bf16[3,32,1024]{2,1,0:T(8,128)(2,1)S(1)}, bf16[3,32,1024]{2,1,0:T(8,128)(2,1)S(1)}, u32[]{:S(2)}, u32[]{:S(2)}) collective-permute-start(bf16[3,32,1024]{2,1,0:T(8,128)(2,1)S(1)} %get-tuple-element.8), channel_id=1, source_target_pairs={{0,140},{4,128},{8,132},{12,136},{16,156},{20,144},{24,148},{28,15... | collective-permute-start | bytes 589832 | tf_op jit(solution)/shard_map/ppermute | solution.py:23
  57.6 5.7 %collective-permute-start.15 = (bf16[3,32,1024]{2,1,0:T(8,128)(2,1)S(1)}, bf16[3,32,1024]{2,1,0:T(8,128)(2,1)S(1)}, u32[]{:S(2)}, u32[]{:S(2)}) collective-permute-start(bf16[3,32,1024]{2,1,0:T(8,128)(2,1)S(1)} %collective-permute-done.13), channel_id=1, source_target_pairs={{0,128},{4,132},{8,136},{12,140},{16,144},{20,148},{24,152},{28,15... | collective-permute-start | bytes 589832 | tf_op jit(solution)/shard_map/ppermute | solution.py:23
  57.6 5.7 %collective-permute-start.16 = (bf16[3,32,1024]{2,1,0:T(8,128)(2,1)S(1)}, bf16[3,32,1024]{2,1,0:T(8,128)(2,1)S(1)}, u32[]{:S(2)}, u32[]{:S(2)}) collective-permute-start(bf16[3,32,1024]{2,1,0:T(8,128)(2,1)S(1)} %collective-permute-done.14), channel_id=1, source_target_pairs={{0,140},{4,128},{8,132},{12,136},{16,156},{20,144},{24,148},{28,15... | collective-permute-start | bytes 589832 | tf_op jit(solution)/shard_map/ppermute | solution.py:23
  60.4 22.2 %copy-start.8 = (bf16[256,1024]{1,0:T(8,128)(2,1)S(1)}, bf16[256,1024]{1,0:T(8,128)(2,1)}, u32[]{:S(2)}) copy-start(bf16[256,1024]{1,0:T(8,128)(2,1)} %param.13) | copy-start | bytes 1572868
  63.4 6.2 %collective-permute-start.17 = (bf16[3,32,1024]{2,1,0:T(8,128)(2,1)S(1)}, bf16[3,32,1024]{2,1,0:T(8,128)(2,1)S(1)}, u32[]{:S(2)}, u32[]{:S(2)}) collective-permute-start(bf16[3,32,1024]{2,1,0:T(8,128)(2,1)S(1)} %collective-permute-done.15), channel_id=1, source_target_pairs={{0,128},{4,132},{8,136},{12,140},{16,144},{20,148},{24,152},{28,15... | collective-permute-start | bytes 589832 | tf_op jit(solution)/shard_map/ppermute | solution.py:23
  63.4 6.3 %collective-permute-start.18 = (bf16[3,32,1024]{2,1,0:T(8,128)(2,1)S(1)}, bf16[3,32,1024]{2,1,0:T(8,128)(2,1)S(1)}, u32[]{:S(2)}, u32[]{:S(2)}) collective-permute-start(bf16[3,32,1024]{2,1,0:T(8,128)(2,1)S(1)} %collective-permute-done.16), channel_id=1, source_target_pairs={{0,140},{4,128},{8,132},{12,136},{16,156},{20,144},{24,148},{28,15... | collective-permute-start | bytes 589832 | tf_op jit(solution)/shard_map/ppermute | solution.py:23
  69.6 6.0 %collective-permute-start.19 = (bf16[3,16,1024]{2,1,0:T(8,128)(2,1)S(1)}, bf16[3,16,1024]{2,1,0:T(8,128)(2,1)S(1)}, u32[]{:S(2)}, u32[]{:S(2)}) collective-permute-start(bf16[3,16,1024]{2,1,0:T(8,128)(2,1)S(1)} %slice.29), channel_id=1, source_target_pairs={{0,128},{4,132},{8,136},{12,140},{16,144},{20,148},{24,152},{28,15... | collective-permute-start | bytes 294920 | tf_op jit(solution)/shard_map/ppermute | solution.py:23
  69.7 5.9 %collective-permute-start.20 = (bf16[3,16,1024]{2,1,0:T(8,128)(2,1)S(1)}, bf16[3,16,1024]{2,1,0:T(8,128)(2,1)S(1)}, u32[]{:S(2)}, u32[]{:S(2)}) collective-permute-start(bf16[3,16,1024]{2,1,0:T(8,128)(2,1)S(1)} %slice.30), channel_id=1, source_target_pairs={{0,140},{4,128},{8,132},{12,136},{16,156},{20,144},{24,148},{28,15... | collective-permute-start | bytes 294920 | tf_op jit(solution)/shard_map/ppermute | solution.py:23
  75.7 9.9 %collective-permute-start.21 = (bf16[3,256,1024]{2,1,0:T(8,128)(2,1)S(1)}, bf16[3,256,1024]{2,1,0:T(8,128)(2,1)S(1)}, u32[]{:S(2)}, u32[]{:S(2)}) collective-permute-start(bf16[3,256,1024]{2,1,0:T(8,128)(2,1)S(1)} %get-tuple-element.30), channel_id=1, source_target_pairs={{0,16},{4,20},{8,24},{12,28},{16,0},{20,4},{24,8},{28,12},{32,48},... | collective-permute-start | bytes 4718600 | tf_op jit(solution)/shard_map/ppermute | solution.py:23
  82.6 14.7 %collective-permute-start.22 = (bf16[256,1024]{1,0:T(8,128)(2,1)S(1)}, bf16[256,1024]{1,0:T(8,128)(2,1)S(1)}, u32[]{:S(2)}, u32[]{:S(2)}) collective-permute-start(bf16[256,1024]{1,0:T(8,128)(2,1)S(1)} %copy-done.8), channel_id=1, source_target_pairs={{0,64},{4,68},{8,72},{12,76},{16,80},{20,84},{24,88},{28,92},{32,9... | collective-permute-start | bytes 1572872 | tf_op jit(solution)/shard_map/ppermute | solution.py:23
  83.9 24.3 %collective-permute-start.24 = (bf16[256,1024]{1,0:T(8,128)(2,1)S(1)}, bf16[256,1024]{1,0:T(8,128)(2,1)}, u32[]{:S(2)}, u32[]{:S(2)}) collective-permute-start(bf16[256,1024]{1,0:T(8,128)(2,1)S(1)} %copy-done.8), channel_id=1, source_target_pairs={{0,96},{4,100},{8,104},{12,108},{16,112},{20,116},{24,120},{28,124... | collective-permute-start | bytes 1572872 | tf_op jit(solution)/shard_map/ppermute | solution.py:23
  84.8 31.6 %collective-permute-start.26 = (bf16[256,1024]{1,0:T(8,128)(2,1)S(1)}, bf16[256,1024]{1,0:T(8,128)(2,1)}, u32[]{:S(2)}, u32[]{:S(2)}) collective-permute-start(bf16[256,1024]{1,0:T(8,128)(2,1)S(1)} %copy-done.8), channel_id=1, source_target_pairs={{0,32},{4,36},{8,40},{12,44},{16,48},{20,52},{24,56},{28,60},{32,6... | collective-permute-start | bytes 1572872 | tf_op jit(solution)/shard_map/ppermute | solution.py:23
  85.8 11.6 %copy-start.6 = (bf16[3,512,1024]{2,1,0:T(8,128)(2,1)}, bf16[3,512,1024]{2,1,0:T(8,128)(2,1)S(1)}, u32[]{:S(2)}) copy-start(bf16[3,512,1024]{2,1,0:T(8,128)(2,1)S(1)} %constant_dynamic-update-slice_fusion.9) | copy-start | bytes 9437188
  102.5 25.0 %collective-permute-start.23 = (bf16[256,1024]{1,0:T(8,128)(2,1)}, bf16[256,1024]{1,0:T(8,128)(2,1)S(1)}, u32[]{:S(2)}, u32[]{:S(2)}) collective-permute-start(bf16[256,1024]{1,0:T(8,128)(2,1)} %convolution_convert_fusion.4), channel_id=1, source_target_pairs={{0,64},{4,68},{8,72},{12,76},{16,80},{20,84},{24,88},{28,92},{32,9... | collective-permute-start | bytes 1572872 | tf_op jit(solution)/shard_map/ppermute | solution.py:23
  114.9 16.1 %collective-permute-start.25 = (bf16[256,1024]{1,0:T(8,128)(2,1)}, bf16[256,1024]{1,0:T(8,128)(2,1)}, u32[]{:S(2)}, u32[]{:S(2)}) collective-permute-start(bf16[256,1024]{1,0:T(8,128)(2,1)} %convolution_convert_fusion.3), channel_id=1, source_target_pairs={{0,32},{4,36},{8,40},{12,44},{16,48},{20,52},{24,56},{28,60},{32,6... | collective-permute-start | bytes 1572872 | tf_op jit(solution)/shard_map/ppermute | solution.py:23
  123.1 12.9 %collective-permute-start.27 = (bf16[256,1024]{1,0:T(8,128)(2,1)}, bf16[256,1024]{1,0:T(8,128)(2,1)}, u32[]{:S(2)}, u32[]{:S(2)}) collective-permute-start(bf16[256,1024]{1,0:T(8,128)(2,1)} %convolution_convert_fusion.2), channel_id=1, source_target_pairs={{0,96},{4,100},{8,104},{12,108},{16,112},{20,116},{24,120},{28,124... | collective-permute-start | bytes 1572872 | tf_op jit(solution)/shard_map/ppermute | solution.py:23

commit v2 on v0

v2 whole, which is shorter than its diff:
```python
import functools

import jax
import jax.numpy as jnp
from jax import lax
from jax.experimental import pallas as pl
from jax.experimental.pallas import tpu as pltpu
from jax.sharding import PartitionSpec as P

AXES = ("view", "render")
LZ, NX, NC, HZ = 2, 4, 2, 4
NZ = LZ * HZ
F32 = jnp.float32
BF16 = jnp.bfloat16
VMEM_BYTES = 48 * 1024 * 1024
OTHERS = ((2, 1), (1, 1), (3, 1), (2, 0), (1, 0), (3, 0), (0, 1))


def move(array, target):
    pairs = []
    for zl in range(LZ):
        for x in range(NX):
            for core in range(NC):
                for zh in range(HZ):
                    tl, tx, tc, th = target(zl, x, core, zh)
                    pairs.append(
                        (((zl * NX + x) * NC + core) * HZ + zh, ((tl * NX + tx) * NC + tc) * HZ + th)
                    )
    return lax.ppermute(array, AXES, pairs)


def along_x(array, step):
    return move(array, lambda zl, x, c, zh: (zl, (x + step) % NX, c, zh))


def along_z(array, step):
    def target(zl, x, c, zh):
        z = (zh * LZ + zl + step) % NZ
        return z % LZ, x, c, z // LZ

    return move(array, target)


def to_owner(array, step_x, step_zl):
    return move(array, lambda zl, x, c, zh: ((zl + step_zl) % LZ, (x + step_x) % NX, c, zh))


def swap_core(array):
    return move(array, lambda zl, x, c, zh: (zl, x, 1 - c, zh))


def contract(left, right, left_dim, right_dim):
    return lax.dot_general(
        left, right, (((left_dim,), (right_dim,)), ((), ())), preferred_element_type=F32
    )


def params():
    return pltpu.CompilerParams(vmem_limit_bytes=VMEM_BYTES)


def delta_kernel(index, keys, values, rates, gate, up, down, out, *old):
    k, v, r = keys[...], values[...], rates[...]
    gate_in = contract(gate[0], k, 0, 1)
    up_in = contract(up[0], k, 0, 1)
    back = contract(down[0], v, 0, 1)
    s = jax.nn.sigmoid(gate_in)
    act = gate_in * s
    hidden = (r * (act * up_in)).astype(BF16)
    rated = r * back
    pre_gate = (rated * up_in * s * (1.0 + gate_in * (1.0 - s))).astype(BF16)
    pre_up = (rated * act).astype(BF16)
    out[0] = contract(pre_gate, k, 1, 0).astype(BF16)
    out[1] = contract(pre_up, k, 1, 0).astype(BF16)
    out[2] = contract(hidden, v, 1, 0).astype(BF16)
    if old:
        rows_out, turned = old
        units = rows_out.shape[1]
        block = pl.multiple_of(index[1], 128)
        row = pl.multiple_of(index[2], units)
        for m, weight in enumerate((gate, up, down)):
            turned[...] = weight[0, :, pl.ds(block, 128)].astype(F32).T
            rows_out[m] = turned[pl.ds(row, units), :]


def deltas(index, keys, values, rates, weights, units, with_old):
    tokens, width = keys.shape
    own = units // (NX * LZ)
    whole = lambda shape: pl.BlockSpec(shape, lambda i, index: (0,) * len(shape))
    column = pl.BlockSpec((1, width, units), lambda i, index: (0, 0, index[0]))
    out_shape = [jax.ShapeDtypeStruct((3, units, width), BF16)]
    scratch = []
    if with_old:
        out_shape.append(jax.ShapeDtypeStruct((3, own, width), F32))
        scratch = [pltpu.VMEM((128, width), F32)]
    return pl.pallas_call(
        delta_kernel,
        name="delta_own" if with_old else "delta_other",
        grid_spec=pltpu.PrefetchScalarGridSpec(
            num_scalar_prefetch=1,
            grid=(1,),
            in_specs=[
                whole((tokens, width)),
                whole((tokens, width)),
                whole((1, tokens)),
                column,
                column,
                column,
            ],
            out_specs=[whole(o.shape) for o in out_shape],
            scratch_shapes=scratch,
        ),
        out_shape=out_shape,
        compiler_params=params(),
        cost_estimate=pl.CostEstimate(
            flops=12 * tokens * width * units, bytes_accessed=8 << 20, transcendentals=tokens * units
        ),
    )(index, keys, values, rates, *weights)


def split_kernel(place, mine, other, keep, *outs):
    x, zl = place[0], place[1]
    own = keep.shape[1]

    def rows(step_x, step_zl):
        start = ((x + step_x) % NX * LZ + (zl + step_zl) % LZ) * own
        part = pl.ds(pl.multiple_of(start, own), own)
        return mine[:, part, :].astype(F32) + other[:, part, :].astype(F32)

    keep[...] = rows(0, 0)
    for out, steps in zip(outs, OTHERS):
        out[...] = rows(*steps).astype(BF16)


def split(place, mine, other):
    _, units, width = mine.shape
    own = units // (NX * LZ)
    vmem = pl.BlockSpec(memory_space=pltpu.VMEM)
    return pl.pallas_call(
        split_kernel,
        name="split",
        in_specs=[pl.BlockSpec(memory_space=pltpu.SMEM), vmem, vmem],
        out_specs=[vmem] * (1 + len(OTHERS)),
        out_shape=[jax.ShapeDtypeStruct((3, own, width), F32)]
        + [jax.ShapeDtypeStruct((3, own, width), BF16)] * len(OTHERS),
        compiler_params=params(),
    )(place, mine, other)


def renorm_kernel(old, keep, *refs):
    out = refs[-1]
    was = old[...]
    summed = keep[...]
    for ref in refs[:-1]:
        summed = summed + ref[...].astype(F32)
    summed = was + summed
    factor = jnp.sqrt(jnp.sum(was * was, axis=-1, keepdims=True)) / jnp.sqrt(
        jnp.sum(summed * summed, axis=-1, keepdims=True) + 1e-06
    )
    out[...] = (summed * factor).astype(BF16)


def renorm(old, keep, got):
    vmem = pl.BlockSpec(memory_space=pltpu.VMEM)
    return pl.pallas_call(
        renorm_kernel,
        name="renorm",
        in_specs=[vmem] * (2 + len(got)),
        out_specs=vmem,
        out_shape=jax.ShapeDtypeStruct(old.shape, BF16),
        compiler_params=params(),
    )(old, keep, *got)


def join_kernel(*refs):
    out = refs[-1]
    at = 0
    for ref in refs[:-1]:
        n = ref.shape[1]
        out[:, at : at + n, :] = ref[...]
        at += n


def join(pieces):
    vmem = pl.BlockSpec(memory_space=pltpu.VMEM)
    units = sum(p.shape[1] for p in pieces)
    return pl.pallas_call(
        join_kernel,
        name="join",
        in_specs=[vmem] * len(pieces),
        out_specs=vmem,
        out_shape=jax.ShapeDtypeStruct((3, units, pieces[0].shape[2]), BF16),
        compiler_params=params(),
    )(*pieces)


def render_kernel(rows, weights, out):
    q = rows[...]
    gate_q = contract(q, weights[0], 1, 1)
    up_q = contract(q, weights[1], 1, 1)
    hidden_q = (gate_q * jax.nn.sigmoid(gate_q) * up_q).astype(BF16)
    out[...] = contract(hidden_q, weights[2], 1, 0).astype(out.dtype)


def render(rows, weights, dtype):
    vmem = pl.BlockSpec(memory_space=pltpu.VMEM)
    n, width = rows.shape
    return pl.pallas_call(
        render_kernel,
        name="render_rows",
        in_specs=[vmem, vmem],
        out_specs=vmem,
        out_shape=jax.ShapeDtypeStruct((n, width), dtype),
        compiler_params=params(),
        cost_estimate=pl.CostEstimate(
            flops=6 * n * width * weights.shape[1],
            bytes_accessed=4 << 20,
            transcendentals=n * weights.shape[1],
        ),
    )(rows, weights)


def total_kernel(*refs):
    total = refs[0][...].astype(F32)
    for ref in refs[1:-1]:
        total = total + ref[...].astype(F32)
    refs[-1][...] = total.astype(BF16)


def total(parts):
    vmem = pl.BlockSpec(memory_space=pltpu.VMEM)
    return pl.pallas_call(
        total_kernel,
        name="total",
        in_specs=[vmem] * len(parts),
        out_specs=vmem,
        out_shape=jax.ShapeDtypeStruct(parts[0].shape, BF16),
        compiler_params=params(),
    )(*parts)


def local(input_keys, input_values, token_rates, gate_weight, up_weight, down_weight, queries):
    view = lax.axis_index("view")
    zl, x, core = view // (NX * NC), (view // NC) % NX, view % NC
    units = gate_weight.shape[2] // NC
    own = units // (NX * LZ)
    start = (x * LZ + zl) * own

    tokens = (input_keys, input_values, token_rates)
    weights = (gate_weight, up_weight, down_weight)
    index = lambda c: jnp.stack([c, start // 128 * 128, start % 128]).astype(jnp.int32)
    (other_units,) = deltas(index(1 - core), *tokens, weights, units, False)
    from_other = swap_core(other_units)
    mine, old = deltas(index(core), *tokens, weights, units, True)
    keep, *sends = split(jnp.stack([x, zl]).astype(jnp.int32), mine, from_other)
    got = [to_owner(s, *steps) for s, steps in zip(sends, OTHERS)]
    queries, *got = lax.optimization_barrier((queries, *got))
    new = renorm(old, keep, got)

    half = own // 2
    right1, right2 = along_z(new, 1), along_z(new, 2)
    left1, left2 = along_z(new, -1), along_z(new, -2)
    right3, left3 = along_z(right2, 1), along_z(left2, -1)
    far = [along_z(right2[:, :half], 2), along_z(left2[:, half:], -2)]
    near = [new, right1, left1, right2, left2]
    pieces = near + [right3, left3] + far
    held = join(pieces + [swap_core(p) for p in pieces])

    asked = [(step, along_x(queries, -step)) for step in (2, 1, 3)]
    got = [along_x(render(rows, held, BF16), step) for step, rows in asked]
    return total([render(queries, held, F32)] + got)


def solution(mesh):
    return jax.shard_map(
        local,
        mesh=mesh,
        in_specs=(
            P("view", "head"),
            P("view", "head"),
            P("head", "view"),
            P("head", None, "render"),
            P("head", None, "render"),
            P("head", None, "render"),
            P(("view", "render"), "head"),
        ),
        out_specs=P(("view", "render"), "head"),
        check_vma=False,
    )
```

time: 436 us -> 128 us (0.29); the launches traced: 428 us -> 127 us
  waiting for transfers between devices: 371 us -> 54.5 us
  starting transfers between devices: 0.31 us -> 44.6 us
  matrix products: 26.9 us -> 0 us
  Pallas kernels: 0 us -> 21.4 us
  between operations: 13.3 us -> 0.15 us
  other arithmetic: 10.4 us -> 0.15 us
    all_gather x3 -> x0, waiting for transfers between devices: 240 us -> none  [the longest x1 86.2 us: local(): lax.all_gather(new_down, 'render', axis=2, tiled=True)[0]]
    psum x1 -> x0, waiting for transfers between devices: 130 us -> none  [local(): lax.psum(grad_down.astype(jnp.bfloat16), 'view').astype(jnp.float32)]
    ppermute x0 -> x31, waiting for transfers between devices: none -> 54.5 us  [move(): return lax.ppermute(array, AXES, pairs)]
    ppermute x0 -> x31, starting transfers between devices: none -> 44.6 us  [move(): return lax.ppermute(array, AXES, pairs)]
    dot_general x8 -> x0, matrix products: 26.9 us -> none  [the longest x1 9.14 us: render_rows(): lax.dot_general(hidden_q, piece_down, (((1,), (1,)), ((), ())), preferred...]
    pallas_call x0 -> x10, Pallas kernels: none -> 21.4 us  [the longest x2 12.9 us: deltas(): pl.pallas_call(delta_kernel, name='delta_own' if with_old else 'delta_oth...]
    convert_element_type x3 -> x0, other arithmetic: 5.22 us -> none  [renorm(): return (summed * factor).astype(jnp.bfloat16)]
    reduce_sum x2 -> x0, other arithmetic: 5.18 us -> none  [renorm(): jnp.sum(old_wide * old_wide, axis=-2, keepdims=True)]
  transfers between devices with their start and end apart: 4 -> 31, of which waited for: 4 -> 16; matrix products, arithmetic and copies ran while one was open for 3% -> 0% of each run, Pallas kernels for 0% -> 10%
where the time goes in v2:
time: 128 us; the launch traced here: 127 us
  waiting for transfers between devices  54.5 us (43%)
  starting transfers between devices  44.6 us (35%)
  Pallas kernels  21.4 us (17%)
  local copies, waits for them, and re-layouts  6.27 us (5%)
    ppermute x31, waiting for transfers between devices, move(): return lax.ppermute(array, AXES, pairs)  54.5 us
    ppermute x31, starting transfers between devices, move(): return lax.ppermute(array, AXES, pairs)  44.6 us
    pallas_call x2, Pallas kernels, deltas(): pl.pallas_call(delta_kernel, name='delta_own' if with_old else 'delta_oth...  12.9 us
    unnamed x14, local copies, waits for them, and re-layouts  6.26 us
    pallas_call x4, Pallas kernels, render(): pl.pallas_call(render_kernel, name='render_rows', in_specs=[vmem, vmem],...  4.35 us
  transfers between devices with their start and end apart: 31, of which 16 were waited for; matrix products, arithmetic and copies ran while one was open for 0% of the time, Pallas kernels for 10%

profile of v2, /device:TPU:1, one launch (start us, length us, event | category | flops | bytes accessed | tf_op | source)
XLA Modules:
  0.0 127.1 jit_solution(3004329397337421615)
XLA Ops:
  0.0 0.1 add_add_fusion
  0.1 1.2 copy-done.2
  1.3 1.2 copy-done.4
  2.5 1.2 copy-done.5
  3.8 0.7 copy-done.6
  4.4 6.5 %delta_other.1 = bf16[3,256,1024]{2,1,0:T(8,128)(2,1)S(1)} custom-call(s32[3]{0:T(128)S(1)} %get-tuple-element.42.index, bf16[1024,1024]{1,0:T(8,128)(2,1)} %keys.3, bf16[1024,1024]{1,0:T(8,128)(2,1)} %values.3, f32[1,1024]{1,0:T(1,128)S(1)} %copy-done.6, bf16[1,1024,512]{2,1,0:T(8,128)(2,1)S(1)} %copy-done.2, bf16[1,1024,512]{2,1,0:T(8,128)(2,1)S(1)} %copy-done.4, ...), custom_call_target="tpu_custom_call" | custom-call | flops 3221225472 | bytes 8388608 | tf_op jit(solution)/shard_map/delta_other/pallas_call | solution.py:96
  10.9 3.3 %collective-permute-start = (bf16[3,256,1024]{2,1,0:T(8,128)(2,1)S(1)}, bf16[3,256,1024]{2,1,0:T(8,128)(2,1)S(1)}, u32[]{:S(2)}, u32[]{:S(2)}) collective-permute-start(bf16[3,256,1024]{2,1,0:T(8,128)(2,1)S(1)} %delta_other.1), channel_id=1, source_target_pairs={{0,16},{4,20},{8,24},{12,28},{16,0},{20,4},{24,8},{28,12},{32,48},... | collective-permute-start | bytes 4718600 | tf_op jit(solution)/shard_map/ppermute | solution.py:29
  14.2 0.1 pad_add_fusion.place
  14.3 6.5 %delta_own.1 = (bf16[3,256,1024]{2,1,0:T(8,128)(2,1)S(1)}, f32[3,32,1024]{2,1,0:T(8,128)S(1)}) custom-call(s32[3]{0:T(128)S(1)} %get-tuple-element.41.index, bf16[1024,1024]{1,0:T(8,128)(2,1)} %keys.3, bf16[1024,1024]{1,0:T(8,128)(2,1)} %values.3, f32[1,1024]{1,0:T(1,128)S(1)} %copy-done.6, bf16[1,1024,512]{2,1,0:T(8,128)(2,1)S(1)} %copy-done.3, ...), custom_call_target="tpu_custom_call" | custom-call | flops 3221225472 | bytes 8388608 | tf_op jit(solution)/shard_map/delta_own/pallas_call | solution.py:96
  20.8 0.0 collective-permute-done.other
  20.8 0.9 split.1
  21.7 0.0 copy-start.1
  21.7 2.5 %collective-permute-start.1 = (bf16[3,32,1024]{2,1,0:T(8,128)(2,1)S(1)}, bf16[3,32,1024]{2,1,0:T(8,128)(2,1)S(1)}, u32[]{:S(2)}, u32[]{:S(2)}) collective-permute-start(bf16[3,32,1024]{2,1,0:T(8,128)(2,1)S(1)} %get-tuple-element.24), channel_id=1, source_target_pairs={{0,192},{4,196},{8,200},{12,204},{16,208},{20,212},{24,216},{28,22... | collective-permute-start | bytes 589832 | tf_op jit(solution)/shard_map/ppermute | solution.py:29
  24.2 0.0 collective-permute-start.2
  24.2 3.6 %collective-permute-start.3 = (bf16[3,32,1024]{2,1,0:T(8,128)(2,1)S(1)}, bf16[3,32,1024]{2,1,0:T(8,128)(2,1)S(1)}, u32[]{:S(2)}, u32[]{:S(2)}) collective-permute-start(bf16[3,32,1024]{2,1,0:T(8,128)(2,1)S(1)} %get-tuple-element.26), channel_id=1, source_target_pairs={{0,224},{4,228},{8,232},{12,236},{16,240},{20,244},{24,248},{28,25... | collective-permute-start | bytes 589832 | tf_op jit(solution)/shard_map/ppermute | solution.py:29
  27.8 0.2 collective-permute-start.5
  28.0 3.2 %collective-permute-done.1.refs_0_ = bf16[3,32,1024]{2,1,0:T(8,128)(2,1)S(1)} collective-permute-done((bf16[3,32,1024]{2,1,0:T(8,128)(2,1)S(1)}, bf16[3,32,1024]{2,1,0:T(8,128)(2,1)S(1)}, u32[]{:S(2)}, u32[]{:S(2)}) %collective-permute-start.1) | collective-permute-done | bytes 196640 | tf_op jit(solution)/shard_map/ppermute | solution.py:29
  31.1 0.3 collective-permute-start.6
  31.5 3.6 %collective-permute-done.2.refs_1_ = bf16[3,32,1024]{2,1,0:T(8,128)(2,1)S(1)} collective-permute-done((bf16[3,32,1024]{2,1,0:T(8,128)(2,1)S(1)}, bf16[3,32,1024]{2,1,0:T(8,128)(2,1)S(1)}, u32[]{:S(2)}, u32[]{:S(2)}) %collective-permute-start.2) | collective-permute-done | bytes 196640 | tf_op jit(solution)/shard_map/ppermute | solution.py:29
  35.1 0.6 collective-permute-start.7
  35.7 2.9 %collective-permute-done.3.refs_2_ = bf16[3,32,1024]{2,1,0:T(8,128)(2,1)S(1)} collective-permute-done((bf16[3,32,1024]{2,1,0:T(8,128)(2,1)S(1)}, bf16[3,32,1024]{2,1,0:T(8,128)(2,1)S(1)}, u32[]{:S(2)}, u32[]{:S(2)}) %collective-permute-start.3) | collective-permute-done | bytes 196640 | tf_op jit(solution)/shard_map/ppermute | solution.py:29
  38.6 1.0 collective-permute-done.4.refs_3_
  39.5 4.2 %collective-permute-done.5.refs_4_ = bf16[3,32,1024]{2,1,0:T(8,128)(2,1)S(1)} collective-permute-done((bf16[3,32,1024]{2,1,0:T(8,128)(2,1)S(1)}, bf16[3,32,1024]{2,1,0:T(8,128)(2,1)S(1)}, u32[]{:S(2)}, u32[]{:S(2)}) %collective-permute-start.5) | collective-permute-done | bytes 196640 | tf_op jit(solution)/shard_map/ppermute | solution.py:29
  43.7 0.3 renorm.1.refs_0_
  44.0 5.0 %collective-permute-start.11 = (bf16[3,32,1024]{2,1,0:T(8,128)(2,1)S(1)}, bf16[3,32,1024]{2,1,0:T(8,128)(2,1)S(1)}, u32[]{:S(2)}, u32[]{:S(2)}) collective-permute-start(bf16[3,32,1024]{2,1,0:T(8,128)(2,1)S(1)} %renorm.1.refs_0_), channel_id=1, source_target_pairs={{0,12},{4,0},{8,4},{12,8},{16,28},{20,16},{24,20},{28,24},{32,44},... | collective-permute-start | bytes 589832 | tf_op jit(solution)/shard_map/ppermute | solution.py:29
  49.0 0.8 collective-permute-start.16
  49.8 3.4 %collective-permute-start.9 = (bf16[3,32,1024]{2,1,0:T(8,128)(2,1)S(1)}, bf16[3,32,1024]{2,1,0:T(8,128)(2,1)S(1)}, u32[]{:S(2)}, u32[]{:S(2)}) collective-permute-start(bf16[3,32,1024]{2,1,0:T(8,128)(2,1)S(1)} %renorm.1.refs_0_), channel_id=1, source_target_pairs={{0,140},{4,128},{8,132},{12,136},{16,156},{20,144},{24,148},{28,15... | collective-permute-start | bytes 589832 | tf_op jit(solution)/shard_map/ppermute | solution.py:29
  53.2 2.5 %collective-permute-done.11.refs_4_ = bf16[3,32,1024]{2,1,0:T(8,128)(2,1)S(1)} collective-permute-done((bf16[3,32,1024]{2,1,0:T(8,128)(2,1)S(1)}, bf16[3,32,1024]{2,1,0:T(8,128)(2,1)S(1)}, u32[]{:S(2)}, u32[]{:S(2)}) %collective-permute-start.11) | collective-permute-done | bytes 196640 | tf_op jit(solution)/shard_map/ppermute | solution.py:29
  55.7 3.4 %collective-permute-start.15 = (bf16[3,16,1024]{2,1,0:T(8,128)(2,1)S(1)}, bf16[3,16,1024]{2,1,0:T(8,128)(2,1)S(1)}, u32[]{:S(2)}, u32[]{:S(2)}) collective-permute-start(bf16[3,16,1024]{2,1,0:T(8,128)(2,1)S(1)} %slice.9), channel_id=1, source_target_pairs={{0,12},{4,0},{8,4},{12,8},{16,28},{20,16},{24,20},{28,24},{32,44},... | collective-permute-start | bytes 294920 | tf_op jit(solution)/shard_map/ppermute | solution.py:29
  59.2 4.4 %collective-permute-start.20 = (bf16[3,32,1024]{2,1,0:T(8,128)(2,1)S(1)}, bf16[3,32,1024]{2,1,0:T(8,128)(2,1)S(1)}, u32[]{:S(2)}, u32[]{:S(2)}) collective-permute-start(bf16[3,32,1024]{2,1,0:T(8,128)(2,1)S(1)} %collective-permute-done.11.refs_4_), channel_id=1, source_target_pairs={{0,16},{4,20},{8,24},{12,28},{16,0},{20,4},{24,8},{28,12},{32,48},... | collective-permute-start | bytes 589832 | tf_op jit(solution)/shard_map/ppermute | solution.py:29
  63.6 0.0 collective-permute-done.16.refs_9_
  63.6 0.1 collective-permute-start.14
  63.7 0.3 collective-permute-done.9.refs_2_
  63.9 2.7 %collective-permute-start.13 = (bf16[3,32,1024]{2,1,0:T(8,128)(2,1)S(1)}, bf16[3,32,1024]{2,1,0:T(8,128)(2,1)S(1)}, u32[]{:S(2)}, u32[]{:S(2)}) collective-permute-start(bf16[3,32,1024]{2,1,0:T(8,128)(2,1)S(1)} %collective-permute-done.11.refs_4_), channel_id=1, source_target_pairs={{0,140},{4,128},{8,132},{12,136},{16,156},{20,144},{24,148},{28,15... | collective-permute-start | bytes 589832 | tf_op jit(solution)/shard_map/ppermute | solution.py:29
  66.6 0.0 collective-permute-done.15.refs_8_
  66.6 1.0 collective-permute-start.24
  67.7 0.0 collective-permute-start.19
  67.7 4.5 %collective-permute-done.14.refs_7_ = bf16[3,16,1024]{2,1,0:T(8,128)(2,1)S(1)} collective-permute-done((bf16[3,16,1024]{2,1,0:T(8,128)(2,1)S(1)}, bf16[3,16,1024]{2,1,0:T(8,128)(2,1)S(1)}, u32[]{:S(2)}, u32[]{:S(2)}) %collective-permute-start.14) | collective-permute-done | bytes 98336 | tf_op jit(solution)/shard_map/ppermute | solution.py:29
  72.2 0.4 collective-permute-start.29
  72.6 1.1 collective-permute-start.23
  73.7 2.3 %collective-permute-start.27 = (bf16[256,1024]{1,0:T(8,128)(2,1)S(1)}, bf16[256,1024]{1,0:T(8,128)(2,1)S(1)}, u32[]{:S(2)}, u32[]{:S(2)}) collective-permute-start(bf16[256,1024]{1,0:T(8,128)(2,1)S(1)} %copy-done.1), channel_id=1, source_target_pairs={{0,96},{4,100},{8,104},{12,108},{16,112},{20,116},{24,120},{28,124... | collective-permute-start | bytes 1572872 | tf_op jit(solution)/shard_map/ppermute | solution.py:29
  76.0 0.3 collective-permute-start.18
  76.3 0.3 collective-permute-start.17
  76.6 2.4 %collective-permute-done.12.refs_5_ = bf16[3,32,1024]{2,1,0:T(8,128)(2,1)S(1)} collective-permute-done((bf16[3,32,1024]{2,1,0:T(8,128)(2,1)S(1)}, bf16[3,32,1024]{2,1,0:T(8,128)(2,1)S(1)}, u32[]{:S(2)}, u32[]{:S(2)}) %collective-permute-start.12) | collective-permute-done | bytes 196640 | tf_op jit(solution)/shard_map/ppermute | solution.py:29
  79.0 1.3 %collective-permute-start.25 = (bf16[256,1024]{1,0:T(8,128)(2,1)S(1)}, bf16[256,1024]{1,0:T(8,128)(2,1)S(1)}, u32[]{:S(2)}, u32[]{:S(2)}) collective-permute-start(bf16[256,1024]{1,0:T(8,128)(2,1)S(1)} %copy-done.1), channel_id=1, source_target_pairs={{0,64},{4,68},{8,72},{12,76},{16,80},{20,84},{24,88},{28,92},{32,9... | collective-permute-start | bytes 1572872 | tf_op jit(solution)/shard_map/ppermute | solution.py:29
  80.3 2.0 %collective-permute-start.22 = (bf16[3,32,1024]{2,1,0:T(8,128)(2,1)S(1)}, bf16[3,32,1024]{2,1,0:T(8,128)(2,1)S(1)}, u32[]{:S(2)}, u32[]{:S(2)}) collective-permute-start(bf16[3,32,1024]{2,1,0:T(8,128)(2,1)S(1)} %collective-permute-done.13.refs_6_), channel_id=1, source_target_pairs={{0,16},{4,20},{8,24},{12,28},{16,0},{20,4},{24,8},{28,12},{32,48},... | collective-permute-start | bytes 589832 | tf_op jit(solution)/shard_map/ppermute | solution.py:29
  82.3 0.1 collective-permute-start.21
  82.4 1.0 collective-permute-done.22.refs_15_
  83.4 0.4 collective-permute-done.21.refs_14_
  83.8 1.8 %join.1.weights = bf16[3,512,1024]{2,1,0:T(8,128)(2,1)} custom-call(bf16[3,32,1024]{2,1,0:T(8,128)(2,1)S(1)} %renorm.1.refs_0_, bf16[3,32,1024]{2,1,0:T(8,128)(2,1)S(1)} %collective-permute-done.8.refs_1_, bf16[3,32,1024]{2,1,0:T(8,128)(2,1)S(1)} %collective-permute-done.9.refs_2_, bf16[3,32,1024]{2,1,0:T(8,128)(2,1)S(1)} %collective-permute-done.10.refs_3_, ...), custom_call_target="tpu_custom_call" | custom-call | tf_op jit(solution)/shard_map/join/pallas_call | solution.py:187
  85.6 1.1 collective-permute-done.29.rows
  86.6 1.9 %copy-done = bf16[3,512,1024]{2,1,0:T(8,128)(2,1)S(1)} copy-done((bf16[3,512,1024]{2,1,0:T(8,128)(2,1)S(1)}, bf16[3,512,1024]{2,1,0:T(8,128)(2,1)}, u32[]{:S(2)}) %copy-start) | copy-done | bytes 3145752
  88.5 1.1 render_rows.7
  89.6 0.4 collective-permute-start.30
  90.0 8.1 %collective-permute-done.27.rows = bf16[256,1024]{1,0:T(8,128)(2,1)S(1)} collective-permute-done((bf16[256,1024]{1,0:T(8,128)(2,1)S(1)}, bf16[256,1024]{1,0:T(8,128)(2,1)S(1)}, u32[]{:S(2)}, u32[]{:S(2)}) %collective-permute-start.27) | collective-permute-done | bytes 524320 | tf_op jit(solution)/shard_map/ppermute | solution.py:29
  98.1 1.1 render_rows.6
  99.2 0.1 collective-permute-start.28
  99.3 1.1 render_rows.5
  100.4 5.0 %collective-permute-start.26 = (bf16[256,1024]{1,0:T(8,128)(2,1)S(1)}, bf16[256,1024]{1,0:T(8,128)(2,1)S(1)}, u32[]{:S(2)}, u32[]{:S(2)}) collective-permute-start(bf16[256,1024]{1,0:T(8,128)(2,1)S(1)} %render_rows.5), channel_id=1, source_target_pairs={{0,64},{4,68},{8,72},{12,76},{16,80},{20,84},{24,88},{28,92},{32,9... | collective-permute-start | bytes 1572872 | tf_op jit(solution)/shard_map/ppermute | solution.py:29
  105.4 1.1 render_rows.4.refs_0_
  106.5 0.5 collective-permute-done.30.refs_3_
  107.0 5.1 %collective-permute-done.28.refs_2_ = bf16[256,1024]{1,0:T(8,128)(2,1)S(1)} collective-permute-done((bf16[256,1024]{1,0:T(8,128)(2,1)S(1)}, bf16[256,1024]{1,0:T(8,128)(2,1)S(1)}, u32[]{:S(2)}, u32[]{:S(2)}) %collective-permute-start.28) | collective-permute-done | bytes 524320 | tf_op jit(solution)/shard_map/ppermute | solution.py:29
  112.1 14.0 %collective-permute-done.26.refs_1_ = bf16[256,1024]{1,0:T(8,128)(2,1)S(1)} collective-permute-done((bf16[256,1024]{1,0:T(8,128)(2,1)S(1)}, bf16[256,1024]{1,0:T(8,128)(2,1)S(1)}, u32[]{:S(2)}, u32[]{:S(2)}) %collective-permute-start.26) | collective-permute-done | bytes 524320 | tf_op jit(solution)/shard_map/ppermute | solution.py:29
  126.1 1.0 total.1
  (26 shorter events, 0.1 us)
Async XLA Ops:
  0.1 1.2 copy-start.2
  1.3 1.2 copy-start.4
  2.5 1.2 copy-start.5
  3.8 0.7 copy-start.6
  4.4 9.9 %copy-start.3 = (bf16[1,1024,512]{2,1,0:T(8,128)(2,1)S(1)}, bf16[1,1024,512]{2,1,0:T(8,128)(2,1)}, u32[]{:S(2)}) copy-start(bf16[1,1024,512]{2,1,0:T(8,128)(2,1)} %gate.3) | copy-start | bytes 3145732
  10.9 9.9 %collective-permute-start = (bf16[3,256,1024]{2,1,0:T(8,128)(2,1)S(1)}, bf16[3,256,1024]{2,1,0:T(8,128)(2,1)S(1)}, u32[]{:S(2)}, u32[]{:S(2)}) collective-permute-start(bf16[3,256,1024]{2,1,0:T(8,128)(2,1)S(1)} %delta_other.1), channel_id=1, source_target_pairs={{0,16},{4,20},{8,24},{12,28},{16,0},{20,4},{24,8},{28,12},{32,48},... | collective-permute-start | bytes 4718600 | tf_op jit(solution)/shard_map/ppermute | solution.py:29
  21.7 50.4 %copy-start.1 = (bf16[256,1024]{1,0:T(8,128)(2,1)S(1)}, bf16[256,1024]{1,0:T(8,128)(2,1)}, u32[]{:S(2)}) copy-start(bf16[256,1024]{1,0:T(8,128)(2,1)} %rows) | copy-start | bytes 1572868
  21.7 9.4 %collective-permute-start.1 = (bf16[3,32,1024]{2,1,0:T(8,128)(2,1)S(1)}, bf16[3,32,1024]{2,1,0:T(8,128)(2,1)S(1)}, u32[]{:S(2)}, u32[]{:S(2)}) collective-permute-start(bf16[3,32,1024]{2,1,0:T(8,128)(2,1)S(1)} %get-tuple-element.24), channel_id=1, source_target_pairs={{0,192},{4,196},{8,200},{12,204},{16,208},{20,212},{24,216},{28,22... | collective-permute-start | bytes 589832 | tf_op jit(solution)/shard_map/ppermute | solution.py:29
  24.2 10.9 %collective-permute-start.2 = (bf16[3,32,1024]{2,1,0:T(8,128)(2,1)S(1)}, bf16[3,32,1024]{2,1,0:T(8,128)(2,1)S(1)}, u32[]{:S(2)}, u32[]{:S(2)}) collective-permute-start(bf16[3,32,1024]{2,1,0:T(8,128)(2,1)S(1)} %get-tuple-element.25), channel_id=1, source_target_pairs={{0,160},{4,164},{8,168},{12,172},{16,176},{20,180},{24,184},{28,18... | collective-permute-start | bytes 589832 | tf_op jit(solution)/shard_map/ppermute | solution.py:29
  24.2 14.4 %collective-permute-start.3 = (bf16[3,32,1024]{2,1,0:T(8,128)(2,1)S(1)}, bf16[3,32,1024]{2,1,0:T(8,128)(2,1)S(1)}, u32[]{:S(2)}, u32[]{:S(2)}) collective-permute-start(bf16[3,32,1024]{2,1,0:T(8,128)(2,1)S(1)} %get-tuple-element.26), channel_id=1, source_target_pairs={{0,224},{4,228},{8,232},{12,236},{16,240},{20,244},{24,248},{28,25... | collective-permute-start | bytes 589832 | tf_op jit(solution)/shard_map/ppermute | solution.py:29
  27.8 11.8 %collective-permute-start.4 = (bf16[3,32,1024]{2,1,0:T(8,128)(2,1)S(1)}, bf16[3,32,1024]{2,1,0:T(8,128)(2,1)S(1)}, u32[]{:S(2)}, u32[]{:S(2)}) collective-permute-start(bf16[3,32,1024]{2,1,0:T(8,128)(2,1)S(1)} %get-tuple-element.27), channel_id=1, source_target_pairs={{0,64},{4,68},{8,72},{12,76},{16,80},{20,84},{24,88},{28,92},{32,9... | collective-permute-start | bytes 589832 | tf_op jit(solution)/shard_map/ppermute | solution.py:29
  27.8 15.9 %collective-permute-start.5 = (bf16[3,32,1024]{2,1,0:T(8,128)(2,1)S(1)}, bf16[3,32,1024]{2,1,0:T(8,128)(2,1)S(1)}, u32[]{:S(2)}, u32[]{:S(2)}) collective-permute-start(bf16[3,32,1024]{2,1,0:T(8,128)(2,1)S(1)} %get-tuple-element.28), channel_id=1, source_target_pairs={{0,32},{4,36},{8,40},{12,44},{16,48},{20,52},{24,56},{28,60},{32,6... | collective-permute-start | bytes 589832 | tf_op jit(solution)/shard_map/ppermute | solution.py:29
  31.1 12.5 %collective-permute-start.6 = (bf16[3,32,1024]{2,1,0:T(8,128)(2,1)S(1)}, bf16[3,32,1024]{2,1,0:T(8,128)(2,1)S(1)}, u32[]{:S(2)}, u32[]{:S(2)}) collective-permute-start(bf16[3,32,1024]{2,1,0:T(8,128)(2,1)S(1)} %get-tuple-element.29), channel_id=1, source_target_pairs={{0,96},{4,100},{8,104},{12,108},{16,112},{20,116},{24,120},{28,124... | collective-permute-start | bytes 589832 | tf_op jit(solution)/shard_map/ppermute | solution.py:29
  35.1 8.6 %collective-permute-start.7 = (bf16[3,32,1024]{2,1,0:T(8,128)(2,1)S(1)}, bf16[3,32,1024]{2,1,0:T(8,128)(2,1)S(1)}, u32[]{:S(2)}, u32[]{:S(2)}) collective-permute-start(bf16[3,32,1024]{2,1,0:T(8,128)(2,1)S(1)} %get-tuple-element.30), channel_id=1, source_target_pairs={{0,128},{4,132},{8,136},{12,140},{16,144},{20,148},{24,152},{28,15... | collective-permute-start | bytes 589832 | tf_op jit(solution)/shard_map/ppermute | solution.py:29
  44.0 11.7 %collective-permute-start.11 = (bf16[3,32,1024]{2,1,0:T(8,128)(2,1)S(1)}, bf16[3,32,1024]{2,1,0:T(8,128)(2,1)S(1)}, u32[]{:S(2)}, u32[]{:S(2)}) collective-permute-start(bf16[3,32,1024]{2,1,0:T(8,128)(2,1)S(1)} %renorm.1.refs_0_), channel_id=1, source_target_pairs={{0,12},{4,0},{8,4},{12,8},{16,28},{20,16},{24,20},{28,24},{32,44},... | collective-permute-start | bytes 589832 | tf_op jit(solution)/shard_map/ppermute | solution.py:29
  49.0 10.1 %collective-permute-start.10 = (bf16[3,32,1024]{2,1,0:T(8,128)(2,1)S(1)}, bf16[3,32,1024]{2,1,0:T(8,128)(2,1)S(1)}, u32[]{:S(2)}, u32[]{:S(2)}) collective-permute-start(bf16[3,32,1024]{2,1,0:T(8,128)(2,1)S(1)} %renorm.1.refs_0_), channel_id=1, source_target_pairs={{0,4},{4,8},{8,12},{12,0},{16,20},{20,24},{24,28},{28,16},{32,36},... | collective-permute-start | bytes 589832 | tf_op jit(solution)/shard_map/ppermute | solution.py:29
  49.0 14.6 %collective-permute-start.16 = (bf16[3,32,1024]{2,1,0:T(8,128)(2,1)S(1)}, bf16[3,32,1024]{2,1,0:T(8,128)(2,1)S(1)}, u32[]{:S(2)}, u32[]{:S(2)}) collective-permute-start(bf16[3,32,1024]{2,1,0:T(8,128)(2,1)S(1)} %renorm.1.refs_0_), channel_id=1, source_target_pairs={{0,16},{4,20},{8,24},{12,28},{16,0},{20,4},{24,8},{28,12},{32,48},... | collective-permute-start | bytes 589832 | tf_op jit(solution)/shard_map/ppermute | solution.py:29
  49.8 14.1 %collective-permute-start.9 = (bf16[3,32,1024]{2,1,0:T(8,128)(2,1)S(1)}, bf16[3,32,1024]{2,1,0:T(8,128)(2,1)S(1)}, u32[]{:S(2)}, u32[]{:S(2)}) collective-permute-start(bf16[3,32,1024]{2,1,0:T(8,128)(2,1)S(1)} %renorm.1.refs_0_), channel_id=1, source_target_pairs={{0,140},{4,128},{8,132},{12,136},{16,156},{20,144},{24,148},{28,15... | collective-permute-start | bytes 589832 | tf_op jit(solution)/shard_map/ppermute | solution.py:29
  53.2 14.4 %collective-permute-start.8 = (bf16[3,32,1024]{2,1,0:T(8,128)(2,1)S(1)}, bf16[3,32,1024]{2,1,0:T(8,128)(2,1)S(1)}, u32[]{:S(2)}, u32[]{:S(2)}) collective-permute-start(bf16[3,32,1024]{2,1,0:T(8,128)(2,1)S(1)} %renorm.1.refs_0_), channel_id=1, source_target_pairs={{0,128},{4,132},{8,136},{12,140},{16,144},{20,148},{24,152},{28,15... | collective-permute-start | bytes 589832 | tf_op jit(solution)/shard_map/ppermute | solution.py:29
  55.7 10.9 %collective-permute-start.15 = (bf16[3,16,1024]{2,1,0:T(8,128)(2,1)S(1)}, bf16[3,16,1024]{2,1,0:T(8,128)(2,1)S(1)}, u32[]{:S(2)}, u32[]{:S(2)}) collective-permute-start(bf16[3,16,1024]{2,1,0:T(8,128)(2,1)S(1)} %slice.9), channel_id=1, source_target_pairs={{0,12},{4,0},{8,4},{12,8},{16,28},{20,16},{24,20},{28,24},{32,44},... | collective-permute-start | bytes 294920 | tf_op jit(solution)/shard_map/ppermute | solution.py:29
  59.2 13.4 %collective-permute-start.20 = (bf16[3,32,1024]{2,1,0:T(8,128)(2,1)S(1)}, bf16[3,32,1024]{2,1,0:T(8,128)(2,1)S(1)}, u32[]{:S(2)}, u32[]{:S(2)}) collective-permute-start(bf16[3,32,1024]{2,1,0:T(8,128)(2,1)S(1)} %collective-permute-done.11.refs_4_), channel_id=1, source_target_pairs={{0,16},{4,20},{8,24},{12,28},{16,0},{20,4},{24,8},{28,12},{32,48},... | collective-permute-start | bytes 589832 | tf_op jit(solution)/shard_map/ppermute | solution.py:29
  63.6 8.6 %collective-permute-start.14 = (bf16[3,16,1024]{2,1,0:T(8,128)(2,1)S(1)}, bf16[3,16,1024]{2,1,0:T(8,128)(2,1)S(1)}, u32[]{:S(2)}, u32[]{:S(2)}) collective-permute-start(bf16[3,16,1024]{2,1,0:T(8,128)(2,1)S(1)} %slice.8), channel_id=1, source_target_pairs={{0,4},{4,8},{8,12},{12,0},{16,20},{20,24},{24,28},{28,16},{32,36},... | collective-permute-start | bytes 294920 | tf_op jit(solution)/shard_map/ppermute | solution.py:29
  63.9 9.7 %collective-permute-start.13 = (bf16[3,32,1024]{2,1,0:T(8,128)(2,1)S(1)}, bf16[3,32,1024]{2,1,0:T(8,128)(2,1)S(1)}, u32[]{:S(2)}, u32[]{:S(2)}) collective-permute-start(bf16[3,32,1024]{2,1,0:T(8,128)(2,1)S(1)} %collective-permute-done.11.refs_4_), channel_id=1, source_target_pairs={{0,140},{4,128},{8,132},{12,136},{16,156},{20,144},{24,148},{28,15... | collective-permute-start | bytes 589832 | tf_op jit(solution)/shard_map/ppermute | solution.py:29
  66.6 5.5 %collective-permute-start.24 = (bf16[3,16,1024]{2,1,0:T(8,128)(2,1)S(1)}, bf16[3,16,1024]{2,1,0:T(8,128)(2,1)S(1)}, u32[]{:S(2)}, u32[]{:S(2)}) collective-permute-start(bf16[3,16,1024]{2,1,0:T(8,128)(2,1)S(1)} %collective-permute-done.15.refs_8_), channel_id=1, source_target_pairs={{0,16},{4,20},{8,24},{12,28},{16,0},{20,4},{24,8},{28,12},{32,48},... | collective-permute-start | bytes 294920 | tf_op jit(solution)/shard_map/ppermute | solution.py:29
  67.7 8.7 %collective-permute-start.19 = (bf16[3,32,1024]{2,1,0:T(8,128)(2,1)S(1)}, bf16[3,32,1024]{2,1,0:T(8,128)(2,1)S(1)}, u32[]{:S(2)}, u32[]{:S(2)}) collective-permute-start(bf16[3,32,1024]{2,1,0:T(8,128)(2,1)S(1)} %collective-permute-done.10.refs_3_), channel_id=1, source_target_pairs={{0,16},{4,20},{8,24},{12,28},{16,0},{20,4},{24,8},{28,12},{32,48},... | collective-permute-start | bytes 589832 | tf_op jit(solution)/shard_map/ppermute | solution.py:29
  72.1 6.9 %collective-permute-start.12 = (bf16[3,32,1024]{2,1,0:T(8,128)(2,1)S(1)}, bf16[3,32,1024]{2,1,0:T(8,128)(2,1)S(1)}, u32[]{:S(2)}, u32[]{:S(2)}) collective-permute-start(bf16[3,32,1024]{2,1,0:T(8,128)(2,1)S(1)} %collective-permute-done.10.refs_3_), channel_id=1, source_target_pairs={{0,128},{4,132},{8,136},{12,140},{16,144},{20,148},{24,152},{28,15... | collective-permute-start | bytes 589832 | tf_op jit(solution)/shard_map/ppermute | solution.py:29
  72.2 14.5 %collective-permute-start.29 = (bf16[256,1024]{1,0:T(8,128)(2,1)S(1)}, bf16[256,1024]{1,0:T(8,128)(2,1)S(1)}, u32[]{:S(2)}, u32[]{:S(2)}) collective-permute-start(bf16[256,1024]{1,0:T(8,128)(2,1)S(1)} %copy-done.1), channel_id=1, source_target_pairs={{0,32},{4,36},{8,40},{12,44},{16,48},{20,52},{24,56},{28,60},{32,6... | collective-permute-start | bytes 1572872 | tf_op jit(solution)/shard_map/ppermute | solution.py:29
  72.6 3.4 %collective-permute-start.23 = (bf16[3,16,1024]{2,1,0:T(8,128)(2,1)S(1)}, bf16[3,16,1024]{2,1,0:T(8,128)(2,1)S(1)}, u32[]{:S(2)}, u32[]{:S(2)}) collective-permute-start(bf16[3,16,1024]{2,1,0:T(8,128)(2,1)S(1)} %collective-permute-done.14.refs_7_), channel_id=1, source_target_pairs={{0,16},{4,20},{8,24},{12,28},{16,0},{20,4},{24,8},{28,12},{32,48},... | collective-permute-start | bytes 294920 | tf_op jit(solution)/shard_map/ppermute | solution.py:29
  73.7 24.4 %collective-permute-start.27 = (bf16[256,1024]{1,0:T(8,128)(2,1)S(1)}, bf16[256,1024]{1,0:T(8,128)(2,1)S(1)}, u32[]{:S(2)}, u32[]{:S(2)}) collective-permute-start(bf16[256,1024]{1,0:T(8,128)(2,1)S(1)} %copy-done.1), channel_id=1, source_target_pairs={{0,96},{4,100},{8,104},{12,108},{16,112},{20,116},{24,120},{28,124... | collective-permute-start | bytes 1572872 | tf_op jit(solution)/shard_map/ppermute | solution.py:29
  76.0 4.4 %collective-permute-start.18 = (bf16[3,32,1024]{2,1,0:T(8,128)(2,1)S(1)}, bf16[3,32,1024]{2,1,0:T(8,128)(2,1)S(1)}, u32[]{:S(2)}, u32[]{:S(2)}) collective-permute-start(bf16[3,32,1024]{2,1,0:T(8,128)(2,1)S(1)} %collective-permute-done.9.refs_2_), channel_id=1, source_target_pairs={{0,16},{4,20},{8,24},{12,28},{16,0},{20,4},{24,8},{28,12},{32,48},... | collective-permute-start | bytes 589832 | tf_op jit(solution)/shard_map/ppermute | solution.py:29
  76.3 6.0 %collective-permute-start.17 = (bf16[3,32,1024]{2,1,0:T(8,128)(2,1)S(1)}, bf16[3,32,1024]{2,1,0:T(8,128)(2,1)S(1)}, u32[]{:S(2)}, u32[]{:S(2)}) collective-permute-start(bf16[3,32,1024]{2,1,0:T(8,128)(2,1)S(1)} %collective-permute-done.8.refs_1_), channel_id=1, source_target_pairs={{0,16},{4,20},{8,24},{12,28},{16,0},{20,4},{24,8},{28,12},{32,48},... | collective-permute-start | bytes 589832 | tf_op jit(solution)/shard_map/ppermute | solution.py:29
  79.0 20.2 %collective-permute-start.25 = (bf16[256,1024]{1,0:T(8,128)(2,1)S(1)}, bf16[256,1024]{1,0:T(8,128)(2,1)S(1)}, u32[]{:S(2)}, u32[]{:S(2)}) collective-permute-start(bf16[256,1024]{1,0:T(8,128)(2,1)S(1)} %copy-done.1), channel_id=1, source_target_pairs={{0,64},{4,68},{8,72},{12,76},{16,80},{20,84},{24,88},{28,92},{32,9... | collective-permute-start | bytes 1572872 | tf_op jit(solution)/shard_map/ppermute | solution.py:29
  80.3 3.0 %collective-permute-start.22 = (bf16[3,32,1024]{2,1,0:T(8,128)(2,1)S(1)}, bf16[3,32,1024]{2,1,0:T(8,128)(2,1)S(1)}, u32[]{:S(2)}, u32[]{:S(2)}) collective-permute-start(bf16[3,32,1024]{2,1,0:T(8,128)(2,1)S(1)} %collective-permute-done.13.refs_6_), channel_id=1, source_target_pairs={{0,16},{4,20},{8,24},{12,28},{16,0},{20,4},{24,8},{28,12},{32,48},... | collective-permute-start | bytes 589832 | tf_op jit(solution)/shard_map/ppermute | solution.py:29
  82.3 1.4 %collective-permute-start.21 = (bf16[3,32,1024]{2,1,0:T(8,128)(2,1)S(1)}, bf16[3,32,1024]{2,1,0:T(8,128)(2,1)S(1)}, u32[]{:S(2)}, u32[]{:S(2)}) collective-permute-start(bf16[3,32,1024]{2,1,0:T(8,128)(2,1)S(1)} %collective-permute-done.12.refs_5_), channel_id=1, source_target_pairs={{0,16},{4,20},{8,24},{12,28},{16,0},{20,4},{24,8},{28,12},{32,48},... | collective-permute-start | bytes 589832 | tf_op jit(solution)/shard_map/ppermute | solution.py:29
  86.6 1.9 %copy-start = (bf16[3,512,1024]{2,1,0:T(8,128)(2,1)S(1)}, bf16[3,512,1024]{2,1,0:T(8,128)(2,1)}, u32[]{:S(2)}) copy-start(bf16[3,512,1024]{2,1,0:T(8,128)(2,1)} %join.1.weights) | copy-start | bytes 9437188
  89.6 17.4 %collective-permute-start.30 = (bf16[256,1024]{1,0:T(8,128)(2,1)S(1)}, bf16[256,1024]{1,0:T(8,128)(2,1)S(1)}, u32[]{:S(2)}, u32[]{:S(2)}) collective-permute-start(bf16[256,1024]{1,0:T(8,128)(2,1)S(1)} %render_rows.7), channel_id=1, source_target_pairs={{0,96},{4,100},{8,104},{12,108},{16,112},{20,116},{24,120},{28,124... | collective-permute-start | bytes 1572872 | tf_op jit(solution)/shard_map/ppermute | solution.py:29
  99.2 12.9 %collective-permute-start.28 = (bf16[256,1024]{1,0:T(8,128)(2,1)S(1)}, bf16[256,1024]{1,0:T(8,128)(2,1)S(1)}, u32[]{:S(2)}, u32[]{:S(2)}) collective-permute-start(bf16[256,1024]{1,0:T(8,128)(2,1)S(1)} %render_rows.6), channel_id=1, source_target_pairs={{0,32},{4,36},{8,40},{12,44},{16,48},{20,52},{24,56},{28,60},{32,6... | collective-permute-start | bytes 1572872 | tf_op jit(solution)/shard_map/ppermute | solution.py:29
  100.4 25.7 %collective-permute-start.26 = (bf16[256,1024]{1,0:T(8,128)(2,1)S(1)}, bf16[256,1024]{1,0:T(8,128)(2,1)S(1)}, u32[]{:S(2)}, u32[]{:S(2)}) collective-permute-start(bf16[256,1024]{1,0:T(8,128)(2,1)S(1)} %render_rows.5), channel_id=1, source_target_pairs={{0,64},{4,68},{8,72},{12,76},{16,80},{20,84},{24,88},{28,92},{32,9... | collective-permute-start | bytes 1572872 | tf_op jit(solution)/shard_map/ppermute | solution.py:29

commit v3 on v0

v3 whole, which is shorter than its diff:
```python
import functools

import jax
import jax.numpy as jnp
from jax import lax
from jax.experimental import pallas as pl
from jax.experimental.pallas import tpu as pltpu
from jax.sharding import PartitionSpec as P

AXES = ("view", "render")
LZ, NX, NC, HZ = 2, 4, 2, 4
NZ = LZ * HZ
F32 = jnp.float32
BF16 = jnp.bfloat16
SHORT = pl.CostEstimate(flops=1, bytes_accessed=1, transcendentals=0)


def move(array, target):
    pairs = []
    for zl in range(LZ):
        for x in range(NX):
            for core in range(NC):
                for zh in range(HZ):
                    tl, tx, tc, th = target(zl, x, core, zh)
                    pairs.append(
                        (((zl * NX + x) * NC + core) * HZ + zh, ((tl * NX + tx) * NC + tc) * HZ + th)
                    )
    return lax.ppermute(array, AXES, pairs)


def along_x(array, step):
    return move(array, lambda zl, x, c, zh: (zl, (x + step) % NX, c, zh))


def to_owner(array, step):
    return move(array, lambda zl, x, c, zh: (c, (x + step) % NX, zl, zh))


def along_z(array, step):
    def target(zl, x, c, zh):
        z = (zh * LZ + zl + (1 - 2 * c) * step) % NZ
        return z % LZ, x, c, z // LZ

    return move(array, target)


def swap_core(array):
    return move(array, lambda zl, x, c, zh: (zl, x, 1 - c, zh))


def contract(left, right, left_dim, right_dim):
    return lax.dot_general(
        left, right, (((left_dim,), (right_dim,)), ((), ())), preferred_element_type=F32
    )


def params(mib=32):
    return pltpu.CompilerParams(vmem_limit_bytes=mib * 1024 * 1024)


def delta_kernel(steps, place, rates, keys, values, gate, up, down, mine, other, *refs):
    old = refs[0] if len(refs) > 5 else None
    k_ref, v_ref, columns, turned, sems = refs[-5:]
    x, zl, core = place[0], place[1], place[2]
    units = gate.shape[2] // NX
    half = units // NC
    n = units * len(steps)

    def fetch(m, weight):
        for b, step in enumerate(steps):
            start = pl.multiple_of((x + step) % NX * units, units)
            yield pltpu.make_async_copy(
                weight.at[0, :, pl.ds(start, units)],
                columns.at[m, :, b * units : (b + 1) * units],
                sems.at[2 + m * len(steps) + b],
            )

    copies = [pltpu.make_async_copy(keys, k_ref, sems.at[0]), *fetch(0, gate), *fetch(1, up)]
    later = [pltpu.make_async_copy(values, v_ref, sems.at[1]), *fetch(2, down)]
    for copy in copies + later:
        copy.start()
    for copy in copies:
        copy.wait()
    k = k_ref[...]
    both = contract(jnp.concatenate([columns[0], columns[1]], 1), k, 0, 1)
    gate_in, up_in = both[:n], both[n:]
    for copy in later:
        copy.wait()
    v, r = v_ref[...], rates[...]
    back = contract(columns[2], v, 0, 1)
    s = jax.nn.sigmoid(gate_in)
    act = gate_in * s
    rated = r * back
    turned[0] = (rated * up_in * s * (1.0 + gate_in * (1.0 - s))).astype(BF16)
    turned[1] = (rated * act).astype(BF16)
    turned[2] = (r * (act * up_in)).astype(BF16)
    parts = [(c, b) for c in (1 - core, core) for b in range(len(steps))]
    rows = [pl.ds(pl.multiple_of(b * units + c * half, half), half) for c, b in parts]
    pres = jnp.concatenate([turned[m, part] for part in rows for m in (0, 1)], 0)
    key_sums = contract(pres, k, 1, 0).astype(BF16)
    value_sums = contract(jnp.concatenate([turned[2, part] for part in rows], 0), v, 1, 0).astype(BF16)
    for i in range(len(parts)):
        out, b = (other, mine)[i // len(steps)], i % len(steps)
        out[b, 0] = key_sums[2 * i * half : (2 * i + 1) * half]
        out[b, 1] = key_sums[(2 * i + 1) * half : (2 * i + 2) * half]
        out[b, 2] = value_sums[i * half : (i + 1) * half]
    if old is not None:
        old_turned = refs[1]
        own = pl.ds(pl.multiple_of(zl * half, half), half)
        for m in range(3):
            old_turned[...] = columns[m, :, (len(steps) - 1) * units :].astype(F32).T
            old[m] = old_turned[own, :]


def deltas(place, steps, rates, arrays):
    count, width = arrays[0].shape
    units = arrays[2].shape[2] // NX
    half = units // NC
    n = units * len(steps)
    vmem = pl.BlockSpec(memory_space=pltpu.VMEM)
    out_shape = [jax.ShapeDtypeStruct((len(steps), 3, half, width), BF16)] * 2
    scratch = [
        pltpu.VMEM((count, width), BF16),
        pltpu.VMEM((count, width), BF16),
        pltpu.VMEM((3, width, n), BF16),
        pltpu.VMEM((3, n, count), BF16),
        pltpu.SemaphoreType.DMA((2 + 3 * len(steps),)),
    ]
    if steps[-1] == 0:
        out_shape.append(jax.ShapeDtypeStruct((3, half, width), F32))
        scratch = [pltpu.VMEM((units, width), F32)] + scratch
    return pl.pallas_call(
        functools.partial(delta_kernel, steps),
        name="delta_%d%d" % steps,
        in_specs=[pl.BlockSpec(memory_space=pltpu.SMEM), vmem]
        + [pl.BlockSpec(memory_space=pl.ANY)] * len(arrays),
        out_specs=[vmem] * len(out_shape),
        out_shape=out_shape,
        scratch_shapes=scratch,
        compiler_params=params(52),
        cost_estimate=SHORT,
    )(place, rates, *arrays)


def call(kernel, name, out_shape, *operands):
    vmem = pl.BlockSpec(memory_space=pltpu.VMEM)
    return pl.pallas_call(
        kernel,
        name=name,
        in_specs=[pl.BlockSpec(memory_space=pltpu.SMEM) if o.ndim == 1 else vmem for o in operands],
        out_specs=jax.tree.map(lambda _: vmem, out_shape),
        out_shape=out_shape,
        compiler_params=params(),
        cost_estimate=SHORT,
    )(*operands)


def add_kernel(mine, other, *outs):
    for i, out in enumerate(outs):
        out[...] = (mine[i].astype(F32) + other[i].astype(F32)).astype(out.dtype)


def add_cores(mine, other):
    block = jax.ShapeDtypeStruct(mine.shape[1:], BF16)
    return call(add_kernel, "add_cores", [block] * mine.shape[0], mine, other)


def sum_kernel(*refs):
    sums = refs[0][...].astype(F32)
    for ref in refs[1:-1]:
        sums = sums + ref[...].astype(F32)
    refs[-1][...] = sums.astype(refs[-1].dtype)


def add_up(name, parts):
    return call(sum_kernel, name, jax.ShapeDtypeStruct(parts[0].shape, BF16), *parts)


def renorm_kernel(place, old, mine, other, out):
    half = out.shape[1] // 2
    was = old[...]
    summed = was + (mine[...].astype(F32) + other[...].astype(F32))
    factor = jnp.sqrt(jnp.sum(was * was, axis=-1, keepdims=True)) / jnp.sqrt(
        jnp.sum(summed * summed, axis=-1, keepdims=True) + 1e-06
    )
    new = (summed * factor).astype(BF16)
    core = place[2]
    for i in range(2):
        at = pl.multiple_of((core + i) % 2 * half, half)
        out[:, pl.ds(at, half), :] = new[:, i * half : (i + 1) * half]


def join_kernel(*refs):
    out = refs[-1]
    at = 0
    for ref in refs[:-1]:
        n = ref.shape[1]
        out[:, at : at + n, :] = ref[...]
        at += n


def join(pieces):
    units = sum(p.shape[1] for p in pieces)
    out = jax.ShapeDtypeStruct((3, units, pieces[0].shape[2]), BF16)
    return call(join_kernel, "join", out, *pieces)


def render_kernel(cuts, *refs):
    rows, pieces, out = refs[: len(cuts)], refs[len(cuts) : -1], refs[-1]
    gate, up, down = (jnp.concatenate([p[m] for p in pieces], 0) for m in range(3))
    q = jnp.concatenate([ref[lo:hi, :] for ref, (lo, hi) in zip(rows, cuts)], 0)
    gate_q = contract(q, gate, 1, 1)
    up_q = contract(q, up, 1, 1)
    hidden_q = (gate_q * jax.nn.sigmoid(gate_q) * up_q).astype(BF16)
    out[...] = contract(hidden_q, down, 1, 0).astype(out.dtype)


def render(rows, pieces, dtype):
    cuts = tuple((lo, hi) for _, lo, hi in rows)
    out = jax.ShapeDtypeStruct((sum(hi - lo for lo, hi in cuts), pieces[0].shape[2]), dtype)
    kernel = functools.partial(render_kernel, cuts)
    return call(kernel, "render_rows", out, *[r[0] for r in rows], *pieces)


def merge_kernel(mid, from_left, from_right, to_right, to_left):
    half = to_right.shape[0]
    to_right[...] = (mid[:half] + from_left[:half].astype(F32)).astype(BF16)
    to_left[...] = (mid[half:] + from_right[:half].astype(F32)).astype(BF16)


def total_kernel(own, from_left, from_right, last_left, last_right, out):
    half = last_left.shape[0]
    top = own[:half] + from_right[half:].astype(F32) + last_left[...].astype(F32)
    low = own[half:] + from_left[half:].astype(F32) + last_right[...].astype(F32)
    out[:half] = top.astype(BF16)
    out[half:] = low.astype(BF16)


def local(input_keys, input_values, token_rates, gate_weight, up_weight, down_weight, queries):
    view = lax.axis_index("view")
    zl, x, core = view // (NX * NC), (view // NC) % NX, view % NC
    place = jnp.stack([x, zl, core]).astype(jnp.int32)

    arrays = (input_keys, input_values, gate_weight, up_weight, down_weight)
    mine, other = deltas(place, (2, 1), token_rates, arrays)
    first = swap_core(other)
    second_mine, other, old = deltas(place, (3, 0), token_rates, arrays)
    chip2, chip1 = add_cores(mine, first)
    got2, got1 = to_owner(chip2, 2), to_owner(chip1, 1)
    chip3, chip0 = add_cores(second_mine, swap_core(other))
    got3, got0 = to_owner(chip3, 3), to_owner(chip0, 0)
    sums = add_up("sum_chips", [got2, got1, got3, got0])
    sums, queries = lax.optimization_barrier((sums, queries))
    out = jax.ShapeDtypeStruct(old.shape, BF16)
    new = call(renorm_kernel, "renorm", out, place, old, sums, swap_core(sums))

    half = queries.shape[0] // 2
    from_right, from_left = along_x(queries, -1), along_x(queries, 1)
    near1, near2 = along_z(new, 1), along_z(new, 2)
    near1, near2, from_right, from_left = lax.optimization_barrier((near1, near2, from_right, from_left))
    far_top, far_low = along_x(from_right[:half], -1), along_x(from_left[half:], 1)
    third, fourth = along_z(near2, 1), along_z(near2[:, : new.shape[1] // 2], 2)
    near = join([near1, near2])
    near_other = swap_core(near)
    third, fourth, far_top, far_low, near_other = lax.optimization_barrier(
        (third, fourth, far_top, far_low, near_other)
    )
    last = join([third, fourth])
    pieces = [new, near, near_other, last, swap_core(last)]

    both = 2 * half
    to_right = render([(far_top, 0, half), (from_right, half, both)], pieces, BF16)
    to_left = render([(far_low, 0, half), (from_left, 0, half)], pieces, BF16)
    got_left, got_right = along_x(to_right, 1), along_x(to_left, -1)
    mid = render([(from_right, 0, half), (from_left, half, both)], pieces, F32)
    own = render([(queries, 0, both)], pieces, F32)
    part = jax.ShapeDtypeStruct((half, own.shape[1]), BF16)
    to_right, to_left = call(merge_kernel, "merge", [part] * 2, mid, got_left, got_right)
    last_left, last_right = along_x(to_right, 1), along_x(to_left, -1)
    out = jax.ShapeDtypeStruct(own.shape, BF16)
    return call(total_kernel, "total", out, own, got_left, got_right, last_left, last_right)


def solution(mesh):
    return jax.shard_map(
        local,
        mesh=mesh,
        in_specs=(
            P("view", "head"),
            P("view", "head"),
            P("head", "view"),
            P("head", None, "render"),
            P("head", None, "render"),
            P("head", None, "render"),
            P(("view", "render"), "head"),
        ),
        out_specs=P(("view", "render"), "head"),
        check_vma=False,
    )
```

time: 436 us -> 106 us (0.24); the launches traced: 428 us -> 104 us
  waiting for transfers between devices: 371 us -> 46.8 us
  starting transfers between devices: 0.31 us -> 35.5 us
  matrix products: 26.9 us -> 0 us
  Pallas kernels: 0 us -> 20.9 us
  between operations: 13.3 us -> 0.17 us
  other arithmetic: 10.4 us -> 0.08 us
  local copies, waits for them, and re-layouts: 6.24 us -> 0.75 us
    all_gather x3 -> x0, waiting for transfers between devices: 240 us -> none  [the longest x1 86.2 us: local(): lax.all_gather(new_down, 'render', axis=2, tiled=True)[0]]
    psum x1 -> x0, waiting for transfers between devices: 130 us -> none  [local(): lax.psum(grad_down.astype(jnp.bfloat16), 'view').astype(jnp.float32)]
    ppermute x0 -> x21, waiting for transfers between devices: none -> 46.8 us  [move(): return lax.ppermute(array, AXES, pairs)]
    ppermute x0 -> x21, starting transfers between devices: none -> 35.5 us  [move(): return lax.ppermute(array, AXES, pairs)]
    dot_general x8 -> x0, matrix products: 26.9 us -> none  [the longest x1 9.14 us: render_rows(): lax.dot_general(hidden_q, piece_down, (((1,), (1,)), ((), ())), preferred...]
    pallas_call x0 -> x14, Pallas kernels: none -> 20.9 us  [the longest x2 14 us: deltas(): pl.pallas_call(functools.partial(delta_kernel, steps), name='delta_%d%d'...]
    unnamed x24 -> x6, local copies, waits for them, and re-layouts: 6.24 us -> 0.7 us
    convert_element_type x3 -> x0, other arithmetic: 5.22 us -> none  [renorm(): return (summed * factor).astype(jnp.bfloat16)]
  transfers between devices with their start and end apart: 4 -> 21, of which waited for: 4 -> 12; matrix products, arithmetic and copies ran while one was open for 3% -> 0% of each run, Pallas kernels for 0% -> 11%
where the time goes in v3:
time: 106 us; the launch traced here: 104 us
  waiting for transfers between devices  46.8 us (44%)
  starting transfers between devices  35.5 us (33%)
  Pallas kernels  20.9 us (20%)
    ppermute x21, waiting for transfers between devices, move(): return lax.ppermute(array, AXES, pairs)  46.8 us
    ppermute x21, starting transfers between devices, move(): return lax.ppermute(array, AXES, pairs)  35.5 us
    pallas_call x2, Pallas kernels, deltas(): pl.pallas_call(functools.partial(delta_kernel, steps), name='delta_%d%d'...  14 us
    pallas_call x12, Pallas kernels, call(): pl.pallas_call(kernel, name=name, in_specs=[pl.BlockSpec(memory_space=plt...  6.89 us
  transfers between devices with their start and end apart: 21, of which 12 were waited for; matrix products, arithmetic and copies ran while one was open for 0% of the time, Pallas kernels for 11%

profile of v3, /device:TPU:1, one launch (start us, length us, event | category | flops | bytes accessed | tf_op | source)
XLA Modules:
  0.0 104.2 jit_solution(8452538596103392218)
XLA Ops:
  0.0 0.1 pad_add_fusion.place
  0.1 0.0 copy-start.2
  0.1 0.7 copy-done.2
  0.8 6.6 %delta_21.1 = (bf16[2,3,64,1024]{3,2,1,0:T(8,128)(2,1)S(1)}, bf16[2,3,64,1024]{3,2,1,0:T(8,128)(2,1)S(1)}) custom-call(s32[3]{0:T(128)S(1)} %pad_add_fusion.place, f32[1,1024]{1,0:T(1,128)S(1)} %copy-done.2, bf16[1024,1024]{1,0:T(8,128)(2,1)} %keys.3, bf16[1024,1024]{1,0:T(8,128)(2,1)} %values.3, bf16[1,1024,512]{2,1,0:T(8,128)(2,1)} %gate.3, ...), custom_call_target="tpu_custom_call" | custom-call | flops 1 | bytes 1 | tf_op jit(solution)/shard_map/delta_21/pallas_call | solution.py:132
  7.4 3.3 %collective-permute-start = (bf16[2,3,64,1024]{3,2,1,0:T(8,128)(2,1)S(1)}, bf16[2,3,64,1024]{3,2,1,0:T(8,128)(2,1)S(1)}, u32[]{:S(2)}, u32[]{:S(2)}) collective-permute-start(bf16[2,3,64,1024]{3,2,1,0:T(8,128)(2,1)S(1)} %get-tuple-element.28), channel_id=1, source_target_pairs={{0,16},{4,20},{8,24},{12,28},{16,0},{20,4},{24,8},{28,12},{32,48},... | collective-permute-start | bytes 2359304 | tf_op jit(solution)/shard_map/ppermute | solution.py:28
  10.7 7.4 %delta_30.1 = (bf16[2,3,64,1024]{3,2,1,0:T(8,128)(2,1)S(1)}, bf16[2,3,64,1024]{3,2,1,0:T(8,128)(2,1)S(1)}, f32[3,64,1024]{2,1,0:T(8,128)}) custom-call(s32[3]{0:T(128)S(1)} %pad_add_fusion.place, f32[1,1024]{1,0:T(1,128)S(1)} %copy-done.2, bf16[1024,1024]{1,0:T(8,128)(2,1)} %keys.3, bf16[1024,1024]{1,0:T(8,128)(2,1)} %values.3, bf16[1,1024,512]{2,1,0:T(8,128)(2,1)} %gate.3, ...), custom_call_target="tpu_custom_call" | custom-call | flops 1 | bytes 1 | tf_op jit(solution)/shard_map/delta_30/pallas_call | solution.py:132
  18.1 0.1 collective-permute-start.3
  18.2 0.0 collective-permute-done.other
  18.2 0.2 add_cores.2
  18.4 0.0 copy-start.1
  18.4 0.0 copy-start
  18.4 2.8 %collective-permute-start.1 = (bf16[3,64,1024]{2,1,0:T(8,128)(2,1)S(1)}, bf16[3,64,1024]{2,1,0:T(8,128)(2,1)S(1)}, u32[]{:S(2)}, u32[]{:S(2)}) collective-permute-start(bf16[3,64,1024]{2,1,0:T(8,128)(2,1)S(1)} %get-tuple-element.29), channel_id=1, source_target_pairs={{0,64},{4,68},{8,72},{12,76},{16,192},{20,196},{24,200},{28,204},{... | collective-permute-start | bytes 1179656 | tf_op jit(solution)/shard_map/ppermute | solution.py:28
  21.3 0.0 collective-permute-start.2
  21.3 0.0 collective-permute-done.3.other
  21.3 0.2 add_cores.3
  21.5 3.9 %collective-permute-start.4 = (bf16[3,64,1024]{2,1,0:T(8,128)(2,1)S(1)}, bf16[3,64,1024]{2,1,0:T(8,128)(2,1)S(1)}, u32[]{:S(2)}, u32[]{:S(2)}) collective-permute-start(bf16[3,64,1024]{2,1,0:T(8,128)(2,1)S(1)} %get-tuple-element.33), channel_id=1, source_target_pairs={{0,96},{4,100},{8,104},{12,108},{16,224},{20,228},{24,232},{28,236... | collective-permute-start | bytes 1179656 | tf_op jit(solution)/shard_map/ppermute | solution.py:28
  25.4 1.9 %collective-permute-start.5 = (bf16[3,64,1024]{2,1,0:T(8,128)(2,1)S(1)}, bf16[3,64,1024]{2,1,0:T(8,128)(2,1)S(1)}, u32[]{:S(2)}, u32[]{:S(2)}) collective-permute-start(bf16[3,64,1024]{2,1,0:T(8,128)(2,1)S(1)} %get-tuple-element.34), channel_id=1, source_target_pairs={{0,0},{4,4},{8,8},{12,12},{16,128},{20,132},{24,136},{28,140},{32,... | collective-permute-start | bytes 1179656 | tf_op jit(solution)/shard_map/ppermute | solution.py:28
  27.3 2.1 %collective-permute-done.1.refs_0_ = bf16[3,64,1024]{2,1,0:T(8,128)(2,1)S(1)} collective-permute-done((bf16[3,64,1024]{2,1,0:T(8,128)(2,1)S(1)}, bf16[3,64,1024]{2,1,0:T(8,128)(2,1)S(1)}, u32[]{:S(2)}, u32[]{:S(2)}) %collective-permute-start.1) | collective-permute-done | bytes 393248 | tf_op jit(solution)/shard_map/ppermute | solution.py:28
  29.4 3.3 %collective-permute-done.2.refs_1_ = bf16[3,64,1024]{2,1,0:T(8,128)(2,1)S(1)} collective-permute-done((bf16[3,64,1024]{2,1,0:T(8,128)(2,1)S(1)}, bf16[3,64,1024]{2,1,0:T(8,128)(2,1)S(1)}, u32[]{:S(2)}, u32[]{:S(2)}) %collective-permute-start.2) | collective-permute-done | bytes 393248 | tf_op jit(solution)/shard_map/ppermute | solution.py:28
  32.8 3.5 %collective-permute-done.4.refs_2_ = bf16[3,64,1024]{2,1,0:T(8,128)(2,1)S(1)} collective-permute-done((bf16[3,64,1024]{2,1,0:T(8,128)(2,1)S(1)}, bf16[3,64,1024]{2,1,0:T(8,128)(2,1)S(1)}, u32[]{:S(2)}, u32[]{:S(2)}) %collective-permute-start.4) | collective-permute-done | bytes 393248 | tf_op jit(solution)/shard_map/ppermute | solution.py:28
  36.3 3.2 %collective-permute-done.5.refs_3_ = bf16[3,64,1024]{2,1,0:T(8,128)(2,1)S(1)} collective-permute-done((bf16[3,64,1024]{2,1,0:T(8,128)(2,1)S(1)}, bf16[3,64,1024]{2,1,0:T(8,128)(2,1)S(1)}, u32[]{:S(2)}, u32[]{:S(2)}) %collective-permute-start.5) | collective-permute-done | bytes 393248 | tf_op jit(solution)/shard_map/ppermute | solution.py:28
  39.5 0.2 sum_chips.1.mine
  39.7 1.6 %collective-permute-start.6 = (bf16[3,64,1024]{2,1,0:T(8,128)(2,1)S(1)}, bf16[3,64,1024]{2,1,0:T(8,128)(2,1)S(1)}, u32[]{:S(2)}, u32[]{:S(2)}) collective-permute-start(bf16[3,64,1024]{2,1,0:T(8,128)(2,1)S(1)} %sum_chips.1.mine), channel_id=1, source_target_pairs={{0,16},{4,20},{8,24},{12,28},{16,0},{20,4},{24,8},{28,12},{32,48},... | collective-permute-start | bytes 1179656 | tf_op jit(solution)/shard_map/ppermute | solution.py:28
  41.2 0.0 copy-done.1
  41.2 0.0 collective-permute-start.10
  41.2 2.7 %collective-permute-start.9 = (bf16[256,1024]{1,0:T(8,128)(2,1)S(1)}, bf16[256,1024]{1,0:T(8,128)(2,1)S(1)}, u32[]{:S(2)}, u32[]{:S(2)}) collective-permute-start(bf16[256,1024]{1,0:T(8,128)(2,1)S(1)} %copy-done.1), channel_id=1, source_target_pairs={{0,96},{4,100},{8,104},{12,108},{16,112},{20,116},{24,120},{28,124... | collective-permute-start | bytes 1572872 | tf_op jit(solution)/shard_map/ppermute | solution.py:28
  43.9 0.0 collective-permute-done.6.other
  43.9 0.0 copy-done
  43.9 0.9 renorm.1.refs_1_.refs_2_
  44.8 4.5 %collective-permute-start.8 = (bf16[3,64,1024]{2,1,0:T(8,128)(2,1)S(1)}, bf16[3,64,1024]{2,1,0:T(8,128)(2,1)S(1)}, u32[]{:S(2)}, u32[]{:S(2)}) collective-permute-start(bf16[3,64,1024]{2,1,0:T(8,128)(2,1)S(1)} %renorm.1.refs_1_.refs_2_), channel_id=1, source_target_pairs={{0,4},{4,8},{8,12},{12,0},{16,28},{20,16},{24,20},{28,24},{32,36},... | collective-permute-start | bytes 1179656 | tf_op jit(solution)/shard_map/ppermute | solution.py:28
  49.3 1.1 %collective-permute-start.7 = (bf16[3,64,1024]{2,1,0:T(8,128)(2,1)S(1)}, bf16[3,64,1024]{2,1,0:T(8,128)(2,1)S(1)}, u32[]{:S(2)}, u32[]{:S(2)}) collective-permute-start(bf16[3,64,1024]{2,1,0:T(8,128)(2,1)S(1)} %renorm.1.refs_1_.refs_2_), channel_id=1, source_target_pairs={{0,128},{4,132},{8,136},{12,140},{16,156},{20,144},{24,148},{28,15... | collective-permute-start | bytes 1179656 | tf_op jit(solution)/shard_map/ppermute | solution.py:28
  50.3 5.6 %collective-permute-done.10.refs_1_ = bf16[256,1024]{1,0:T(8,128)(2,1)S(1)} collective-permute-done((bf16[256,1024]{1,0:T(8,128)(2,1)S(1)}, bf16[256,1024]{1,0:T(8,128)(2,1)S(1)}, u32[]{:S(2)}, u32[]{:S(2)}) %collective-permute-start.10) | collective-permute-done | bytes 524320 | tf_op jit(solution)/shard_map/ppermute | solution.py:28
  55.9 0.0 collective-permute-done.9.refs_1_.refs_0_
  55.9 1.0 collective-permute-done.8.refs_1_
  56.9 6.5 %collective-permute-done.7.refs_0_ = bf16[3,64,1024]{2,1,0:T(8,128)(2,1)S(1)} collective-permute-done((bf16[3,64,1024]{2,1,0:T(8,128)(2,1)S(1)}, bf16[3,64,1024]{2,1,0:T(8,128)(2,1)S(1)}, u32[]{:S(2)}, u32[]{:S(2)}) %collective-permute-start.7) | collective-permute-done | bytes 393248 | tf_op jit(solution)/shard_map/ppermute | solution.py:28
  63.4 0.1 join.2.refs_2_.refs_3_
  63.5 0.9 collective-permute-start.15
  64.4 1.3 %collective-permute-start.11 = (bf16[3,64,1024]{2,1,0:T(8,128)(2,1)S(1)}, bf16[3,64,1024]{2,1,0:T(8,128)(2,1)S(1)}, u32[]{:S(2)}, u32[]{:S(2)}) collective-permute-start(bf16[3,64,1024]{2,1,0:T(8,128)(2,1)S(1)} %collective-permute-done.8.refs_1_), channel_id=1, source_target_pairs={{0,128},{4,132},{8,136},{12,140},{16,156},{20,144},{24,148},{28,15... | collective-permute-start | bytes 1179656 | tf_op jit(solution)/shard_map/ppermute | solution.py:28
  65.8 0.3 collective-permute-start.14
  66.1 2.5 %collective-permute-start.13 = (bf16[128,1024]{1,0:T(8,128)(2,1)S(1)}, bf16[128,1024]{1,0:T(8,128)(2,1)S(1)}, u32[]{:S(2)}, u32[]{:S(2)}) collective-permute-start(bf16[128,1024]{1,0:T(8,128)(2,1)S(1)} %slice.10), channel_id=1, source_target_pairs={{0,96},{4,100},{8,104},{12,108},{16,112},{20,116},{24,120},{28,124... | collective-permute-start | bytes 786440 | tf_op jit(solution)/shard_map/ppermute | solution.py:28
  68.6 2.1 %collective-permute-start.12 = (bf16[3,32,1024]{2,1,0:T(8,128)(2,1)S(1)}, bf16[3,32,1024]{2,1,0:T(8,128)(2,1)S(1)}, u32[]{:S(2)}, u32[]{:S(2)}) collective-permute-start(bf16[3,32,1024]{2,1,0:T(8,128)(2,1)S(1)} %slice.9), channel_id=1, source_target_pairs={{0,4},{4,8},{8,12},{12,0},{16,28},{20,16},{24,20},{28,24},{32,36},... | collective-permute-start | bytes 589832 | tf_op jit(solution)/shard_map/ppermute | solution.py:28
  70.7 5.6 %collective-permute-done.12.refs_1_ = bf16[3,32,1024]{2,1,0:T(8,128)(2,1)S(1)} collective-permute-done((bf16[3,32,1024]{2,1,0:T(8,128)(2,1)S(1)}, bf16[3,32,1024]{2,1,0:T(8,128)(2,1)S(1)}, u32[]{:S(2)}, u32[]{:S(2)}) %collective-permute-start.12) | collective-permute-done | bytes 196640 | tf_op jit(solution)/shard_map/ppermute | solution.py:28
  76.2 0.0 collective-permute-done.14.refs_0_
  76.2 0.0 collective-permute-done.13.refs_0_
  76.2 0.0 collective-permute-done.11.refs_0_
  76.2 0.0 collective-permute-done.15.refs_3_.refs_4_
  76.3 0.1 collective-permute-start.16
  76.4 2.0 %collective-permute-done.16.refs_5_.refs_6_ = bf16[3,96,1024]{2,1,0:T(8,128)(2,1)S(1)} collective-permute-done((bf16[3,96,1024]{2,1,0:T(8,128)(2,1)S(1)}, bf16[3,96,1024]{2,1,0:T(8,128)(2,1)S(1)}, u32[]{:S(2)}, u32[]{:S(2)}) %collective-permute-start.16) | collective-permute-done | bytes 589856 | tf_op jit(solution)/shard_map/ppermute | solution.py:28
  78.4 1.1 %render_rows.5 = bf16[256,1024]{1,0:T(8,128)(2,1)S(1)} custom-call(bf16[128,1024]{1,0:T(8,128)(2,1)S(1)} %collective-permute-done.13.refs_0_, bf16[256,1024]{1,0:T(8,128)(2,1)S(1)} %collective-permute-done.9.refs_1_.refs_0_, bf16[3,64,1024]{2,1,0:T(8,128)(2,1)S(1)} %renorm.1.refs_1_.refs_2_, bf16[3,128,1024]{2,1,0:T(8,128)(2,1)S(1)} %join.2.refs_2_.refs_3_, ...), custom_call_target="tpu_custom_call" | custom-call | flops 1 | bytes 1 | tf_op jit(solution)/shard_map/render_rows/pallas_call | solution.py:147
  79.5 0.2 collective-permute-start.17
  79.7 1.1 %render_rows.6 = bf16[256,1024]{1,0:T(8,128)(2,1)S(1)} custom-call(bf16[128,1024]{1,0:T(8,128)(2,1)S(1)} %collective-permute-done.14.refs_0_, bf16[256,1024]{1,0:T(8,128)(2,1)S(1)} %collective-permute-done.10.refs_1_, bf16[3,64,1024]{2,1,0:T(8,128)(2,1)S(1)} %renorm.1.refs_1_.refs_2_, bf16[3,128,1024]{2,1,0:T(8,128)(2,1)S(1)} %join.2.refs_2_.refs_3_, ...), custom_call_target="tpu_custom_call" | custom-call | flops 1 | bytes 1 | tf_op jit(solution)/shard_map/render_rows/pallas_call | solution.py:147
  80.8 2.6 %collective-permute-start.18 = (bf16[256,1024]{1,0:T(8,128)(2,1)S(1)}, bf16[256,1024]{1,0:T(8,128)(2,1)S(1)}, u32[]{:S(2)}, u32[]{:S(2)}) collective-permute-start(bf16[256,1024]{1,0:T(8,128)(2,1)S(1)} %render_rows.6), channel_id=1, source_target_pairs={{0,96},{4,100},{8,104},{12,108},{16,112},{20,116},{24,120},{28,124... | collective-permute-start | bytes 1572872 | tf_op jit(solution)/shard_map/ppermute | solution.py:28
  83.4 1.1 %render_rows.7.mid = f32[256,1024]{1,0:T(8,128)S(1)} custom-call(bf16[256,1024]{1,0:T(8,128)(2,1)S(1)} %collective-permute-done.9.refs_1_.refs_0_, bf16[256,1024]{1,0:T(8,128)(2,1)S(1)} %collective-permute-done.10.refs_1_, bf16[3,64,1024]{2,1,0:T(8,128)(2,1)S(1)} %renorm.1.refs_1_.refs_2_, bf16[3,128,1024]{2,1,0:T(8,128)(2,1)S(1)} %join.2.refs_2_.refs_3_, ...), custom_call_target="tpu_custom_call" | custom-call | flops 1 | bytes 1 | tf_op jit(solution)/shard_map/render_rows/pallas_call | solution.py:147
  84.5 9.6 %collective-permute-done.17.from_left = bf16[256,1024]{1,0:T(8,128)(2,1)S(1)} collective-permute-done((bf16[256,1024]{1,0:T(8,128)(2,1)S(1)}, bf16[256,1024]{1,0:T(8,128)(2,1)S(1)}, u32[]{:S(2)}, u32[]{:S(2)}) %collective-permute-start.17) | collective-permute-done | bytes 524320 | tf_op jit(solution)/shard_map/ppermute | solution.py:28
  94.2 0.1 collective-permute-done.18.from_right
  94.3 0.1 merge.1
  94.4 0.1 collective-permute-start.19
  94.5 3.5 %collective-permute-start.20 = (bf16[128,1024]{1,0:T(8,128)(2,1)S(1)}, bf16[128,1024]{1,0:T(8,128)(2,1)S(1)}, u32[]{:S(2)}, u32[]{:S(2)}) collective-permute-start(bf16[128,1024]{1,0:T(8,128)(2,1)S(1)} %get-tuple-element.48), channel_id=1, source_target_pairs={{0,96},{4,100},{8,104},{12,108},{16,112},{20,116},{24,120},{28,124... | collective-permute-start | bytes 786440 | tf_op jit(solution)/shard_map/ppermute | solution.py:28
  98.0 1.1 %render_rows.4.own = f32[256,1024]{1,0:T(8,128)S(1)} custom-call(bf16[256,1024]{1,0:T(8,128)(2,1)S(1)} %copy-done.1, bf16[3,64,1024]{2,1,0:T(8,128)(2,1)S(1)} %renorm.1.refs_1_.refs_2_, bf16[3,128,1024]{2,1,0:T(8,128)(2,1)S(1)} %join.2.refs_2_.refs_3_, bf16[3,128,1024]{2,1,0:T(8,128)(2,1)S(1)} %collective-permute-done.15.refs_3_.refs_4_, ...), custom_call_target="tpu_custom_call" | custom-call | flops 1 | bytes 1 | tf_op jit(solution)/shard_map/render_rows/pallas_call | solution.py:147
  99.0 4.2 %collective-permute-done.19.last_left = bf16[128,1024]{1,0:T(8,128)(2,1)S(1)} collective-permute-done((bf16[128,1024]{1,0:T(8,128)(2,1)S(1)}, bf16[128,1024]{1,0:T(8,128)(2,1)S(1)}, u32[]{:S(2)}, u32[]{:S(2)}) %collective-permute-start.19) | collective-permute-done | bytes 262176 | tf_op jit(solution)/shard_map/ppermute | solution.py:28
  103.2 0.0 collective-permute-done.20.last_right
  103.2 0.9 total.1
  (4 shorter events, 0.1 us)
Async XLA Ops:
  0.1 0.7 copy-start.2
  7.4 10.9 %collective-permute-start = (bf16[2,3,64,1024]{3,2,1,0:T(8,128)(2,1)S(1)}, bf16[2,3,64,1024]{3,2,1,0:T(8,128)(2,1)S(1)}, u32[]{:S(2)}, u32[]{:S(2)}) collective-permute-start(bf16[2,3,64,1024]{3,2,1,0:T(8,128)(2,1)S(1)} %get-tuple-element.28), channel_id=1, source_target_pairs={{0,16},{4,20},{8,24},{12,28},{16,0},{20,4},{24,8},{28,12},{32,48},... | collective-permute-start | bytes 2359304 | tf_op jit(solution)/shard_map/ppermute | solution.py:28
  18.1 3.1 %collective-permute-start.3 = (bf16[2,3,64,1024]{3,2,1,0:T(8,128)(2,1)S(1)}, bf16[2,3,64,1024]{3,2,1,0:T(8,128)(2,1)S(1)}, u32[]{:S(2)}, u32[]{:S(2)}) collective-permute-start(bf16[2,3,64,1024]{3,2,1,0:T(8,128)(2,1)S(1)} %get-tuple-element.32), channel_id=1, source_target_pairs={{0,16},{4,20},{8,24},{12,28},{16,0},{20,4},{24,8},{28,12},{32,48},... | collective-permute-start | bytes 2359304 | tf_op jit(solution)/shard_map/ppermute | solution.py:28
  18.4 22.8 %copy-start.1 = (bf16[256,1024]{1,0:T(8,128)(2,1)S(1)}, bf16[256,1024]{1,0:T(8,128)(2,1)}, u32[]{:S(2)}) copy-start(bf16[256,1024]{1,0:T(8,128)(2,1)} %refs_0_) | copy-start | bytes 1572868
  18.4 25.5 %copy-start = (f32[3,64,1024]{2,1,0:T(8,128)S(1)}, f32[3,64,1024]{2,1,0:T(8,128)}, u32[]{:S(2)}) copy-start(f32[3,64,1024]{2,1,0:T(8,128)} %get-tuple-element.36.old) | copy-start | bytes 2359300
  18.4 11.0 %collective-permute-start.1 = (bf16[3,64,1024]{2,1,0:T(8,128)(2,1)S(1)}, bf16[3,64,1024]{2,1,0:T(8,128)(2,1)S(1)}, u32[]{:S(2)}, u32[]{:S(2)}) collective-permute-start(bf16[3,64,1024]{2,1,0:T(8,128)(2,1)S(1)} %get-tuple-element.29), channel_id=1, source_target_pairs={{0,64},{4,68},{8,72},{12,76},{16,192},{20,196},{24,200},{28,204},{... | collective-permute-start | bytes 1179656 | tf_op jit(solution)/shard_map/ppermute | solution.py:28
  21.3 11.5 %collective-permute-start.2 = (bf16[3,64,1024]{2,1,0:T(8,128)(2,1)S(1)}, bf16[3,64,1024]{2,1,0:T(8,128)(2,1)S(1)}, u32[]{:S(2)}, u32[]{:S(2)}) collective-permute-start(bf16[3,64,1024]{2,1,0:T(8,128)(2,1)S(1)} %get-tuple-element.30), channel_id=1, source_target_pairs={{0,32},{4,36},{8,40},{12,44},{16,160},{20,164},{24,168},{28,172},{... | collective-permute-start | bytes 1179656 | tf_op jit(solution)/shard_map/ppermute | solution.py:28
  21.5 14.8 %collective-permute-start.4 = (bf16[3,64,1024]{2,1,0:T(8,128)(2,1)S(1)}, bf16[3,64,1024]{2,1,0:T(8,128)(2,1)S(1)}, u32[]{:S(2)}, u32[]{:S(2)}) collective-permute-start(bf16[3,64,1024]{2,1,0:T(8,128)(2,1)S(1)} %get-tuple-element.33), channel_id=1, source_target_pairs={{0,96},{4,100},{8,104},{12,108},{16,224},{20,228},{24,232},{28,236... | collective-permute-start | bytes 1179656 | tf_op jit(solution)/shard_map/ppermute | solution.py:28
  25.4 14.1 %collective-permute-start.5 = (bf16[3,64,1024]{2,1,0:T(8,128)(2,1)S(1)}, bf16[3,64,1024]{2,1,0:T(8,128)(2,1)S(1)}, u32[]{:S(2)}, u32[]{:S(2)}) collective-permute-start(bf16[3,64,1024]{2,1,0:T(8,128)(2,1)S(1)} %get-tuple-element.34), channel_id=1, source_target_pairs={{0,0},{4,4},{8,8},{12,12},{16,128},{20,132},{24,136},{28,140},{32,... | collective-permute-start | bytes 1179656 | tf_op jit(solution)/shard_map/ppermute | solution.py:28
  39.7 4.3 %collective-permute-start.6 = (bf16[3,64,1024]{2,1,0:T(8,128)(2,1)S(1)}, bf16[3,64,1024]{2,1,0:T(8,128)(2,1)S(1)}, u32[]{:S(2)}, u32[]{:S(2)}) collective-permute-start(bf16[3,64,1024]{2,1,0:T(8,128)(2,1)S(1)} %sum_chips.1.mine), channel_id=1, source_target_pairs={{0,16},{4,20},{8,24},{12,28},{16,0},{20,4},{24,8},{28,12},{32,48},... | collective-permute-start | bytes 1179656 | tf_op jit(solution)/shard_map/ppermute | solution.py:28
  41.2 14.7 %collective-permute-start.10 = (bf16[256,1024]{1,0:T(8,128)(2,1)S(1)}, bf16[256,1024]{1,0:T(8,128)(2,1)S(1)}, u32[]{:S(2)}, u32[]{:S(2)}) collective-permute-start(bf16[256,1024]{1,0:T(8,128)(2,1)S(1)} %copy-done.1), channel_id=1, source_target_pairs={{0,32},{4,36},{8,40},{12,44},{16,48},{20,52},{24,56},{28,60},{32,6... | collective-permute-start | bytes 1572872 | tf_op jit(solution)/shard_map/ppermute | solution.py:28
  41.2 14.7 %collective-permute-start.9 = (bf16[256,1024]{1,0:T(8,128)(2,1)S(1)}, bf16[256,1024]{1,0:T(8,128)(2,1)S(1)}, u32[]{:S(2)}, u32[]{:S(2)}) collective-permute-start(bf16[256,1024]{1,0:T(8,128)(2,1)S(1)} %copy-done.1), channel_id=1, source_target_pairs={{0,96},{4,100},{8,104},{12,108},{16,112},{20,116},{24,120},{28,124... | collective-permute-start | bytes 1572872 | tf_op jit(solution)/shard_map/ppermute | solution.py:28
  44.8 12.2 %collective-permute-start.8 = (bf16[3,64,1024]{2,1,0:T(8,128)(2,1)S(1)}, bf16[3,64,1024]{2,1,0:T(8,128)(2,1)S(1)}, u32[]{:S(2)}, u32[]{:S(2)}) collective-permute-start(bf16[3,64,1024]{2,1,0:T(8,128)(2,1)S(1)} %renorm.1.refs_1_.refs_2_), channel_id=1, source_target_pairs={{0,4},{4,8},{8,12},{12,0},{16,28},{20,16},{24,20},{28,24},{32,36},... | collective-permute-start | bytes 1179656 | tf_op jit(solution)/shard_map/ppermute | solution.py:28
  49.3 14.2 %collective-permute-start.7 = (bf16[3,64,1024]{2,1,0:T(8,128)(2,1)S(1)}, bf16[3,64,1024]{2,1,0:T(8,128)(2,1)S(1)}, u32[]{:S(2)}, u32[]{:S(2)}) collective-permute-start(bf16[3,64,1024]{2,1,0:T(8,128)(2,1)S(1)} %renorm.1.refs_1_.refs_2_), channel_id=1, source_target_pairs={{0,128},{4,132},{8,136},{12,140},{16,156},{20,144},{24,148},{28,15... | collective-permute-start | bytes 1179656 | tf_op jit(solution)/shard_map/ppermute | solution.py:28
  63.5 12.8 %collective-permute-start.15 = (bf16[3,128,1024]{2,1,0:T(8,128)(2,1)S(1)}, bf16[3,128,1024]{2,1,0:T(8,128)(2,1)S(1)}, u32[]{:S(2)}, u32[]{:S(2)}) collective-permute-start(bf16[3,128,1024]{2,1,0:T(8,128)(2,1)S(1)} %join.2.refs_2_.refs_3_), channel_id=1, source_target_pairs={{0,16},{4,20},{8,24},{12,28},{16,0},{20,4},{24,8},{28,12},{32,48},... | collective-permute-start | bytes 2359304 | tf_op jit(solution)/shard_map/ppermute | solution.py:28
  64.4 11.8 %collective-permute-start.11 = (bf16[3,64,1024]{2,1,0:T(8,128)(2,1)S(1)}, bf16[3,64,1024]{2,1,0:T(8,128)(2,1)S(1)}, u32[]{:S(2)}, u32[]{:S(2)}) collective-permute-start(bf16[3,64,1024]{2,1,0:T(8,128)(2,1)S(1)} %collective-permute-done.8.refs_1_), channel_id=1, source_target_pairs={{0,128},{4,132},{8,136},{12,140},{16,156},{20,144},{24,148},{28,15... | collective-permute-start | bytes 1179656 | tf_op jit(solution)/shard_map/ppermute | solution.py:28
  65.8 10.4 %collective-permute-start.14 = (bf16[128,1024]{1,0:T(8,128)(2,1)S(1)}, bf16[128,1024]{1,0:T(8,128)(2,1)S(1)}, u32[]{:S(2)}, u32[]{:S(2)}) collective-permute-start(bf16[128,1024]{1,0:T(8,128)(2,1)S(1)} %slice.11), channel_id=1, source_target_pairs={{0,32},{4,36},{8,40},{12,44},{16,48},{20,52},{24,56},{28,60},{32,6... | collective-permute-start | bytes 786440 | tf_op jit(solution)/shard_map/ppermute | solution.py:28
  66.1 10.2 %collective-permute-start.13 = (bf16[128,1024]{1,0:T(8,128)(2,1)S(1)}, bf16[128,1024]{1,0:T(8,128)(2,1)S(1)}, u32[]{:S(2)}, u32[]{:S(2)}) collective-permute-start(bf16[128,1024]{1,0:T(8,128)(2,1)S(1)} %slice.10), channel_id=1, source_target_pairs={{0,96},{4,100},{8,104},{12,108},{16,112},{20,116},{24,120},{28,124... | collective-permute-start | bytes 786440 | tf_op jit(solution)/shard_map/ppermute | solution.py:28
  68.6 7.7 %collective-permute-start.12 = (bf16[3,32,1024]{2,1,0:T(8,128)(2,1)S(1)}, bf16[3,32,1024]{2,1,0:T(8,128)(2,1)S(1)}, u32[]{:S(2)}, u32[]{:S(2)}) collective-permute-start(bf16[3,32,1024]{2,1,0:T(8,128)(2,1)S(1)} %slice.9), channel_id=1, source_target_pairs={{0,4},{4,8},{8,12},{12,0},{16,28},{20,16},{24,20},{28,24},{32,36},... | collective-permute-start | bytes 589832 | tf_op jit(solution)/shard_map/ppermute | solution.py:28
  76.3 2.1 %collective-permute-start.16 = (bf16[3,96,1024]{2,1,0:T(8,128)(2,1)S(1)}, bf16[3,96,1024]{2,1,0:T(8,128)(2,1)S(1)}, u32[]{:S(2)}, u32[]{:S(2)}) collective-permute-start(bf16[3,96,1024]{2,1,0:T(8,128)(2,1)S(1)} %join.3.refs_4_.refs_5_), channel_id=1, source_target_pairs={{0,16},{4,20},{8,24},{12,28},{16,0},{20,4},{24,8},{28,12},{32,48},... | collective-permute-start | bytes 1769480 | tf_op jit(solution)/shard_map/ppermute | solution.py:28
  79.5 14.7 %collective-permute-start.17 = (bf16[256,1024]{1,0:T(8,128)(2,1)S(1)}, bf16[256,1024]{1,0:T(8,128)(2,1)S(1)}, u32[]{:S(2)}, u32[]{:S(2)}) collective-permute-start(bf16[256,1024]{1,0:T(8,128)(2,1)S(1)} %render_rows.5), channel_id=1, source_target_pairs={{0,32},{4,36},{8,40},{12,44},{16,48},{20,52},{24,56},{28,60},{32,6... | collective-permute-start | bytes 1572872 | tf_op jit(solution)/shard_map/ppermute | solution.py:28
  80.8 13.5 %collective-permute-start.18 = (bf16[256,1024]{1,0:T(8,128)(2,1)S(1)}, bf16[256,1024]{1,0:T(8,128)(2,1)S(1)}, u32[]{:S(2)}, u32[]{:S(2)}) collective-permute-start(bf16[256,1024]{1,0:T(8,128)(2,1)S(1)} %render_rows.6), channel_id=1, source_target_pairs={{0,96},{4,100},{8,104},{12,108},{16,112},{20,116},{24,120},{28,124... | collective-permute-start | bytes 1572872 | tf_op jit(solution)/shard_map/ppermute | solution.py:28
  94.4 8.8 %collective-permute-start.19 = (bf16[128,1024]{1,0:T(8,128)(2,1)S(1)}, bf16[128,1024]{1,0:T(8,128)(2,1)S(1)}, u32[]{:S(2)}, u32[]{:S(2)}) collective-permute-start(bf16[128,1024]{1,0:T(8,128)(2,1)S(1)} %get-tuple-element.47), channel_id=1, source_target_pairs={{0,32},{4,36},{8,40},{12,44},{16,48},{20,52},{24,56},{28,60},{32,6... | collective-permute-start | bytes 786440 | tf_op jit(solution)/shard_map/ppermute | solution.py:28
  94.5 8.8 %collective-permute-start.20 = (bf16[128,1024]{1,0:T(8,128)(2,1)S(1)}, bf16[128,1024]{1,0:T(8,128)(2,1)S(1)}, u32[]{:S(2)}, u32[]{:S(2)}) collective-permute-start(bf16[128,1024]{1,0:T(8,128)(2,1)S(1)} %get-tuple-element.48), channel_id=1, source_target_pairs={{0,96},{4,100},{8,104},{12,108},{16,112},{20,116},{24,120},{28,124... | collective-permute-start | bytes 786440 | tf_op jit(solution)/shard_map/ppermute | solution.py:28

commit v4 on v3

v4 whole, which is shorter than its diff:
```python
import functools

import jax
import jax.numpy as jnp
from jax import lax
from jax.experimental import pallas as pl
from jax.experimental.pallas import tpu as pltpu
from jax.sharding import PartitionSpec as P

AXES = ("view", "render")
LZ, NX, NC, HZ = 2, 4, 2, 4
NZ = LZ * HZ
F32 = jnp.float32
BF16 = jnp.bfloat16
STEPS = (2, 1, 3, 0)
GROUPS = ((0, 1), (2, 3))
DELTA_US, SUM_US, OWN_US = 0.0, 10.0, 10.0


def move(array, target):
    pairs = []
    for zl in range(LZ):
        for x in range(NX):
            for core in range(NC):
                for zh in range(HZ):
                    tl, tx, tc, th = target(zl, x, core, zh)
                    pairs.append(
                        (((zl * NX + x) * NC + core) * HZ + zh, ((tl * NX + tx) * NC + tc) * HZ + th)
                    )
    return lax.ppermute(array, AXES, pairs)


def along_x(array, step):
    return move(array, lambda zl, x, c, zh: (zl, (x + step) % NX, c, zh))


def to_owner(array, step):
    return move(array, lambda zl, x, c, zh: (c, (x + step) % NX, zl, zh))


def along_z(array, step):
    def target(zl, x, c, zh):
        z = (zh * LZ + zl + (1 - 2 * c) * step) % NZ
        return z % LZ, x, c, z // LZ

    return move(array, target)


def swap_core(array):
    return move(array, lambda zl, x, c, zh: (zl, x, 1 - c, zh))


def contract(left, right, left_dim, right_dim):
    return lax.dot_general(
        left, right, (((left_dim,), (right_dim,)), ((), ())), preferred_element_type=F32
    )


def cost(us):
    return pl.CostEstimate(flops=1 + int(us * 1.15e9), bytes_accessed=1, transcendentals=0)


def params(mib=32):
    return pltpu.CompilerParams(vmem_limit_bytes=mib * 1024 * 1024)


def delta_kernel(group, place, rates, keys, values, gate, up, down, *refs):
    mine, others, old = refs[: len(GROUPS)], refs[len(GROUPS) : 2 * len(GROUPS)], refs[2 * len(GROUPS)]
    old_turned, k_ref, v_ref, columns, turned, sems = refs[-6:]
    x, zl, core = place[0], place[1], place[2]
    units = gate.shape[2] // NX
    half = units // NC
    n = units * group

    def fetch(m, weight, i):
        start = pl.multiple_of((x + STEPS[i]) % NX * units, units)
        return pltpu.make_async_copy(
            weight.at[0, :, pl.ds(start, units)],
            columns.at[m, :, i * units : (i + 1) * units],
            sems.at[2 + m * NX + i],
        )

    early = keys.shape[0] // 2
    key_copies = [
        pltpu.make_async_copy(keys.at[lo : lo + early], k_ref.at[lo : lo + early], sems.at[3 * NX + 3 + i])
        for i, lo in enumerate((0, early))
    ]
    value_copy = pltpu.make_async_copy(values, v_ref, sems.at[1])
    copies = [[fetch(m, w, i) for i in range(NX)] for m, w in enumerate((gate, up, down))]
    key_copies[0].start()
    for i in range(group):
        copies[0][i].start()
        copies[1][i].start()
    key_copies[1].start()
    value_copy.start()
    for i in range(group):
        copies[2][i].start()
    for i in range(group, NX):
        for m in range(3):
            copies[m][i].start()

    key_copies[0].wait()
    for first in range(0, NX, group):
        blocks = range(first, first + group)
        cut = slice(first * units, first * units + n)
        for i in blocks:
            copies[0][i].wait()
            copies[1][i].wait()
        early_in = [contract(columns[m, :, cut], k_ref[:early], 0, 1) for m in range(2)]
        if not first:
            key_copies[1].wait()
        late_in = [contract(columns[m, :, cut], k_ref[early:], 0, 1) for m in range(2)]
        gate_in, up_in = (jnp.concatenate(pair, 1) for pair in zip(early_in, late_in))
        k = k_ref[...]
        if not first:
            value_copy.wait()
        for i in blocks:
            copies[2][i].wait()
        v, r = v_ref[...], rates[...]
        back = contract(columns[2, :, cut], v, 0, 1)
        s = jax.nn.sigmoid(gate_in)
        act = gate_in * s
        rated = r * back
        turned[0, cut] = (rated * up_in * s * (1.0 + gate_in * (1.0 - s))).astype(BF16)
        turned[1, cut] = (rated * act).astype(BF16)
        turned[2, cut] = (r * (act * up_in)).astype(BF16)
        parts = [(c, i) for c in (1 - core, core) for i in blocks]
        rows = [pl.ds(pl.multiple_of(i * units + c * half, half), half) for c, i in parts]
        pres = jnp.concatenate([turned[m, part] for part in rows for m in (0, 1)], 0)
        key_sums = contract(pres, k, 1, 0).astype(BF16)
        hidden = jnp.concatenate([turned[2, part] for part in rows], 0)
        value_sums = contract(hidden, v, 1, 0).astype(BF16)
        for at, (_, i) in enumerate(parts):
            g = next(g for g in reversed(range(len(GROUPS))) if GROUPS[g][0] <= i)
            out = (mine if at >= group else others)[g].at[i - GROUPS[g][0]]
            out[0] = key_sums[2 * at * half : (2 * at + 1) * half]
            out[1] = key_sums[(2 * at + 1) * half : (2 * at + 2) * half]
            out[2] = value_sums[at * half : (at + 1) * half]
    own = pl.ds(pl.multiple_of(zl * half, half), half)
    for m in range(3):
        old_turned[...] = columns[m, :, (NX - 1) * units :].astype(F32).T
        old[m] = old_turned[own, :].astype(BF16)


def deltas(place, rates, arrays, group=4):
    count, width = arrays[0].shape
    n = arrays[2].shape[2]
    units = n // NX
    half = units // NC
    vmem = pl.BlockSpec(memory_space=pltpu.VMEM)
    out_shape = [jax.ShapeDtypeStruct((len(g), 3, half, width), BF16) for g in GROUPS * 2]
    out_shape.append(jax.ShapeDtypeStruct((3, half, width), BF16))
    return pl.pallas_call(
        functools.partial(delta_kernel, group),
        name="deltas",
        in_specs=[pl.BlockSpec(memory_space=pltpu.SMEM), vmem]
        + [pl.BlockSpec(memory_space=pl.ANY)] * len(arrays),
        out_specs=[vmem] * len(out_shape),
        out_shape=out_shape,
        scratch_shapes=[
            pltpu.VMEM((units, width), F32),
            pltpu.VMEM((count, width), BF16),
            pltpu.VMEM((count, width), BF16),
            pltpu.VMEM((3, width, n), BF16),
            pltpu.VMEM((3, n, count), BF16),
            pltpu.SemaphoreType.DMA((3 * NX + 5,)),
        ],
        compiler_params=params(50),
        cost_estimate=cost(DELTA_US),
    )(place, rates, *arrays)


def call(kernel, name, out_shape, *operands, us=0.0):
    vmem = pl.BlockSpec(memory_space=pltpu.VMEM)
    return pl.pallas_call(
        kernel,
        name=name,
        in_specs=[pl.BlockSpec(memory_space=pltpu.SMEM) if o.ndim == 1 else vmem for o in operands],
        out_specs=jax.tree.map(lambda _: vmem, out_shape),
        out_shape=out_shape,
        compiler_params=params(),
        cost_estimate=cost(us),
    )(*operands)


def add_kernel(mine, other, *outs):
    for i, out in enumerate(outs):
        out[...] = (mine[i].astype(F32) + other[i].astype(F32)).astype(out.dtype)


def add_cores(mine, other):
    block = jax.ShapeDtypeStruct(mine.shape[1:], BF16)
    return call(add_kernel, "add_cores", [block] * mine.shape[0], mine, other)


def sum_kernel(*refs):
    sums = refs[0][...].astype(F32)
    for ref in refs[1:-1]:
        sums = sums + ref[...].astype(F32)
    refs[-1][...] = sums.astype(refs[-1].dtype)


def add_up(name, parts, us):
    return call(sum_kernel, name, jax.ShapeDtypeStruct(parts[0].shape, BF16), *parts, us=us)


def renorm_kernel(place, old, mine, other, *outs):
    n = outs[0].shape[1]
    for m in range(3):
        halves = []
        for i in range(2):
            part = slice(i * n, (i + 1) * n)
            was = old[m, part, :].astype(F32)
            summed = was + (mine[m, part, :].astype(F32) + other[m, part, :].astype(F32))
            factor = jnp.sqrt(jnp.sum(was * was, axis=-1, keepdims=True)) / jnp.sqrt(
                jnp.sum(summed * summed, axis=-1, keepdims=True) + 1e-06
            )
            halves.append((summed * factor).astype(BF16))
        for i, out in enumerate(outs):
            out[m] = jnp.where(place[2] == i, halves[0], halves[1])


def join_kernel(*refs):
    out = refs[-1]
    at = 0
    for ref in refs[:-1]:
        n = ref.shape[1]
        out[:, at : at + n, :] = ref[...]
        at += n


def join(pieces):
    units = sum(p.shape[1] for p in pieces)
    out = jax.ShapeDtypeStruct((3, units, pieces[0].shape[2]), BF16)
    return call(join_kernel, "join", out, *pieces)


def render_kernel(cuts, count, *refs):
    rows, pieces, outs = refs[: len(cuts)], refs[len(cuts) : -count], refs[-count:]
    gate, up, down = (jnp.concatenate([p[m] for p in pieces], 0) for m in range(3))
    q = jnp.concatenate([ref[lo:hi, :] for ref, (lo, hi) in zip(rows, cuts)], 0)
    gate_q = contract(q, gate, 1, 1)
    up_q = contract(q, up, 1, 1)
    hidden_q = (gate_q * jax.nn.sigmoid(gate_q) * up_q).astype(BF16)
    partial = contract(hidden_q, down, 1, 0)
    n = outs[0].shape[0]
    for i, out in enumerate(outs):
        out[...] = partial[i * n : (i + 1) * n].astype(out.dtype)


def render(rows, pieces, outs):
    kernel = functools.partial(render_kernel, tuple((lo, hi) for _, lo, hi in rows), len(outs))
    return call(kernel, "render_rows", outs, *[r[0] for r in rows], *pieces)


def merge_kernel(mid, relay_left, relay_right, to_right, to_left):
    half = to_right.shape[0]
    to_right[...] = (mid[:half] + relay_left[...].astype(F32)).astype(BF16)
    to_left[...] = (mid[half:] + relay_right[...].astype(F32)).astype(BF16)


def own_kernel(own, from_left, from_right, out):
    half = from_left.shape[0]
    out[:half] = own[:half] + from_right[...].astype(F32)
    out[half:] = own[half:] + from_left[...].astype(F32)


def total_kernel(own, last_left, last_right, out):
    half = last_left.shape[0]
    out[:half] = (own[:half] + last_left[...].astype(F32)).astype(BF16)
    out[half:] = (own[half:] + last_right[...].astype(F32)).astype(BF16)


def local(input_keys, input_values, token_rates, gate_weight, up_weight, down_weight, queries):
    view = lax.axis_index("view")
    zl, x, core = view // (NX * NC), (view // NC) % NX, view % NC
    place = jnp.stack([x, zl, core]).astype(jnp.int32)

    arrays = (input_keys, input_values, gate_weight, up_weight, down_weight)
    *parts, old = deltas(place, token_rates, arrays)
    chips = []
    for mine, other in zip(parts, parts[len(GROUPS) :]):
        chips += add_cores(mine, swap_core(other))
    got = [to_owner(chip, step) for chip, step in zip(chips, STEPS)]

    queries, *got[:2] = lax.optimization_barrier((queries, *got[:2]))
    half = queries.shape[0] // 2
    from_right, from_left = along_x(queries, -1), along_x(queries, 1)
    sums = add_up("sum_chips", got, SUM_US)
    out = jax.ShapeDtypeStruct((3, sums.shape[1] // 2, sums.shape[2]), BF16)
    news = call(renorm_kernel, "renorm", [out] * 2, place, old, sums, swap_core(sums))
    first = [along_z(new, 1) for new in news]
    second = [along_z(piece, 1) for piece in first]
    third = [along_z(piece, 1) for piece in second]
    far_top, far_low = along_x(from_right[:half], -1), along_x(from_left[half:], 1)
    third[1], far_top, far_low = lax.optimization_barrier((third[1], far_top, far_low))
    fourth = along_z(third[0], 1)
    near, last = join(first + second), join(third + [fourth])
    pieces = list(news) + [near, swap_core(near), last, swap_core(last)]

    both = 2 * half
    part = jax.ShapeDtypeStruct((half, queries.shape[1]), BF16)
    to_right, to_left = render([(far_top, 0, half), (far_low, 0, half)], pieces, [part] * 2)
    relay_left, relay_right = along_x(to_right, 1), along_x(to_left, -1)
    to_right, to_left = render([(from_right, half, both), (from_left, 0, half)], pieces, [part] * 2)
    from_left_x, from_right_x = along_x(to_right, 1), along_x(to_left, -1)
    wide = jax.ShapeDtypeStruct((both, queries.shape[1]), F32)
    (mid,) = render([(from_right, 0, half), (from_left, half, both)], pieces, [wide])
    (own,) = render([(queries, 0, both)], pieces, [wide])
    to_right, to_left = call(merge_kernel, "merge", [part] * 2, mid, relay_left, relay_right)
    last_left, last_right = along_x(to_right, 1), along_x(to_left, -1)
    own = call(own_kernel, "own", wide, own, from_left_x, from_right_x, us=OWN_US)
    out = jax.ShapeDtypeStruct(own.shape, BF16)
    return call(total_kernel, "total", out, own, last_left, last_right)


def solution(mesh):
    return jax.shard_map(
        local,
        mesh=mesh,
        in_specs=(
            P("view", "head"),
            P("view", "head"),
            P("head", "view"),
            P("head", None, "render"),
            P("head", None, "render"),
            P("head", None, "render"),
            P(("view", "render"), "head"),
        ),
        out_specs=P(("view", "render"), "head"),
        check_vma=False,
    )
```

time: 106 us -> 96.6 us (0.911); the launches traced: 104 us -> 96.4 us
  waiting for transfers between devices: 46.8 us -> 29.3 us
  starting transfers between devices: 35.5 us -> 48.6 us
  Pallas kernels: 20.9 us -> 17.5 us
    ppermute x21 -> x26, waiting for transfers between devices: 46.8 us -> 29.3 us  [move(): return lax.ppermute(array, AXES, pairs)]
    ppermute x21 -> x26, starting transfers between devices: 35.5 us -> 48.6 us  [move(): return lax.ppermute(array, AXES, pairs)]
    pallas_call x2 -> x1, Pallas kernels: 14 us -> 10.6 us  [deltas(): pl.pallas_call(functools.partial(delta_kernel, group), name='deltas', in_...]
    pallas_call x12 -> x13, Pallas kernels: 6.89 us -> 6.96 us  [call(): pl.pallas_call(kernel, name=name, in_specs=[pl.BlockSpec(memory_space=plt...]
  transfers between devices with their start and end apart: 21 -> 26, of which waited for: 12 -> 12; matrix products, arithmetic and copies ran while one was open for 0% -> 0% of each run, Pallas kernels for 11% -> 5%
where the time goes in v4:
time: 96.6 us; the launch traced here: 96.4 us
  starting transfers between devices  48.6 us (50%)
  waiting for transfers between devices  29.3 us (30%)
  Pallas kernels  17.5 us (18%)
    ppermute x26, starting transfers between devices, move(): return lax.ppermute(array, AXES, pairs)  48.6 us
    ppermute x26, waiting for transfers between devices, move(): return lax.ppermute(array, AXES, pairs)  29.3 us
    pallas_call x1, Pallas kernels, deltas(): pl.pallas_call(functools.partial(delta_kernel, group), name='deltas', in_...  10.6 us
    pallas_call x13, Pallas kernels, call(): pl.pallas_call(kernel, name=name, in_specs=[pl.BlockSpec(memory_space=plt...  6.96 us
  transfers between devices with their start and end apart: 26, of which 12 were waited for; matrix products, arithmetic and copies ran while one was open for 0% of the time, Pallas kernels for 5%

profile of v4, /device:TPU:1, one launch (start us, length us, event | category | flops | bytes accessed | tf_op | source)
XLA Modules:
  0.0 96.4 jit_solution(16077559747911662222)
XLA Ops:
  0.0 0.1 pad_add_fusion.place
  0.1 0.7 copy-done.1
  0.8 10.6 %deltas.1 = (bf16[2,3,64,1024]{3,2,1,0:T(8,128)(2,1)S(1)}, bf16[2,3,64,1024]{3,2,1,0:T(8,128)(2,1)S(1)}, bf16[2,3,64,1024]{3,2,1,0:T(8,128)(2,1)S(1)}, bf16[2,3,...) custom-call(s32[3]{0:T(128)S(1)} %pad_add_fusion.place, f32[1,1024]{1,0:T(1,128)S(1)} %copy-done.1, ...), custom_call_target="tpu_custom_call" | custom-call | flops 1 | bytes 1 | tf_op jit(solution)/shard_map/deltas/pallas_call | solution.py:153
  11.3 3.3 %collective-permute-start = (bf16[2,3,64,1024]{3,2,1,0:T(8,128)(2,1)S(1)}, bf16[2,3,64,1024]{3,2,1,0:T(8,128)(2,1)S(1)}, u32[]{:S(2)}, u32[]{:S(2)}) collective-permute-start(bf16[2,3,64,1024]{3,2,1,0:T(8,128)(2,1)S(1)} %get-tuple-element.29), channel_id=1, source_target_pairs={{0,16},{4,20},{8,24},{12,28},{16,0},{20,4},{24,8},{28,12},{32,48},... | collective-permute-start | bytes 2359304 | tf_op jit(solution)/shard_map/ppermute | solution.py:30
  14.7 0.1 collective-permute-start.3
  14.8 1.8 %collective-permute-done.other = bf16[2,3,64,1024]{3,2,1,0:T(8,128)(2,1)S(1)} collective-permute-done((bf16[2,3,64,1024]{3,2,1,0:T(8,128)(2,1)S(1)}, bf16[2,3,64,1024]{3,2,1,0:T(8,128)(2,1)S(1)}, u32[]{:S(2)}, u32[]{:S(2)}) %collective-permute-start) | collective-permute-done | bytes 786464 | tf_op jit(solution)/shard_map/ppermute | solution.py:30
  16.6 0.2 add_cores.2
  16.8 2.7 %collective-permute-start.1 = (bf16[3,64,1024]{2,1,0:T(8,128)(2,1)S(1)}, bf16[3,64,1024]{2,1,0:T(8,128)(2,1)S(1)}, u32[]{:S(2)}, u32[]{:S(2)}) collective-permute-start(bf16[3,64,1024]{2,1,0:T(8,128)(2,1)S(1)} %get-tuple-element.30), channel_id=1, source_target_pairs={{0,64},{4,68},{8,72},{12,76},{16,192},{20,196},{24,200},{28,204},{... | collective-permute-start | bytes 1179656 | tf_op jit(solution)/shard_map/ppermute | solution.py:30
  19.5 0.0 collective-permute-start.2
  19.5 0.0 collective-permute-done.3.other
  19.5 0.2 add_cores.3
  19.7 3.9 %collective-permute-start.4 = (bf16[3,64,1024]{2,1,0:T(8,128)(2,1)S(1)}, bf16[3,64,1024]{2,1,0:T(8,128)(2,1)S(1)}, u32[]{:S(2)}, u32[]{:S(2)}) collective-permute-start(bf16[3,64,1024]{2,1,0:T(8,128)(2,1)S(1)} %get-tuple-element.38), channel_id=1, source_target_pairs={{0,96},{4,100},{8,104},{12,108},{16,224},{20,228},{24,232},{28,236... | collective-permute-start | bytes 1179656 | tf_op jit(solution)/shard_map/ppermute | solution.py:30
  23.6 2.0 %collective-permute-start.5 = (bf16[3,64,1024]{2,1,0:T(8,128)(2,1)S(1)}, bf16[3,64,1024]{2,1,0:T(8,128)(2,1)S(1)}, u32[]{:S(2)}, u32[]{:S(2)}) collective-permute-start(bf16[3,64,1024]{2,1,0:T(8,128)(2,1)S(1)} %get-tuple-element.39), channel_id=1, source_target_pairs={{0,0},{4,4},{8,8},{12,12},{16,128},{20,132},{24,136},{28,140},{32,... | collective-permute-start | bytes 1179656 | tf_op jit(solution)/shard_map/ppermute | solution.py:30
  25.6 2.1 %collective-permute-done.1.refs_0_ = bf16[3,64,1024]{2,1,0:T(8,128)(2,1)S(1)} collective-permute-done((bf16[3,64,1024]{2,1,0:T(8,128)(2,1)S(1)}, bf16[3,64,1024]{2,1,0:T(8,128)(2,1)S(1)}, u32[]{:S(2)}, u32[]{:S(2)}) %collective-permute-start.1) | collective-permute-done | bytes 393248 | tf_op jit(solution)/shard_map/ppermute | solution.py:30
  27.7 3.4 %collective-permute-done.2.refs_1_ = bf16[3,64,1024]{2,1,0:T(8,128)(2,1)S(1)} collective-permute-done((bf16[3,64,1024]{2,1,0:T(8,128)(2,1)S(1)}, bf16[3,64,1024]{2,1,0:T(8,128)(2,1)S(1)}, u32[]{:S(2)}, u32[]{:S(2)}) %collective-permute-start.2) | collective-permute-done | bytes 393248 | tf_op jit(solution)/shard_map/ppermute | solution.py:30
  31.1 3.5 %collective-permute-done.4.refs_2_ = bf16[3,64,1024]{2,1,0:T(8,128)(2,1)S(1)} collective-permute-done((bf16[3,64,1024]{2,1,0:T(8,128)(2,1)S(1)}, bf16[3,64,1024]{2,1,0:T(8,128)(2,1)S(1)}, u32[]{:S(2)}, u32[]{:S(2)}) %collective-permute-start.4) | collective-permute-done | bytes 393248 | tf_op jit(solution)/shard_map/ppermute | solution.py:30
  34.6 3.2 %collective-permute-done.5.refs_3_ = bf16[3,64,1024]{2,1,0:T(8,128)(2,1)S(1)} collective-permute-done((bf16[3,64,1024]{2,1,0:T(8,128)(2,1)S(1)}, bf16[3,64,1024]{2,1,0:T(8,128)(2,1)S(1)}, u32[]{:S(2)}, u32[]{:S(2)}) %collective-permute-start.5) | collective-permute-done | bytes 393248 | tf_op jit(solution)/shard_map/ppermute | solution.py:30
  37.8 0.2 sum_chips.1.mine
  38.0 1.4 %collective-permute-start.6 = (bf16[3,64,1024]{2,1,0:T(8,128)(2,1)S(1)}, bf16[3,64,1024]{2,1,0:T(8,128)(2,1)S(1)}, u32[]{:S(2)}, u32[]{:S(2)}) collective-permute-start(bf16[3,64,1024]{2,1,0:T(8,128)(2,1)S(1)} %sum_chips.1.mine), channel_id=1, source_target_pairs={{0,16},{4,20},{8,24},{12,28},{16,0},{20,4},{24,8},{28,12},{32,48},... | collective-permute-start | bytes 1179656 | tf_op jit(solution)/shard_map/ppermute | solution.py:30
  39.4 0.0 collective-permute-start.16
  39.4 2.7 %collective-permute-start.14 = (bf16[256,1024]{1,0:T(8,128)(2,1)S(1)}, bf16[256,1024]{1,0:T(8,128)(2,1)S(1)}, u32[]{:S(2)}, u32[]{:S(2)}) collective-permute-start(bf16[256,1024]{1,0:T(8,128)(2,1)S(1)} %copy-done), channel_id=1, source_target_pairs={{0,96},{4,100},{8,104},{12,108},{16,112},{20,116},{24,120},{28,124... | collective-permute-start | bytes 1572872 | tf_op jit(solution)/shard_map/ppermute | solution.py:30
  42.1 0.0 collective-permute-done.6.other
  42.1 0.9 renorm.1
  43.0 4.4 %collective-permute-start.7 = (bf16[3,32,1024]{2,1,0:T(8,128)(2,1)S(1)}, bf16[3,32,1024]{2,1,0:T(8,128)(2,1)S(1)}, u32[]{:S(2)}, u32[]{:S(2)}) collective-permute-start(bf16[3,32,1024]{2,1,0:T(8,128)(2,1)S(1)} %get-tuple-element.40.refs_1_.refs_2_), channel_id=1, source_target_pairs={{0,128},{4,132},{8,136},{12,140},{16,156},{20,144},{24,148},{28,15... | collective-permute-start | bytes 589832 | tf_op jit(solution)/shard_map/ppermute | solution.py:30
  47.4 0.4 collective-permute-start.8
  47.9 2.2 %collective-permute-done.7.refs_0_ = bf16[3,32,1024]{2,1,0:T(8,128)(2,1)S(1)} collective-permute-done((bf16[3,32,1024]{2,1,0:T(8,128)(2,1)S(1)}, bf16[3,32,1024]{2,1,0:T(8,128)(2,1)S(1)}, u32[]{:S(2)}, u32[]{:S(2)}) %collective-permute-start.7) | collective-permute-done | bytes 196640 | tf_op jit(solution)/shard_map/ppermute | solution.py:30
  50.0 3.4 %collective-permute-start.9 = (bf16[3,32,1024]{2,1,0:T(8,128)(2,1)S(1)}, bf16[3,32,1024]{2,1,0:T(8,128)(2,1)S(1)}, u32[]{:S(2)}, u32[]{:S(2)}) collective-permute-start(bf16[3,32,1024]{2,1,0:T(8,128)(2,1)S(1)} %collective-permute-done.7.refs_0_), channel_id=1, source_target_pairs={{0,128},{4,132},{8,136},{12,140},{16,156},{20,144},{24,148},{28,15... | collective-permute-start | bytes 589832 | tf_op jit(solution)/shard_map/ppermute | solution.py:30
  53.5 2.1 %collective-permute-start.10 = (bf16[3,32,1024]{2,1,0:T(8,128)(2,1)S(1)}, bf16[3,32,1024]{2,1,0:T(8,128)(2,1)S(1)}, u32[]{:S(2)}, u32[]{:S(2)}) collective-permute-start(bf16[3,32,1024]{2,1,0:T(8,128)(2,1)S(1)} %collective-permute-done.8.refs_1_), channel_id=1, source_target_pairs={{0,128},{4,132},{8,136},{12,140},{16,156},{20,144},{24,148},{28,15... | collective-permute-start | bytes 589832 | tf_op jit(solution)/shard_map/ppermute | solution.py:30
  55.6 0.5 collective-permute-done.9.refs_2_
  56.1 3.1 %collective-permute-start.12 = (bf16[3,32,1024]{2,1,0:T(8,128)(2,1)S(1)}, bf16[3,32,1024]{2,1,0:T(8,128)(2,1)S(1)}, u32[]{:S(2)}, u32[]{:S(2)}) collective-permute-start(bf16[3,32,1024]{2,1,0:T(8,128)(2,1)S(1)} %collective-permute-done.9.refs_2_), channel_id=1, source_target_pairs={{0,128},{4,132},{8,136},{12,140},{16,156},{20,144},{24,148},{28,15... | collective-permute-start | bytes 589832 | tf_op jit(solution)/shard_map/ppermute | solution.py:30
  59.2 0.1 collective-permute-start.17
  59.3 0.0 collective-permute-done.14.refs_0_
  59.3 2.7 %collective-permute-start.15 = (bf16[128,1024]{1,0:T(8,128)(2,1)S(1)}, bf16[128,1024]{1,0:T(8,128)(2,1)S(1)}, u32[]{:S(2)}, u32[]{:S(2)}) collective-permute-start(bf16[128,1024]{1,0:T(8,128)(2,1)S(1)} %slice.8), channel_id=1, source_target_pairs={{0,96},{4,100},{8,104},{12,108},{16,112},{20,116},{24,120},{28,124... | collective-permute-start | bytes 786440 | tf_op jit(solution)/shard_map/ppermute | solution.py:30
  62.1 0.0 collective-permute-done.10.refs_3_
  62.1 0.0 collective-permute-start.13
  62.1 0.0 collective-permute-done.12.refs_0_
  62.1 2.8 %collective-permute-start.18 = (bf16[3,32,1024]{2,1,0:T(8,128)(2,1)S(1)}, bf16[3,32,1024]{2,1,0:T(8,128)(2,1)S(1)}, u32[]{:S(2)}, u32[]{:S(2)}) collective-permute-start(bf16[3,32,1024]{2,1,0:T(8,128)(2,1)S(1)} %collective-permute-done.12.refs_0_), channel_id=1, source_target_pairs={{0,128},{4,132},{8,136},{12,140},{16,156},{20,144},{24,148},{28,15... | collective-permute-start | bytes 589832 | tf_op jit(solution)/shard_map/ppermute | solution.py:30
  64.9 0.1 join.2.refs_3_.refs_4_
  65.0 0.9 collective-permute-start.11
  65.9 2.8 %collective-permute-done.17.refs_1_ = bf16[128,1024]{1,0:T(8,128)(2,1)S(1)} collective-permute-done((bf16[128,1024]{1,0:T(8,128)(2,1)S(1)}, bf16[128,1024]{1,0:T(8,128)(2,1)S(1)}, u32[]{:S(2)}, u32[]{:S(2)}) %collective-permute-start.17) | collective-permute-done | bytes 262176 | tf_op jit(solution)/shard_map/ppermute | solution.py:30
  68.7 0.0 collective-permute-done.15.refs_0_
  68.7 0.0 collective-permute-done.13.refs_1_
  68.7 0.2 collective-permute-done.18.refs_2_
  68.9 3.9 %collective-permute-start.19 = (bf16[3,96,1024]{2,1,0:T(8,128)(2,1)S(1)}, bf16[3,96,1024]{2,1,0:T(8,128)(2,1)S(1)}, u32[]{:S(2)}, u32[]{:S(2)}) collective-permute-start(bf16[3,96,1024]{2,1,0:T(8,128)(2,1)S(1)} %join.3.refs_5_.refs_6_), channel_id=1, source_target_pairs={{0,16},{4,20},{8,24},{12,28},{16,0},{20,4},{24,8},{28,12},{32,48},... | collective-permute-start | bytes 1769480 | tf_op jit(solution)/shard_map/ppermute | solution.py:30
  72.8 0.0 collective-permute-done.11.refs_4_.refs_5_
  72.8 1.6 %collective-permute-done.19.refs_6_.refs_7_ = bf16[3,96,1024]{2,1,0:T(8,128)(2,1)S(1)} collective-permute-done((bf16[3,96,1024]{2,1,0:T(8,128)(2,1)S(1)}, bf16[3,96,1024]{2,1,0:T(8,128)(2,1)S(1)}, u32[]{:S(2)}, u32[]{:S(2)}) %collective-permute-start.19) | collective-permute-done | bytes 589856 | tf_op jit(solution)/shard_map/ppermute | solution.py:30
  74.4 1.1 %render_rows.7 = (bf16[128,1024]{1,0:T(8,128)(2,1)S(1)}, bf16[128,1024]{1,0:T(8,128)(2,1)S(1)}) custom-call(bf16[128,1024]{1,0:T(8,128)(2,1)S(1)} %collective-permute-done.15.refs_0_, bf16[128,1024]{1,0:T(8,128)(2,1)S(1)} %collective-permute-done.17.refs_1_, bf16[3,32,1024]{2,1,0:T(8,128)(2,1)S(1)} %get-tuple-element.40.refs_1_.refs_2_, ...), custom_call_target="tpu_custom_call" | custom-call | flops 1 | bytes 1 | tf_op jit(solution)/shard_map/render_rows/pallas_call | solution.py:175
  75.5 0.1 collective-permute-start.22
  75.6 2.6 %collective-permute-start.23 = (bf16[128,1024]{1,0:T(8,128)(2,1)S(1)}, bf16[128,1024]{1,0:T(8,128)(2,1)S(1)}, u32[]{:S(2)}, u32[]{:S(2)}) collective-permute-start(bf16[128,1024]{1,0:T(8,128)(2,1)S(1)} %get-tuple-element.48), channel_id=1, source_target_pairs={{0,96},{4,100},{8,104},{12,108},{16,112},{20,116},{24,120},{28,124... | collective-permute-start | bytes 786440 | tf_op jit(solution)/shard_map/ppermute | solution.py:30
  78.3 1.1 %render_rows.5 = (bf16[128,1024]{1,0:T(8,128)(2,1)S(1)}, bf16[128,1024]{1,0:T(8,128)(2,1)S(1)}) custom-call(bf16[256,1024]{1,0:T(8,128)(2,1)S(1)} %collective-permute-done.14.refs_0_, bf16[256,1024]{1,0:T(8,128)(2,1)S(1)} %collective-permute-done.16.refs_1_, bf16[3,32,1024]{2,1,0:T(8,128)(2,1)S(1)} %get-tuple-element.40.refs_1_.refs_2_, ...), custom_call_target="tpu_custom_call" | custom-call | flops 1 | bytes 1 | tf_op jit(solution)/shard_map/render_rows/pallas_call | solution.py:175
  79.3 0.3 collective-permute-start.20
  79.7 2.7 %collective-permute-start.21 = (bf16[128,1024]{1,0:T(8,128)(2,1)S(1)}, bf16[128,1024]{1,0:T(8,128)(2,1)S(1)}, u32[]{:S(2)}, u32[]{:S(2)}) collective-permute-start(bf16[128,1024]{1,0:T(8,128)(2,1)S(1)} %get-tuple-element.44), channel_id=1, source_target_pairs={{0,96},{4,100},{8,104},{12,108},{16,112},{20,116},{24,120},{28,124... | collective-permute-start | bytes 786440 | tf_op jit(solution)/shard_map/ppermute | solution.py:30
  82.3 1.1 %render_rows.6.mid = f32[256,1024]{1,0:T(8,128)S(1)} custom-call(bf16[256,1024]{1,0:T(8,128)(2,1)S(1)} %collective-permute-done.14.refs_0_, bf16[256,1024]{1,0:T(8,128)(2,1)S(1)} %collective-permute-done.16.refs_1_, bf16[3,32,1024]{2,1,0:T(8,128)(2,1)S(1)} %get-tuple-element.40.refs_1_.refs_2_, bf16[3,32,1024]{2,1,0:T(8,128)(2,1)S(1)} %get-tuple-element.41.refs_2_.refs_3_, ...), custom_call_target="tpu_custom_call" | custom-call | flops 1 | bytes 1 | tf_op jit(solution)/shard_map/render_rows/pallas_call | solution.py:175
  83.4 1.1 %render_rows.4.own = f32[256,1024]{1,0:T(8,128)S(1)} custom-call(bf16[256,1024]{1,0:T(8,128)(2,1)S(1)} %copy-done, bf16[3,32,1024]{2,1,0:T(8,128)(2,1)S(1)} %get-tuple-element.40.refs_1_.refs_2_, bf16[3,32,1024]{2,1,0:T(8,128)(2,1)S(1)} %get-tuple-element.41.refs_2_.refs_3_, bf16[3,128,1024]{2,1,0:T(8,128)(2,1)S(1)} %join.2.refs_3_.refs_4_, ...), custom_call_target="tpu_custom_call" | custom-call | flops 1 | bytes 1 | tf_op jit(solution)/shard_map/render_rows/pallas_call | solution.py:175
  84.5 0.0 collective-permute-done.23.relay_right
  84.5 0.1 merge.1
  84.6 0.1 collective-permute-start.24
  84.7 2.7 %collective-permute-start.25 = (bf16[128,1024]{1,0:T(8,128)(2,1)S(1)}, bf16[128,1024]{1,0:T(8,128)(2,1)S(1)}, u32[]{:S(2)}, u32[]{:S(2)}) collective-permute-start(bf16[128,1024]{1,0:T(8,128)(2,1)S(1)} %get-tuple-element.50), channel_id=1, source_target_pairs={{0,96},{4,100},{8,104},{12,108},{16,112},{20,116},{24,120},{28,124... | collective-permute-start | bytes 786440 | tf_op jit(solution)/shard_map/ppermute | solution.py:30
  87.4 2.5 %collective-permute-done.20.from_left = bf16[128,1024]{1,0:T(8,128)(2,1)S(1)} collective-permute-done((bf16[128,1024]{1,0:T(8,128)(2,1)S(1)}, bf16[128,1024]{1,0:T(8,128)(2,1)S(1)}, u32[]{:S(2)}, u32[]{:S(2)}) %collective-permute-start.20) | collective-permute-done | bytes 262176 | tf_op jit(solution)/shard_map/ppermute | solution.py:30
  89.9 0.0 collective-permute-done.21.from_right
  89.9 0.1 own.1
  90.0 5.5 %collective-permute-done.24.last_left = bf16[128,1024]{1,0:T(8,128)(2,1)S(1)} collective-permute-done((bf16[128,1024]{1,0:T(8,128)(2,1)S(1)}, bf16[128,1024]{1,0:T(8,128)(2,1)S(1)}, u32[]{:S(2)}, u32[]{:S(2)}) %collective-permute-start.24) | collective-permute-done | bytes 262176 | tf_op jit(solution)/shard_map/ppermute | solution.py:30
  95.5 0.0 collective-permute-done.25.last_right
  95.5 0.9 total.1
  (9 shorter events, 0.1 us)
Async XLA Ops:
  0.1 0.7 copy-start.1
  11.3 5.2 %collective-permute-start = (bf16[2,3,64,1024]{3,2,1,0:T(8,128)(2,1)S(1)}, bf16[2,3,64,1024]{3,2,1,0:T(8,128)(2,1)S(1)}, u32[]{:S(2)}, u32[]{:S(2)}) collective-permute-start(bf16[2,3,64,1024]{3,2,1,0:T(8,128)(2,1)S(1)} %get-tuple-element.29), channel_id=1, source_target_pairs={{0,16},{4,20},{8,24},{12,28},{16,0},{20,4},{24,8},{28,12},{32,48},... | collective-permute-start | bytes 2359304 | tf_op jit(solution)/shard_map/ppermute | solution.py:30
  14.7 4.8 %collective-permute-start.3 = (bf16[2,3,64,1024]{3,2,1,0:T(8,128)(2,1)S(1)}, bf16[2,3,64,1024]{3,2,1,0:T(8,128)(2,1)S(1)}, u32[]{:S(2)}, u32[]{:S(2)}) collective-permute-start(bf16[2,3,64,1024]{3,2,1,0:T(8,128)(2,1)S(1)} %get-tuple-element.37), channel_id=1, source_target_pairs={{0,16},{4,20},{8,24},{12,28},{16,0},{20,4},{24,8},{28,12},{32,48},... | collective-permute-start | bytes 2359304 | tf_op jit(solution)/shard_map/ppermute | solution.py:30
  16.8 11.0 %collective-permute-start.1 = (bf16[3,64,1024]{2,1,0:T(8,128)(2,1)S(1)}, bf16[3,64,1024]{2,1,0:T(8,128)(2,1)S(1)}, u32[]{:S(2)}, u32[]{:S(2)}) collective-permute-start(bf16[3,64,1024]{2,1,0:T(8,128)(2,1)S(1)} %get-tuple-element.30), channel_id=1, source_target_pairs={{0,64},{4,68},{8,72},{12,76},{16,192},{20,196},{24,200},{28,204},{... | collective-permute-start | bytes 1179656 | tf_op jit(solution)/shard_map/ppermute | solution.py:30
  19.5 11.6 %collective-permute-start.2 = (bf16[3,64,1024]{2,1,0:T(8,128)(2,1)S(1)}, bf16[3,64,1024]{2,1,0:T(8,128)(2,1)S(1)}, u32[]{:S(2)}, u32[]{:S(2)}) collective-permute-start(bf16[3,64,1024]{2,1,0:T(8,128)(2,1)S(1)} %get-tuple-element.31), channel_id=1, source_target_pairs={{0,32},{4,36},{8,40},{12,44},{16,160},{20,164},{24,168},{28,172},{... | collective-permute-start | bytes 1179656 | tf_op jit(solution)/shard_map/ppermute | solution.py:30
  19.7 14.9 %collective-permute-start.4 = (bf16[3,64,1024]{2,1,0:T(8,128)(2,1)S(1)}, bf16[3,64,1024]{2,1,0:T(8,128)(2,1)S(1)}, u32[]{:S(2)}, u32[]{:S(2)}) collective-permute-start(bf16[3,64,1024]{2,1,0:T(8,128)(2,1)S(1)} %get-tuple-element.38), channel_id=1, source_target_pairs={{0,96},{4,100},{8,104},{12,108},{16,224},{20,228},{24,232},{28,236... | collective-permute-start | bytes 1179656 | tf_op jit(solution)/shard_map/ppermute | solution.py:30
  23.6 15.8 %copy-start = (bf16[256,1024]{1,0:T(8,128)(2,1)S(1)}, bf16[256,1024]{1,0:T(8,128)(2,1)}, u32[]{:S(2)}) copy-start(bf16[256,1024]{1,0:T(8,128)(2,1)} %refs_0_) | copy-start | bytes 1572868
  23.6 14.2 %collective-permute-start.5 = (bf16[3,64,1024]{2,1,0:T(8,128)(2,1)S(1)}, bf16[3,64,1024]{2,1,0:T(8,128)(2,1)S(1)}, u32[]{:S(2)}, u32[]{:S(2)}) collective-permute-start(bf16[3,64,1024]{2,1,0:T(8,128)(2,1)S(1)} %get-tuple-element.39), channel_id=1, source_target_pairs={{0,0},{4,4},{8,8},{12,12},{16,128},{20,132},{24,136},{28,140},{32,... | collective-permute-start | bytes 1179656 | tf_op jit(solution)/shard_map/ppermute | solution.py:30
  38.0 4.1 %collective-permute-start.6 = (bf16[3,64,1024]{2,1,0:T(8,128)(2,1)S(1)}, bf16[3,64,1024]{2,1,0:T(8,128)(2,1)S(1)}, u32[]{:S(2)}, u32[]{:S(2)}) collective-permute-start(bf16[3,64,1024]{2,1,0:T(8,128)(2,1)S(1)} %sum_chips.1.mine), channel_id=1, source_target_pairs={{0,16},{4,20},{8,24},{12,28},{16,0},{20,4},{24,8},{28,12},{32,48},... | collective-permute-start | bytes 1179656 | tf_op jit(solution)/shard_map/ppermute | solution.py:30
  39.4 19.8 %collective-permute-start.16 = (bf16[256,1024]{1,0:T(8,128)(2,1)S(1)}, bf16[256,1024]{1,0:T(8,128)(2,1)S(1)}, u32[]{:S(2)}, u32[]{:S(2)}) collective-permute-start(bf16[256,1024]{1,0:T(8,128)(2,1)S(1)} %copy-done), channel_id=1, source_target_pairs={{0,32},{4,36},{8,40},{12,44},{16,48},{20,52},{24,56},{28,60},{32,6... | collective-permute-start | bytes 1572872 | tf_op jit(solution)/shard_map/ppermute | solution.py:30
  39.4 19.9 %collective-permute-start.14 = (bf16[256,1024]{1,0:T(8,128)(2,1)S(1)}, bf16[256,1024]{1,0:T(8,128)(2,1)S(1)}, u32[]{:S(2)}, u32[]{:S(2)}) collective-permute-start(bf16[256,1024]{1,0:T(8,128)(2,1)S(1)} %copy-done), channel_id=1, source_target_pairs={{0,96},{4,100},{8,104},{12,108},{16,112},{20,116},{24,120},{28,124... | collective-permute-start | bytes 1572872 | tf_op jit(solution)/shard_map/ppermute | solution.py:30
  43.0 7.0 %collective-permute-start.7 = (bf16[3,32,1024]{2,1,0:T(8,128)(2,1)S(1)}, bf16[3,32,1024]{2,1,0:T(8,128)(2,1)S(1)}, u32[]{:S(2)}, u32[]{:S(2)}) collective-permute-start(bf16[3,32,1024]{2,1,0:T(8,128)(2,1)S(1)} %get-tuple-element.40.refs_1_.refs_2_), channel_id=1, source_target_pairs={{0,128},{4,132},{8,136},{12,140},{16,156},{20,144},{24,148},{28,15... | collective-permute-start | bytes 589832 | tf_op jit(solution)/shard_map/ppermute | solution.py:30
  47.4 6.0 %collective-permute-start.8 = (bf16[3,32,1024]{2,1,0:T(8,128)(2,1)S(1)}, bf16[3,32,1024]{2,1,0:T(8,128)(2,1)S(1)}, u32[]{:S(2)}, u32[]{:S(2)}) collective-permute-start(bf16[3,32,1024]{2,1,0:T(8,128)(2,1)S(1)} %get-tuple-element.41.refs_2_.refs_3_), channel_id=1, source_target_pairs={{0,128},{4,132},{8,136},{12,140},{16,156},{20,144},{24,148},{28,15... | collective-permute-start | bytes 589832 | tf_op jit(solution)/shard_map/ppermute | solution.py:30
  50.0 6.0 %collective-permute-start.9 = (bf16[3,32,1024]{2,1,0:T(8,128)(2,1)S(1)}, bf16[3,32,1024]{2,1,0:T(8,128)(2,1)S(1)}, u32[]{:S(2)}, u32[]{:S(2)}) collective-permute-start(bf16[3,32,1024]{2,1,0:T(8,128)(2,1)S(1)} %collective-permute-done.7.refs_0_), channel_id=1, source_target_pairs={{0,128},{4,132},{8,136},{12,140},{16,156},{20,144},{24,148},{28,15... | collective-permute-start | bytes 589832 | tf_op jit(solution)/shard_map/ppermute | solution.py:30
  53.5 8.6 %collective-permute-start.10 = (bf16[3,32,1024]{2,1,0:T(8,128)(2,1)S(1)}, bf16[3,32,1024]{2,1,0:T(8,128)(2,1)S(1)}, u32[]{:S(2)}, u32[]{:S(2)}) collective-permute-start(bf16[3,32,1024]{2,1,0:T(8,128)(2,1)S(1)} %collective-permute-done.8.refs_1_), channel_id=1, source_target_pairs={{0,128},{4,132},{8,136},{12,140},{16,156},{20,144},{24,148},{28,15... | collective-permute-start | bytes 589832 | tf_op jit(solution)/shard_map/ppermute | solution.py:30
  56.1 6.0 %collective-permute-start.12 = (bf16[3,32,1024]{2,1,0:T(8,128)(2,1)S(1)}, bf16[3,32,1024]{2,1,0:T(8,128)(2,1)S(1)}, u32[]{:S(2)}, u32[]{:S(2)}) collective-permute-start(bf16[3,32,1024]{2,1,0:T(8,128)(2,1)S(1)} %collective-permute-done.9.refs_2_), channel_id=1, source_target_pairs={{0,128},{4,132},{8,136},{12,140},{16,156},{20,144},{24,148},{28,15... | collective-permute-start | bytes 589832 | tf_op jit(solution)/shard_map/ppermute | solution.py:30
  59.2 9.5 %collective-permute-start.17 = (bf16[128,1024]{1,0:T(8,128)(2,1)S(1)}, bf16[128,1024]{1,0:T(8,128)(2,1)S(1)}, u32[]{:S(2)}, u32[]{:S(2)}) collective-permute-start(bf16[128,1024]{1,0:T(8,128)(2,1)S(1)} %slice.9), channel_id=1, source_target_pairs={{0,32},{4,36},{8,40},{12,44},{16,48},{20,52},{24,56},{28,60},{32,6... | collective-permute-start | bytes 786440 | tf_op jit(solution)/shard_map/ppermute | solution.py:30
  59.3 9.3 %collective-permute-start.15 = (bf16[128,1024]{1,0:T(8,128)(2,1)S(1)}, bf16[128,1024]{1,0:T(8,128)(2,1)S(1)}, u32[]{:S(2)}, u32[]{:S(2)}) collective-permute-start(bf16[128,1024]{1,0:T(8,128)(2,1)S(1)} %slice.8), channel_id=1, source_target_pairs={{0,96},{4,100},{8,104},{12,108},{16,112},{20,116},{24,120},{28,124... | collective-permute-start | bytes 786440 | tf_op jit(solution)/shard_map/ppermute | solution.py:30
  62.1 6.6 %collective-permute-start.13 = (bf16[3,32,1024]{2,1,0:T(8,128)(2,1)S(1)}, bf16[3,32,1024]{2,1,0:T(8,128)(2,1)S(1)}, u32[]{:S(2)}, u32[]{:S(2)}) collective-permute-start(bf16[3,32,1024]{2,1,0:T(8,128)(2,1)S(1)} %collective-permute-done.10.refs_3_), channel_id=1, source_target_pairs={{0,128},{4,132},{8,136},{12,140},{16,156},{20,144},{24,148},{28,15... | collective-permute-start | bytes 589832 | tf_op jit(solution)/shard_map/ppermute | solution.py:30
  62.1 6.7 %collective-permute-start.18 = (bf16[3,32,1024]{2,1,0:T(8,128)(2,1)S(1)}, bf16[3,32,1024]{2,1,0:T(8,128)(2,1)S(1)}, u32[]{:S(2)}, u32[]{:S(2)}) collective-permute-start(bf16[3,32,1024]{2,1,0:T(8,128)(2,1)S(1)} %collective-permute-done.12.refs_0_), channel_id=1, source_target_pairs={{0,128},{4,132},{8,136},{12,140},{16,156},{20,144},{24,148},{28,15... | collective-permute-start | bytes 589832 | tf_op jit(solution)/shard_map/ppermute | solution.py:30
  65.0 7.8 %collective-permute-start.11 = (bf16[3,128,1024]{2,1,0:T(8,128)(2,1)S(1)}, bf16[3,128,1024]{2,1,0:T(8,128)(2,1)S(1)}, u32[]{:S(2)}, u32[]{:S(2)}) collective-permute-start(bf16[3,128,1024]{2,1,0:T(8,128)(2,1)S(1)} %join.2.refs_3_.refs_4_), channel_id=1, source_target_pairs={{0,16},{4,20},{8,24},{12,28},{16,0},{20,4},{24,8},{28,12},{32,48},... | collective-permute-start | bytes 2359304 | tf_op jit(solution)/shard_map/ppermute | solution.py:30
  68.9 5.5 %collective-permute-start.19 = (bf16[3,96,1024]{2,1,0:T(8,128)(2,1)S(1)}, bf16[3,96,1024]{2,1,0:T(8,128)(2,1)S(1)}, u32[]{:S(2)}, u32[]{:S(2)}) collective-permute-start(bf16[3,96,1024]{2,1,0:T(8,128)(2,1)S(1)} %join.3.refs_5_.refs_6_), channel_id=1, source_target_pairs={{0,16},{4,20},{8,24},{12,28},{16,0},{20,4},{24,8},{28,12},{32,48},... | collective-permute-start | bytes 1769480 | tf_op jit(solution)/shard_map/ppermute | solution.py:30
  75.5 9.0 %collective-permute-start.22 = (bf16[128,1024]{1,0:T(8,128)(2,1)S(1)}, bf16[128,1024]{1,0:T(8,128)(2,1)S(1)}, u32[]{:S(2)}, u32[]{:S(2)}) collective-permute-start(bf16[128,1024]{1,0:T(8,128)(2,1)S(1)} %get-tuple-element.47), channel_id=1, source_target_pairs={{0,32},{4,36},{8,40},{12,44},{16,48},{20,52},{24,56},{28,60},{32,6... | collective-permute-start | bytes 786440 | tf_op jit(solution)/shard_map/ppermute | solution.py:30
  75.6 8.9 %collective-permute-start.23 = (bf16[128,1024]{1,0:T(8,128)(2,1)S(1)}, bf16[128,1024]{1,0:T(8,128)(2,1)S(1)}, u32[]{:S(2)}, u32[]{:S(2)}) collective-permute-start(bf16[128,1024]{1,0:T(8,128)(2,1)S(1)} %get-tuple-element.48), channel_id=1, source_target_pairs={{0,96},{4,100},{8,104},{12,108},{16,112},{20,116},{24,120},{28,124... | collective-permute-start | bytes 786440 | tf_op jit(solution)/shard_map/ppermute | solution.py:30
  79.3 10.6 %collective-permute-start.20 = (bf16[128,1024]{1,0:T(8,128)(2,1)S(1)}, bf16[128,1024]{1,0:T(8,128)(2,1)S(1)}, u32[]{:S(2)}, u32[]{:S(2)}) collective-permute-start(bf16[128,1024]{1,0:T(8,128)(2,1)S(1)} %get-tuple-element.43), channel_id=1, source_target_pairs={{0,32},{4,36},{8,40},{12,44},{16,48},{20,52},{24,56},{28,60},{32,6... | collective-permute-start | bytes 786440 | tf_op jit(solution)/shard_map/ppermute | solution.py:30
  79.7 10.3 %collective-permute-start.21 = (bf16[128,1024]{1,0:T(8,128)(2,1)S(1)}, bf16[128,1024]{1,0:T(8,128)(2,1)S(1)}, u32[]{:S(2)}, u32[]{:S(2)}) collective-permute-start(bf16[128,1024]{1,0:T(8,128)(2,1)S(1)} %get-tuple-element.44), channel_id=1, source_target_pairs={{0,96},{4,100},{8,104},{12,108},{16,112},{20,116},{24,120},{28,124... | collective-permute-start | bytes 786440 | tf_op jit(solution)/shard_map/ppermute | solution.py:30
  84.6 10.9 %collective-permute-start.24 = (bf16[128,1024]{1,0:T(8,128)(2,1)S(1)}, bf16[128,1024]{1,0:T(8,128)(2,1)S(1)}, u32[]{:S(2)}, u32[]{:S(2)}) collective-permute-start(bf16[128,1024]{1,0:T(8,128)(2,1)S(1)} %get-tuple-element.49), channel_id=1, source_target_pairs={{0,32},{4,36},{8,40},{12,44},{16,48},{20,52},{24,56},{28,60},{32,6... | collective-permute-start | bytes 786440 | tf_op jit(solution)/shard_map/ppermute | solution.py:30
  84.7 10.8 %collective-permute-start.25 = (bf16[128,1024]{1,0:T(8,128)(2,1)S(1)}, bf16[128,1024]{1,0:T(8,128)(2,1)S(1)}, u32[]{:S(2)}, u32[]{:S(2)}) collective-permute-start(bf16[128,1024]{1,0:T(8,128)(2,1)S(1)} %get-tuple-element.50), channel_id=1, source_target_pairs={{0,96},{4,100},{8,104},{12,108},{16,112},{20,116},{24,120},{28,124... | collective-permute-start | bytes 786440 | tf_op jit(solution)/shard_map/ppermute | solution.py:30

commit v5 on v4

v5 whole, which is shorter than its diff:
```python
import functools

import jax
import jax.numpy as jnp
from jax import lax
from jax.experimental import pallas as pl
from jax.experimental.pallas import tpu as pltpu
from jax.sharding import PartitionSpec as P

AXES = ("view", "render")
LZ, NX, NC, HZ = 2, 4, 2, 4
NZ = LZ * HZ
F32 = jnp.float32
BF16 = jnp.bfloat16
STEPS = (2, 1, 3, 0)
GROUPS = ((0, 1), (2, 3))
DELTA_US, SUM_US, OWN_US = 0.0, 10.0, 10.0


def move(array, target):
    pairs = []
    for zl in range(LZ):
        for x in range(NX):
            for core in range(NC):
                for zh in range(HZ):
                    tl, tx, tc, th = target(zl, x, core, zh)
                    pairs.append(
                        (((zl * NX + x) * NC + core) * HZ + zh, ((tl * NX + tx) * NC + tc) * HZ + th)
                    )
    return lax.ppermute(array, AXES, pairs)


def along_x(array, step):
    return move(array, lambda zl, x, c, zh: (zl, (x + step) % NX, c, zh))


def to_owner(array, step):
    return move(array, lambda zl, x, c, zh: (c, (x + step) % NX, zl, zh))


def along_z(array, step):
    def target(zl, x, c, zh):
        z = (zh * LZ + zl + (1 - 2 * c) * step) % NZ
        return z % LZ, x, c, z // LZ

    return move(array, target)


def swap_core(array):
    return move(array, lambda zl, x, c, zh: (zl, x, 1 - c, zh))


def coordinates():
    view = lax.axis_index("view")
    return lax.rem(lax.div(view, NC), NX), lax.div(view, NX * NC), lax.rem(view, NC)


def contract(left, right, left_dim, right_dim):
    return lax.dot_general(
        left, right, (((left_dim,), (right_dim,)), ((), ())), preferred_element_type=F32
    )


def cost(us):
    return pl.CostEstimate(flops=1 + int(us * 1.15e9), bytes_accessed=1, transcendentals=0)


def params(mib=32):
    return pltpu.CompilerParams(vmem_limit_bytes=mib * 1024 * 1024)


def delta_kernel(rates, keys, values, gate, up, down, *refs):
    groups = len(GROUPS)
    mine, other, old = refs[:groups], refs[groups : 2 * groups], refs[2 * groups]
    old_turned, k_ref, v_ref, columns, turned, sems = refs[2 * groups + 1 :]
    x, zl, core = coordinates()
    units = gate.shape[2] // NX
    half = units // NC
    early = keys.shape[0] // 2

    copies = [
        pltpu.make_async_copy(keys.at[:early], k_ref.at[:early], sems.at[0]),
        pltpu.make_async_copy(gate.at[0], columns.at[0], sems.at[1]),
        pltpu.make_async_copy(up.at[0], columns.at[1], sems.at[2]),
        pltpu.make_async_copy(keys.at[early:], k_ref.at[early:], sems.at[3]),
        pltpu.make_async_copy(values, v_ref, sems.at[4]),
        pltpu.make_async_copy(down.at[0], columns.at[2], sems.at[5]),
    ]
    for copy in copies:
        copy.start()
    copies[0].wait()
    parts = []
    for m in range(2):
        copies[1 + m].wait()
        parts.append(contract(columns[m], k_ref[:early], 0, 1))
    copies[3].wait()
    gate_in, up_in = (
        jnp.concatenate([part, contract(columns[m], k_ref[early:], 0, 1)], 1)
        for m, part in enumerate(parts)
    )
    copies[4].wait()
    copies[5].wait()
    k, v, r = k_ref[...], v_ref[...], rates[...]
    back = contract(columns[2], v, 0, 1)
    s = jax.nn.sigmoid(gate_in)
    act = gate_in * s
    rated = r * back
    turned[0] = (rated * up_in * s * (1.0 + gate_in * (1.0 - s))).astype(BF16)
    turned[1] = (rated * act).astype(BF16)
    turned[2] = (r * (act * up_in)).astype(BF16)
    pairs = [(c, i) for c in (1 - core, core) for i in range(NX)]
    rows = [
        pl.ds(pl.multiple_of((x + STEPS[i]) % NX * units + c * half, half), half) for c, i in pairs
    ]
    for m, tokens in enumerate((k, k, v)):
        sums = contract(jnp.concatenate([turned[m, part] for part in rows], 0), tokens, 1, 0).astype(BF16)
        for at, (_, i) in enumerate(pairs):
            g = next(g for g in range(groups) if i in GROUPS[g])
            (mine if at >= NX else other)[g][i - GROUPS[g][0], m] = sums[at * half : (at + 1) * half]
    block = pl.ds(pl.multiple_of(x * units, units), units)
    own = pl.ds(pl.multiple_of(zl * half, half), half)
    for m in range(3):
        old_turned[...] = columns[m, :, block].astype(F32).T
        old[m] = old_turned[own, :].astype(BF16)


def deltas(rates, arrays):
    count, width = arrays[0].shape
    n = arrays[2].shape[2]
    units = n // NX
    half = units // NC
    vmem = pl.BlockSpec(memory_space=pltpu.VMEM)
    out_shape = [jax.ShapeDtypeStruct((len(g), 3, half, width), BF16) for g in GROUPS * 2]
    out_shape.append(jax.ShapeDtypeStruct((3, half, width), BF16))
    return pl.pallas_call(
        delta_kernel,
        name="deltas",
        in_specs=[vmem] + [pl.BlockSpec(memory_space=pl.ANY)] * len(arrays),
        out_specs=[vmem] * len(out_shape),
        out_shape=out_shape,
        scratch_shapes=[
            pltpu.VMEM((units, width), F32),
            pltpu.VMEM((count, width), BF16),
            pltpu.VMEM((count, width), BF16),
            pltpu.VMEM((3, width, n), BF16),
            pltpu.VMEM((3, n, count), BF16),
            pltpu.SemaphoreType.DMA((6,)),
        ],
        compiler_params=params(50),
        cost_estimate=cost(DELTA_US),
    )(rates, *arrays)


def call(kernel, name, out_shape, *operands, us=0.0):
    vmem = pl.BlockSpec(memory_space=pltpu.VMEM)
    return pl.pallas_call(
        kernel,
        name=name,
        in_specs=[vmem] * len(operands),
        out_specs=jax.tree.map(lambda _: vmem, out_shape),
        out_shape=out_shape,
        compiler_params=params(),
        cost_estimate=cost(us),
    )(*operands)


def add_kernel(mine, other, *outs):
    for i, out in enumerate(outs):
        out[...] = (mine[i].astype(F32) + other[i].astype(F32)).astype(out.dtype)


def add_cores(mine, other):
    block = jax.ShapeDtypeStruct(mine.shape[1:], BF16)
    return call(add_kernel, "add_cores", [block] * mine.shape[0], mine, other)


def sum_kernel(*refs):
    sums = refs[0][...].astype(F32)
    for ref in refs[1:-1]:
        sums = sums + ref[...].astype(F32)
    refs[-1][...] = sums.astype(refs[-1].dtype)


def add_up(name, parts, us):
    return call(sum_kernel, name, jax.ShapeDtypeStruct(parts[0].shape, BF16), *parts, us=us)


def renorm_kernel(old, mine, other, *outs):
    n = outs[0].shape[1]
    _, _, core = coordinates()
    for m in range(3):
        halves = []
        for i in range(2):
            part = slice(i * n, (i + 1) * n)
            was = old[m, part, :].astype(F32)
            summed = was + (mine[m, part, :].astype(F32) + other[m, part, :].astype(F32))
            factor = jnp.sqrt(jnp.sum(was * was, axis=-1, keepdims=True)) / jnp.sqrt(
                jnp.sum(summed * summed, axis=-1, keepdims=True) + 1e-06
            )
            halves.append(summed * factor)
        for i, out in enumerate(outs):
            out[m] = jnp.where(core == i, halves[0], halves[1]).astype(BF16)


def join_kernel(*refs):
    out = refs[-1]
    at = 0
    for ref in refs[:-1]:
        n = ref.shape[1]
        out[:, at : at + n, :] = ref[...]
        at += n


def join(pieces):
    units = sum(p.shape[1] for p in pieces)
    out = jax.ShapeDtypeStruct((3, units, pieces[0].shape[2]), BF16)
    return call(join_kernel, "join", out, *pieces)


def render_kernel(cuts, count, added, *refs):
    rows, pieces, outs = refs[: len(cuts)], refs[len(cuts) : -count], refs[-count:]
    if added:
        *pieces, before = pieces
    gate, up, down = (jnp.concatenate([p[m] for p in pieces], 0) for m in range(3))
    q = jnp.concatenate([ref[lo:hi, :] for ref, (lo, hi) in zip(rows, cuts)], 0)
    gate_q = contract(q, gate, 1, 1)
    up_q = contract(q, up, 1, 1)
    hidden_q = (gate_q * jax.nn.sigmoid(gate_q) * up_q).astype(BF16)
    partial = contract(hidden_q, down, 1, 0)
    if added:
        partial = before[...] + partial
    n = outs[0].shape[0]
    for i, out in enumerate(outs):
        out[...] = partial[i * n : (i + 1) * n].astype(out.dtype)


def render(rows, pieces, outs, before=None):
    cuts = tuple((lo, hi) for _, lo, hi in rows)
    kernel = functools.partial(render_kernel, cuts, len(outs), before is not None)
    operands = [r[0] for r in rows] + list(pieces) + ([] if before is None else [before])
    return call(kernel, "render_rows", outs, *operands)


def merge_kernel(mid, relay_left, relay_right, to_right, to_left):
    half = to_right.shape[0]
    to_right[...] = (mid[:half] + relay_left[...].astype(F32)).astype(BF16)
    to_left[...] = (mid[half:] + relay_right[...].astype(F32)).astype(BF16)


def own_kernel(own, from_left, from_right, out):
    half = from_left.shape[0]
    out[:half] = own[:half] + from_right[...].astype(F32)
    out[half:] = own[half:] + from_left[...].astype(F32)


def total_kernel(own, last_left, last_right, out):
    half = last_left.shape[0]
    out[:half] = (own[:half] + last_left[...].astype(F32)).astype(BF16)
    out[half:] = (own[half:] + last_right[...].astype(F32)).astype(BF16)


def local(input_keys, input_values, token_rates, gate_weight, up_weight, down_weight, queries):
    arrays = (input_keys, input_values, gate_weight, up_weight, down_weight)
    *parts, old = deltas(token_rates, arrays)
    chips = []
    for mine, other in zip(parts, parts[len(GROUPS) :]):
        chips += add_cores(mine, swap_core(other))
    got = [to_owner(chip, step) for chip, step in zip(chips, STEPS)]

    queries, *got[:2] = lax.optimization_barrier((queries, *got[:2]))
    half = queries.shape[0] // 2
    from_right, from_left = along_x(queries, -1), along_x(queries, 1)
    sums = add_up("sum_chips", got, SUM_US)
    out = jax.ShapeDtypeStruct((3, sums.shape[1] // 2, sums.shape[2]), BF16)
    news = call(renorm_kernel, "renorm", [out] * 2, old, sums, swap_core(sums))
    first = [along_z(new, 1) for new in news]
    second = [along_z(piece, 1) for piece in first]
    third = [along_z(piece, 1) for piece in second]
    far_top, far_low = along_x(from_right[:half], -1), along_x(from_left[half:], 1)
    third[1], far_top, far_low = lax.optimization_barrier((third[1], far_top, far_low))
    fourth = along_z(third[0], 1)
    near, last = join(first + second), join(third + [fourth])
    early, late = list(news) + [near, last], [swap_core(near), swap_core(last)]

    both, width = 2 * half, queries.shape[1]
    part = jax.ShapeDtypeStruct((half, width), BF16)
    wide = jax.ShapeDtypeStruct((both, width), F32)
    sets = [
        ([(far_top, 0, half), (far_low, 0, half)], [part] * 2),
        ([(from_right, half, both), (from_left, 0, half)], [part] * 2),
        ([(from_right, 0, half), (from_left, half, both)], [wide]),
        ([(queries, 0, both)], [wide]),
    ]
    (before,) = render(sets[0][0], early, [wide])
    late[1], before = lax.optimization_barrier((late[1], before))
    to_right, to_left = render(sets[0][0], late, sets[0][1], before)
    direct, (mid,), (own,) = (render(rows, early + late, outs) for rows, outs in sets[1:])
    relay_left, relay_right = along_x(to_right, 1), along_x(to_left, -1)
    from_left_x, from_right_x = along_x(direct[0], 1), along_x(direct[1], -1)
    to_right, to_left = call(merge_kernel, "merge", [part] * 2, mid, relay_left, relay_right)
    last_left, last_right = along_x(to_right, 1), along_x(to_left, -1)
    own = call(own_kernel, "own", wide, own, from_left_x, from_right_x, us=OWN_US)
    out = jax.ShapeDtypeStruct(own.shape, BF16)
    return call(total_kernel, "total", out, own, last_left, last_right)


def solution(mesh):
    return jax.shard_map(
        local,
        mesh=mesh,
        in_specs=(
            P("view", "head"),
            P("view", "head"),
            P("head", "view"),
            P("head", None, "render"),
            P("head", None, "render"),
            P("head", None, "render"),
            P(("view", "render"), "head"),
        ),
        out_specs=P(("view", "render"), "head"),
        check_vma=False,
    )
```

time: 96.6 us -> 94.7 us (0.980)
    pallas_call x14 -> x15, Pallas kernels: 17.5 us -> 16.7 us  [the longest x1 9.71 us: deltas(): pl.pallas_call(delta_kernel, name='deltas', in_specs=[vmem] + [pl.BlockSp...]
  transfers between devices with their start and end apart: 26 -> 26, of which waited for: 12 -> 12; matrix products, arithmetic and copies ran while one was open for 0% -> 0% of each run, Pallas kernels for 5% -> 6%
where the time goes in v5:
time: 94.7 us; the launch traced here: 94.6 us
  starting transfers between devices  48.3 us (51%)
  waiting for transfers between devices  28.6 us (30%)
  Pallas kernels  16.7 us (18%)
    ppermute x26, starting transfers between devices, move(): return lax.ppermute(array, AXES, pairs)  48.3 us
    ppermute x26, waiting for transfers between devices, move(): return lax.ppermute(array, AXES, pairs)  28.6 us
    pallas_call x1, Pallas kernels, deltas(): pl.pallas_call(delta_kernel, name='deltas', in_specs=[vmem] + [pl.BlockSp...  9.71 us
    pallas_call x14, Pallas kernels, call(): pl.pallas_call(kernel, name=name, in_specs=[vmem] * len(operands), out_sp...  7.04 us
  transfers between devices with their start and end apart: 26, of which 12 were waited for; matrix products, arithmetic and copies ran while one was open for 0% of the time, Pallas kernels for 6%

profile of v5, /device:TPU:1, one launch (start us, length us, event | category | flops | bytes accessed | tf_op | source)
XLA Modules:
  0.0 94.6 jit_solution(12045444274351959850)
XLA Ops:
  0.0 0.7 copy-done.1
  0.7 9.7 %deltas.1 = (bf16[2,3,64,1024]{3,2,1,0:T(8,128)(2,1)S(1)}, bf16[2,3,64,1024]{3,2,1,0:T(8,128)(2,1)S(1)}, bf16[2,3,64,1024]{3,2,1,0:T(8,128)(2,1)S(1)}, bf16[2,3,...) custom-call(f32[1,1024]{1,0:T(1,128)S(1)} %copy-done.1, bf16[1024,1024]{1,0:T(8,128)(2,1)} %keys.1, ...), custom_call_target="tpu_custom_call" | custom-call | flops 1 | bytes 1 | tf_op jit(solution)/shard_map/deltas/pallas_call | solution.py:135
  10.4 3.3 %collective-permute-start = (bf16[2,3,64,1024]{3,2,1,0:T(8,128)(2,1)S(1)}, bf16[2,3,64,1024]{3,2,1,0:T(8,128)(2,1)S(1)}, u32[]{:S(2)}, u32[]{:S(2)}) collective-permute-start(bf16[2,3,64,1024]{3,2,1,0:T(8,128)(2,1)S(1)} %get-tuple-element.31), channel_id=1, source_target_pairs={{0,16},{4,20},{8,24},{12,28},{16,0},{20,4},{24,8},{28,12},{32,48},... | collective-permute-start | bytes 2359304 | tf_op jit(solution)/shard_map/ppermute | solution.py:30
  13.7 0.1 collective-permute-start.3
  13.8 1.8 %collective-permute-done.other = bf16[2,3,64,1024]{3,2,1,0:T(8,128)(2,1)S(1)} collective-permute-done((bf16[2,3,64,1024]{3,2,1,0:T(8,128)(2,1)S(1)}, bf16[2,3,64,1024]{3,2,1,0:T(8,128)(2,1)S(1)}, u32[]{:S(2)}, u32[]{:S(2)}) %collective-permute-start) | collective-permute-done | bytes 786464 | tf_op jit(solution)/shard_map/ppermute | solution.py:30
  15.7 0.2 add_cores.2
  15.8 2.7 %collective-permute-start.1 = (bf16[3,64,1024]{2,1,0:T(8,128)(2,1)S(1)}, bf16[3,64,1024]{2,1,0:T(8,128)(2,1)S(1)}, u32[]{:S(2)}, u32[]{:S(2)}) collective-permute-start(bf16[3,64,1024]{2,1,0:T(8,128)(2,1)S(1)} %get-tuple-element.32), channel_id=1, source_target_pairs={{0,64},{4,68},{8,72},{12,76},{16,192},{20,196},{24,200},{28,204},{... | collective-permute-start | bytes 1179656 | tf_op jit(solution)/shard_map/ppermute | solution.py:30
  18.5 0.0 collective-permute-start.2
  18.5 0.0 collective-permute-done.3.other
  18.6 0.2 add_cores.3
  18.7 3.9 %collective-permute-start.4 = (bf16[3,64,1024]{2,1,0:T(8,128)(2,1)S(1)}, bf16[3,64,1024]{2,1,0:T(8,128)(2,1)S(1)}, u32[]{:S(2)}, u32[]{:S(2)}) collective-permute-start(bf16[3,64,1024]{2,1,0:T(8,128)(2,1)S(1)} %get-tuple-element.40), channel_id=1, source_target_pairs={{0,96},{4,100},{8,104},{12,108},{16,224},{20,228},{24,232},{28,236... | collective-permute-start | bytes 1179656 | tf_op jit(solution)/shard_map/ppermute | solution.py:30
  22.7 2.0 %collective-permute-start.5 = (bf16[3,64,1024]{2,1,0:T(8,128)(2,1)S(1)}, bf16[3,64,1024]{2,1,0:T(8,128)(2,1)S(1)}, u32[]{:S(2)}, u32[]{:S(2)}) collective-permute-start(bf16[3,64,1024]{2,1,0:T(8,128)(2,1)S(1)} %get-tuple-element.41), channel_id=1, source_target_pairs={{0,0},{4,4},{8,8},{12,12},{16,128},{20,132},{24,136},{28,140},{32,... | collective-permute-start | bytes 1179656 | tf_op jit(solution)/shard_map/ppermute | solution.py:30
  24.7 2.1 %collective-permute-done.1.refs_0_ = bf16[3,64,1024]{2,1,0:T(8,128)(2,1)S(1)} collective-permute-done((bf16[3,64,1024]{2,1,0:T(8,128)(2,1)S(1)}, bf16[3,64,1024]{2,1,0:T(8,128)(2,1)S(1)}, u32[]{:S(2)}, u32[]{:S(2)}) %collective-permute-start.1) | collective-permute-done | bytes 393248 | tf_op jit(solution)/shard_map/ppermute | solution.py:30
  26.8 3.3 %collective-permute-done.2.refs_1_ = bf16[3,64,1024]{2,1,0:T(8,128)(2,1)S(1)} collective-permute-done((bf16[3,64,1024]{2,1,0:T(8,128)(2,1)S(1)}, bf16[3,64,1024]{2,1,0:T(8,128)(2,1)S(1)}, u32[]{:S(2)}, u32[]{:S(2)}) %collective-permute-start.2) | collective-permute-done | bytes 393248 | tf_op jit(solution)/shard_map/ppermute | solution.py:30
  30.2 3.5 %collective-permute-done.4.refs_2_ = bf16[3,64,1024]{2,1,0:T(8,128)(2,1)S(1)} collective-permute-done((bf16[3,64,1024]{2,1,0:T(8,128)(2,1)S(1)}, bf16[3,64,1024]{2,1,0:T(8,128)(2,1)S(1)}, u32[]{:S(2)}, u32[]{:S(2)}) %collective-permute-start.4) | collective-permute-done | bytes 393248 | tf_op jit(solution)/shard_map/ppermute | solution.py:30
  33.7 3.2 %collective-permute-done.5.refs_3_ = bf16[3,64,1024]{2,1,0:T(8,128)(2,1)S(1)} collective-permute-done((bf16[3,64,1024]{2,1,0:T(8,128)(2,1)S(1)}, bf16[3,64,1024]{2,1,0:T(8,128)(2,1)S(1)}, u32[]{:S(2)}, u32[]{:S(2)}) %collective-permute-start.5) | collective-permute-done | bytes 393248 | tf_op jit(solution)/shard_map/ppermute | solution.py:30
  36.9 0.2 sum_chips.1.mine
  37.1 1.4 %collective-permute-start.6 = (bf16[3,64,1024]{2,1,0:T(8,128)(2,1)S(1)}, bf16[3,64,1024]{2,1,0:T(8,128)(2,1)S(1)}, u32[]{:S(2)}, u32[]{:S(2)}) collective-permute-start(bf16[3,64,1024]{2,1,0:T(8,128)(2,1)S(1)} %sum_chips.1.mine), channel_id=1, source_target_pairs={{0,16},{4,20},{8,24},{12,28},{16,0},{20,4},{24,8},{28,12},{32,48},... | collective-permute-start | bytes 1179656 | tf_op jit(solution)/shard_map/ppermute | solution.py:30
  38.5 0.0 collective-permute-start.15
  38.5 2.7 %collective-permute-start.13 = (bf16[256,1024]{1,0:T(8,128)(2,1)S(1)}, bf16[256,1024]{1,0:T(8,128)(2,1)S(1)}, u32[]{:S(2)}, u32[]{:S(2)}) collective-permute-start(bf16[256,1024]{1,0:T(8,128)(2,1)S(1)} %copy-done), channel_id=1, source_target_pairs={{0,96},{4,100},{8,104},{12,108},{16,112},{20,116},{24,120},{28,124... | collective-permute-start | bytes 1572872 | tf_op jit(solution)/shard_map/ppermute | solution.py:30
  41.2 0.0 collective-permute-done.6.other
  41.2 0.4 renorm.1
  41.6 4.4 %collective-permute-start.7 = (bf16[3,32,1024]{2,1,0:T(8,128)(2,1)S(1)}, bf16[3,32,1024]{2,1,0:T(8,128)(2,1)S(1)}, u32[]{:S(2)}, u32[]{:S(2)}) collective-permute-start(bf16[3,32,1024]{2,1,0:T(8,128)(2,1)S(1)} %get-tuple-element.42.refs_2_.refs_1_), channel_id=1, source_target_pairs={{0,128},{4,132},{8,136},{12,140},{16,156},{20,144},{24,148},{28,15... | collective-permute-start | bytes 589832 | tf_op jit(solution)/shard_map/ppermute | solution.py:30
  46.0 0.4 collective-permute-start.8
  46.4 2.2 %collective-permute-done.7.refs_0_ = bf16[3,32,1024]{2,1,0:T(8,128)(2,1)S(1)} collective-permute-done((bf16[3,32,1024]{2,1,0:T(8,128)(2,1)S(1)}, bf16[3,32,1024]{2,1,0:T(8,128)(2,1)S(1)}, u32[]{:S(2)}, u32[]{:S(2)}) %collective-permute-start.7) | collective-permute-done | bytes 196640 | tf_op jit(solution)/shard_map/ppermute | solution.py:30
  48.6 3.4 %collective-permute-start.9 = (bf16[3,32,1024]{2,1,0:T(8,128)(2,1)S(1)}, bf16[3,32,1024]{2,1,0:T(8,128)(2,1)S(1)}, u32[]{:S(2)}, u32[]{:S(2)}) collective-permute-start(bf16[3,32,1024]{2,1,0:T(8,128)(2,1)S(1)} %collective-permute-done.7.refs_0_), channel_id=1, source_target_pairs={{0,128},{4,132},{8,136},{12,140},{16,156},{20,144},{24,148},{28,15... | collective-permute-start | bytes 589832 | tf_op jit(solution)/shard_map/ppermute | solution.py:30
  52.0 2.1 %collective-permute-start.10 = (bf16[3,32,1024]{2,1,0:T(8,128)(2,1)S(1)}, bf16[3,32,1024]{2,1,0:T(8,128)(2,1)S(1)}, u32[]{:S(2)}, u32[]{:S(2)}) collective-permute-start(bf16[3,32,1024]{2,1,0:T(8,128)(2,1)S(1)} %collective-permute-done.8.refs_1_), channel_id=1, source_target_pairs={{0,128},{4,132},{8,136},{12,140},{16,156},{20,144},{24,148},{28,15... | collective-permute-start | bytes 589832 | tf_op jit(solution)/shard_map/ppermute | solution.py:30
  54.1 0.5 collective-permute-done.9.refs_2_
  54.6 3.4 %collective-permute-start.11 = (bf16[3,32,1024]{2,1,0:T(8,128)(2,1)S(1)}, bf16[3,32,1024]{2,1,0:T(8,128)(2,1)S(1)}, u32[]{:S(2)}, u32[]{:S(2)}) collective-permute-start(bf16[3,32,1024]{2,1,0:T(8,128)(2,1)S(1)} %collective-permute-done.9.refs_2_), channel_id=1, source_target_pairs={{0,128},{4,132},{8,136},{12,140},{16,156},{20,144},{24,148},{28,15... | collective-permute-start | bytes 589832 | tf_op jit(solution)/shard_map/ppermute | solution.py:30
  58.0 0.0 collective-permute-done.15.refs_1_
  58.0 0.1 collective-permute-start.16
  58.1 0.0 collective-permute-done.13.refs_0_
  58.2 2.7 %collective-permute-start.14 = (bf16[128,1024]{1,0:T(8,128)(2,1)S(1)}, bf16[128,1024]{1,0:T(8,128)(2,1)S(1)}, u32[]{:S(2)}, u32[]{:S(2)}) collective-permute-start(bf16[128,1024]{1,0:T(8,128)(2,1)S(1)} %slice.8), channel_id=1, source_target_pairs={{0,96},{4,100},{8,104},{12,108},{16,112},{20,116},{24,120},{28,124... | collective-permute-start | bytes 786440 | tf_op jit(solution)/shard_map/ppermute | solution.py:30
  60.9 0.0 collective-permute-start.12
  60.9 2.8 %collective-permute-start.17 = (bf16[3,32,1024]{2,1,0:T(8,128)(2,1)S(1)}, bf16[3,32,1024]{2,1,0:T(8,128)(2,1)S(1)}, u32[]{:S(2)}, u32[]{:S(2)}) collective-permute-start(bf16[3,32,1024]{2,1,0:T(8,128)(2,1)S(1)} %collective-permute-done.11.refs_0_), channel_id=1, source_target_pairs={{0,128},{4,132},{8,136},{12,140},{16,156},{20,144},{24,148},{28,15... | collective-permute-start | bytes 589832 | tf_op jit(solution)/shard_map/ppermute | solution.py:30
  63.7 0.1 join.2.refs_4_.refs_3_
  63.8 0.7 collective-permute-start.18
  64.5 3.0 %collective-permute-done.16.refs_1_ = bf16[128,1024]{1,0:T(8,128)(2,1)S(1)} collective-permute-done((bf16[128,1024]{1,0:T(8,128)(2,1)S(1)}, bf16[128,1024]{1,0:T(8,128)(2,1)S(1)}, u32[]{:S(2)}, u32[]{:S(2)}) %collective-permute-start.16) | collective-permute-done | bytes 262176 | tf_op jit(solution)/shard_map/ppermute | solution.py:30
  67.4 0.0 collective-permute-done.14.refs_0_
  67.4 0.0 collective-permute-done.12.refs_1_
  67.4 0.1 collective-permute-done.17.refs_2_
  67.6 3.8 %collective-permute-start.19 = (bf16[3,96,1024]{2,1,0:T(8,128)(2,1)S(1)}, bf16[3,96,1024]{2,1,0:T(8,128)(2,1)S(1)}, u32[]{:S(2)}, u32[]{:S(2)}) collective-permute-start(bf16[3,96,1024]{2,1,0:T(8,128)(2,1)S(1)} %join.3.refs_5_.refs_4_), channel_id=1, source_target_pairs={{0,16},{4,20},{8,24},{12,28},{16,0},{20,4},{24,8},{28,12},{32,48},... | collective-permute-start | bytes 1769480 | tf_op jit(solution)/shard_map/ppermute | solution.py:30
  71.3 1.0 %render_rows.5.refs_4_ = f32[256,1024]{1,0:T(8,128)S(1)} custom-call(bf16[128,1024]{1,0:T(8,128)(2,1)S(1)} %collective-permute-done.14.refs_0_, bf16[128,1024]{1,0:T(8,128)(2,1)S(1)} %collective-permute-done.16.refs_1_, bf16[3,32,1024]{2,1,0:T(8,128)(2,1)S(1)} %get-tuple-element.42.refs_2_.refs_1_, ...), custom_call_target="tpu_custom_call" | custom-call | flops 1 | bytes 1 | tf_op jit(solution)/shard_map/render_rows/pallas_call | solution.py:156
  72.4 0.6 collective-permute-done.19.refs_6_.refs_7_.refs_3_
  73.0 0.0 collective-permute-done.18.refs_5_.refs_6_.refs_2_
  73.0 0.7 render_rows.9
  73.6 0.1 collective-permute-start.22
  73.7 2.6 %collective-permute-start.23 = (bf16[128,1024]{1,0:T(8,128)(2,1)S(1)}, bf16[128,1024]{1,0:T(8,128)(2,1)S(1)}, u32[]{:S(2)}, u32[]{:S(2)}) collective-permute-start(bf16[128,1024]{1,0:T(8,128)(2,1)S(1)} %get-tuple-element.52), channel_id=1, source_target_pairs={{0,96},{4,100},{8,104},{12,108},{16,112},{20,116},{24,120},{28,124... | collective-permute-start | bytes 786440 | tf_op jit(solution)/shard_map/ppermute | solution.py:30
  76.4 1.1 %render_rows.7 = (bf16[128,1024]{1,0:T(8,128)(2,1)S(1)}, bf16[128,1024]{1,0:T(8,128)(2,1)S(1)}) custom-call(bf16[256,1024]{1,0:T(8,128)(2,1)S(1)} %collective-permute-done.13.refs_0_, bf16[256,1024]{1,0:T(8,128)(2,1)S(1)} %collective-permute-done.15.refs_1_, bf16[3,32,1024]{2,1,0:T(8,128)(2,1)S(1)} %get-tuple-element.42.refs_2_.refs_1_, ...), custom_call_target="tpu_custom_call" | custom-call | flops 1 | bytes 1 | tf_op jit(solution)/shard_map/render_rows/pallas_call | solution.py:156
  77.5 0.1 collective-permute-start.20
  77.6 2.7 %collective-permute-start.21 = (bf16[128,1024]{1,0:T(8,128)(2,1)S(1)}, bf16[128,1024]{1,0:T(8,128)(2,1)S(1)}, u32[]{:S(2)}, u32[]{:S(2)}) collective-permute-start(bf16[128,1024]{1,0:T(8,128)(2,1)S(1)} %get-tuple-element.49), channel_id=1, source_target_pairs={{0,96},{4,100},{8,104},{12,108},{16,112},{20,116},{24,120},{28,124... | collective-permute-start | bytes 786440 | tf_op jit(solution)/shard_map/ppermute | solution.py:30
  80.2 1.1 %render_rows.8.mid = f32[256,1024]{1,0:T(8,128)S(1)} custom-call(bf16[256,1024]{1,0:T(8,128)(2,1)S(1)} %collective-permute-done.13.refs_0_, bf16[256,1024]{1,0:T(8,128)(2,1)S(1)} %collective-permute-done.15.refs_1_, bf16[3,32,1024]{2,1,0:T(8,128)(2,1)S(1)} %get-tuple-element.42.refs_2_.refs_1_, bf16[3,32,1024]{2,1,0:T(8,128)(2,1)S(1)} %get-tuple-element.43.refs_3_.refs_2_, ...), custom_call_target="tpu_custom_call" | custom-call | flops 1 | bytes 1 | tf_op jit(solution)/shard_map/render_rows/pallas_call | solution.py:156
  81.3 1.1 %render_rows.6.own = f32[256,1024]{1,0:T(8,128)S(1)} custom-call(bf16[256,1024]{1,0:T(8,128)(2,1)S(1)} %copy-done, bf16[3,32,1024]{2,1,0:T(8,128)(2,1)S(1)} %get-tuple-element.42.refs_2_.refs_1_, bf16[3,32,1024]{2,1,0:T(8,128)(2,1)S(1)} %get-tuple-element.43.refs_3_.refs_2_, bf16[3,128,1024]{2,1,0:T(8,128)(2,1)S(1)} %join.2.refs_4_.refs_3_, ...), custom_call_target="tpu_custom_call" | custom-call | flops 1 | bytes 1 | tf_op jit(solution)/shard_map/render_rows/pallas_call | solution.py:156
  82.4 0.0 collective-permute-done.22.relay_left
  82.4 0.0 collective-permute-done.23.relay_right
  82.5 0.1 merge.1
  82.6 0.1 collective-permute-start.24
  82.6 2.7 %collective-permute-start.25 = (bf16[128,1024]{1,0:T(8,128)(2,1)S(1)}, bf16[128,1024]{1,0:T(8,128)(2,1)S(1)}, u32[]{:S(2)}, u32[]{:S(2)}) collective-permute-start(bf16[128,1024]{1,0:T(8,128)(2,1)S(1)} %get-tuple-element.54), channel_id=1, source_target_pairs={{0,96},{4,100},{8,104},{12,108},{16,112},{20,116},{24,120},{28,124... | collective-permute-start | bytes 786440 | tf_op jit(solution)/shard_map/ppermute | solution.py:30
  85.3 2.8 %collective-permute-done.20.from_left = bf16[128,1024]{1,0:T(8,128)(2,1)S(1)} collective-permute-done((bf16[128,1024]{1,0:T(8,128)(2,1)S(1)}, bf16[128,1024]{1,0:T(8,128)(2,1)S(1)}, u32[]{:S(2)}, u32[]{:S(2)}) %collective-permute-start.20) | collective-permute-done | bytes 262176 | tf_op jit(solution)/shard_map/ppermute | solution.py:30
  88.1 0.0 collective-permute-done.21.from_right
  88.1 0.1 own.1
  88.2 5.5 %collective-permute-done.24.last_left = bf16[128,1024]{1,0:T(8,128)(2,1)S(1)} collective-permute-done((bf16[128,1024]{1,0:T(8,128)(2,1)S(1)}, bf16[128,1024]{1,0:T(8,128)(2,1)S(1)}, u32[]{:S(2)}, u32[]{:S(2)}) %collective-permute-start.24) | collective-permute-done | bytes 262176 | tf_op jit(solution)/shard_map/ppermute | solution.py:30
  93.7 0.0 collective-permute-done.25.last_right
  93.7 0.9 total.1
  (9 shorter events, 0.1 us)
Async XLA Ops:
  0.0 0.7 copy-start.1
  10.4 5.2 %collective-permute-start = (bf16[2,3,64,1024]{3,2,1,0:T(8,128)(2,1)S(1)}, bf16[2,3,64,1024]{3,2,1,0:T(8,128)(2,1)S(1)}, u32[]{:S(2)}, u32[]{:S(2)}) collective-permute-start(bf16[2,3,64,1024]{3,2,1,0:T(8,128)(2,1)S(1)} %get-tuple-element.31), channel_id=1, source_target_pairs={{0,16},{4,20},{8,24},{12,28},{16,0},{20,4},{24,8},{28,12},{32,48},... | collective-permute-start | bytes 2359304 | tf_op jit(solution)/shard_map/ppermute | solution.py:30
  13.7 4.8 %collective-permute-start.3 = (bf16[2,3,64,1024]{3,2,1,0:T(8,128)(2,1)S(1)}, bf16[2,3,64,1024]{3,2,1,0:T(8,128)(2,1)S(1)}, u32[]{:S(2)}, u32[]{:S(2)}) collective-permute-start(bf16[2,3,64,1024]{3,2,1,0:T(8,128)(2,1)S(1)} %get-tuple-element.39), channel_id=1, source_target_pairs={{0,16},{4,20},{8,24},{12,28},{16,0},{20,4},{24,8},{28,12},{32,48},... | collective-permute-start | bytes 2359304 | tf_op jit(solution)/shard_map/ppermute | solution.py:30
  15.8 11.0 %collective-permute-start.1 = (bf16[3,64,1024]{2,1,0:T(8,128)(2,1)S(1)}, bf16[3,64,1024]{2,1,0:T(8,128)(2,1)S(1)}, u32[]{:S(2)}, u32[]{:S(2)}) collective-permute-start(bf16[3,64,1024]{2,1,0:T(8,128)(2,1)S(1)} %get-tuple-element.32), channel_id=1, source_target_pairs={{0,64},{4,68},{8,72},{12,76},{16,192},{20,196},{24,200},{28,204},{... | collective-permute-start | bytes 1179656 | tf_op jit(solution)/shard_map/ppermute | solution.py:30
  18.5 11.6 %collective-permute-start.2 = (bf16[3,64,1024]{2,1,0:T(8,128)(2,1)S(1)}, bf16[3,64,1024]{2,1,0:T(8,128)(2,1)S(1)}, u32[]{:S(2)}, u32[]{:S(2)}) collective-permute-start(bf16[3,64,1024]{2,1,0:T(8,128)(2,1)S(1)} %get-tuple-element.33), channel_id=1, source_target_pairs={{0,32},{4,36},{8,40},{12,44},{16,160},{20,164},{24,168},{28,172},{... | collective-permute-start | bytes 1179656 | tf_op jit(solution)/shard_map/ppermute | solution.py:30
  18.7 14.9 %collective-permute-start.4 = (bf16[3,64,1024]{2,1,0:T(8,128)(2,1)S(1)}, bf16[3,64,1024]{2,1,0:T(8,128)(2,1)S(1)}, u32[]{:S(2)}, u32[]{:S(2)}) collective-permute-start(bf16[3,64,1024]{2,1,0:T(8,128)(2,1)S(1)} %get-tuple-element.40), channel_id=1, source_target_pairs={{0,96},{4,100},{8,104},{12,108},{16,224},{20,228},{24,232},{28,236... | collective-permute-start | bytes 1179656 | tf_op jit(solution)/shard_map/ppermute | solution.py:30
  22.7 15.9 %copy-start = (bf16[256,1024]{1,0:T(8,128)(2,1)S(1)}, bf16[256,1024]{1,0:T(8,128)(2,1)}, u32[]{:S(2)}) copy-start(bf16[256,1024]{1,0:T(8,128)(2,1)} %refs_0_) | copy-start | bytes 1572868
  22.7 14.2 %collective-permute-start.5 = (bf16[3,64,1024]{2,1,0:T(8,128)(2,1)S(1)}, bf16[3,64,1024]{2,1,0:T(8,128)(2,1)S(1)}, u32[]{:S(2)}, u32[]{:S(2)}) collective-permute-start(bf16[3,64,1024]{2,1,0:T(8,128)(2,1)S(1)} %get-tuple-element.41), channel_id=1, source_target_pairs={{0,0},{4,4},{8,8},{12,12},{16,128},{20,132},{24,136},{28,140},{32,... | collective-permute-start | bytes 1179656 | tf_op jit(solution)/shard_map/ppermute | solution.py:30
  37.1 4.1 %collective-permute-start.6 = (bf16[3,64,1024]{2,1,0:T(8,128)(2,1)S(1)}, bf16[3,64,1024]{2,1,0:T(8,128)(2,1)S(1)}, u32[]{:S(2)}, u32[]{:S(2)}) collective-permute-start(bf16[3,64,1024]{2,1,0:T(8,128)(2,1)S(1)} %sum_chips.1.mine), channel_id=1, source_target_pairs={{0,16},{4,20},{8,24},{12,28},{16,0},{20,4},{24,8},{28,12},{32,48},... | collective-permute-start | bytes 1179656 | tf_op jit(solution)/shard_map/ppermute | solution.py:30
  38.5 19.5 %collective-permute-start.15 = (bf16[256,1024]{1,0:T(8,128)(2,1)S(1)}, bf16[256,1024]{1,0:T(8,128)(2,1)S(1)}, u32[]{:S(2)}, u32[]{:S(2)}) collective-permute-start(bf16[256,1024]{1,0:T(8,128)(2,1)S(1)} %copy-done), channel_id=1, source_target_pairs={{0,32},{4,36},{8,40},{12,44},{16,48},{20,52},{24,56},{28,60},{32,6... | collective-permute-start | bytes 1572872 | tf_op jit(solution)/shard_map/ppermute | solution.py:30
  38.5 19.6 %collective-permute-start.13 = (bf16[256,1024]{1,0:T(8,128)(2,1)S(1)}, bf16[256,1024]{1,0:T(8,128)(2,1)S(1)}, u32[]{:S(2)}, u32[]{:S(2)}) collective-permute-start(bf16[256,1024]{1,0:T(8,128)(2,1)S(1)} %copy-done), channel_id=1, source_target_pairs={{0,96},{4,100},{8,104},{12,108},{16,112},{20,116},{24,120},{28,124... | collective-permute-start | bytes 1572872 | tf_op jit(solution)/shard_map/ppermute | solution.py:30
  41.6 7.0 %collective-permute-start.7 = (bf16[3,32,1024]{2,1,0:T(8,128)(2,1)S(1)}, bf16[3,32,1024]{2,1,0:T(8,128)(2,1)S(1)}, u32[]{:S(2)}, u32[]{:S(2)}) collective-permute-start(bf16[3,32,1024]{2,1,0:T(8,128)(2,1)S(1)} %get-tuple-element.42.refs_2_.refs_1_), channel_id=1, source_target_pairs={{0,128},{4,132},{8,136},{12,140},{16,156},{20,144},{24,148},{28,15... | collective-permute-start | bytes 589832 | tf_op jit(solution)/shard_map/ppermute | solution.py:30
  46.0 6.0 %collective-permute-start.8 = (bf16[3,32,1024]{2,1,0:T(8,128)(2,1)S(1)}, bf16[3,32,1024]{2,1,0:T(8,128)(2,1)S(1)}, u32[]{:S(2)}, u32[]{:S(2)}) collective-permute-start(bf16[3,32,1024]{2,1,0:T(8,128)(2,1)S(1)} %get-tuple-element.43.refs_3_.refs_2_), channel_id=1, source_target_pairs={{0,128},{4,132},{8,136},{12,140},{16,156},{20,144},{24,148},{28,15... | collective-permute-start | bytes 589832 | tf_op jit(solution)/shard_map/ppermute | solution.py:30
  48.6 6.0 %collective-permute-start.9 = (bf16[3,32,1024]{2,1,0:T(8,128)(2,1)S(1)}, bf16[3,32,1024]{2,1,0:T(8,128)(2,1)S(1)}, u32[]{:S(2)}, u32[]{:S(2)}) collective-permute-start(bf16[3,32,1024]{2,1,0:T(8,128)(2,1)S(1)} %collective-permute-done.7.refs_0_), channel_id=1, source_target_pairs={{0,128},{4,132},{8,136},{12,140},{16,156},{20,144},{24,148},{28,15... | collective-permute-start | bytes 589832 | tf_op jit(solution)/shard_map/ppermute | solution.py:30
  52.0 8.9 %collective-permute-start.10 = (bf16[3,32,1024]{2,1,0:T(8,128)(2,1)S(1)}, bf16[3,32,1024]{2,1,0:T(8,128)(2,1)S(1)}, u32[]{:S(2)}, u32[]{:S(2)}) collective-permute-start(bf16[3,32,1024]{2,1,0:T(8,128)(2,1)S(1)} %collective-permute-done.8.refs_1_), channel_id=1, source_target_pairs={{0,128},{4,132},{8,136},{12,140},{16,156},{20,144},{24,148},{28,15... | collective-permute-start | bytes 589832 | tf_op jit(solution)/shard_map/ppermute | solution.py:30
  54.6 6.3 %collective-permute-start.11 = (bf16[3,32,1024]{2,1,0:T(8,128)(2,1)S(1)}, bf16[3,32,1024]{2,1,0:T(8,128)(2,1)S(1)}, u32[]{:S(2)}, u32[]{:S(2)}) collective-permute-start(bf16[3,32,1024]{2,1,0:T(8,128)(2,1)S(1)} %collective-permute-done.9.refs_2_), channel_id=1, source_target_pairs={{0,128},{4,132},{8,136},{12,140},{16,156},{20,144},{24,148},{28,15... | collective-permute-start | bytes 589832 | tf_op jit(solution)/shard_map/ppermute | solution.py:30
  58.0 9.4 %collective-permute-start.16 = (bf16[128,1024]{1,0:T(8,128)(2,1)S(1)}, bf16[128,1024]{1,0:T(8,128)(2,1)S(1)}, u32[]{:S(2)}, u32[]{:S(2)}) collective-permute-start(bf16[128,1024]{1,0:T(8,128)(2,1)S(1)} %slice.9), channel_id=1, source_target_pairs={{0,32},{4,36},{8,40},{12,44},{16,48},{20,52},{24,56},{28,60},{32,6... | collective-permute-start | bytes 786440 | tf_op jit(solution)/shard_map/ppermute | solution.py:30
  58.2 9.3 %collective-permute-start.14 = (bf16[128,1024]{1,0:T(8,128)(2,1)S(1)}, bf16[128,1024]{1,0:T(8,128)(2,1)S(1)}, u32[]{:S(2)}, u32[]{:S(2)}) collective-permute-start(bf16[128,1024]{1,0:T(8,128)(2,1)S(1)} %slice.8), channel_id=1, source_target_pairs={{0,96},{4,100},{8,104},{12,108},{16,112},{20,116},{24,120},{28,124... | collective-permute-start | bytes 786440 | tf_op jit(solution)/shard_map/ppermute | solution.py:30
  60.9 6.5 %collective-permute-start.12 = (bf16[3,32,1024]{2,1,0:T(8,128)(2,1)S(1)}, bf16[3,32,1024]{2,1,0:T(8,128)(2,1)S(1)}, u32[]{:S(2)}, u32[]{:S(2)}) collective-permute-start(bf16[3,32,1024]{2,1,0:T(8,128)(2,1)S(1)} %collective-permute-done.10.refs_3_), channel_id=1, source_target_pairs={{0,128},{4,132},{8,136},{12,140},{16,156},{20,144},{24,148},{28,15... | collective-permute-start | bytes 589832 | tf_op jit(solution)/shard_map/ppermute | solution.py:30
  60.9 6.6 %collective-permute-start.17 = (bf16[3,32,1024]{2,1,0:T(8,128)(2,1)S(1)}, bf16[3,32,1024]{2,1,0:T(8,128)(2,1)S(1)}, u32[]{:S(2)}, u32[]{:S(2)}) collective-permute-start(bf16[3,32,1024]{2,1,0:T(8,128)(2,1)S(1)} %collective-permute-done.11.refs_0_), channel_id=1, source_target_pairs={{0,128},{4,132},{8,136},{12,140},{16,156},{20,144},{24,148},{28,15... | collective-permute-start | bytes 589832 | tf_op jit(solution)/shard_map/ppermute | solution.py:30
  63.8 9.2 %collective-permute-start.18 = (bf16[3,128,1024]{2,1,0:T(8,128)(2,1)S(1)}, bf16[3,128,1024]{2,1,0:T(8,128)(2,1)S(1)}, u32[]{:S(2)}, u32[]{:S(2)}) collective-permute-start(bf16[3,128,1024]{2,1,0:T(8,128)(2,1)S(1)} %join.2.refs_4_.refs_3_), channel_id=1, source_target_pairs={{0,16},{4,20},{8,24},{12,28},{16,0},{20,4},{24,8},{28,12},{32,48},... | collective-permute-start | bytes 2359304 | tf_op jit(solution)/shard_map/ppermute | solution.py:30
  67.6 5.4 %collective-permute-start.19 = (bf16[3,96,1024]{2,1,0:T(8,128)(2,1)S(1)}, bf16[3,96,1024]{2,1,0:T(8,128)(2,1)S(1)}, u32[]{:S(2)}, u32[]{:S(2)}) collective-permute-start(bf16[3,96,1024]{2,1,0:T(8,128)(2,1)S(1)} %join.3.refs_5_.refs_4_), channel_id=1, source_target_pairs={{0,16},{4,20},{8,24},{12,28},{16,0},{20,4},{24,8},{28,12},{32,48},... | collective-permute-start | bytes 1769480 | tf_op jit(solution)/shard_map/ppermute | solution.py:30
  73.6 8.8 %collective-permute-start.22 = (bf16[128,1024]{1,0:T(8,128)(2,1)S(1)}, bf16[128,1024]{1,0:T(8,128)(2,1)S(1)}, u32[]{:S(2)}, u32[]{:S(2)}) collective-permute-start(bf16[128,1024]{1,0:T(8,128)(2,1)S(1)} %get-tuple-element.51), channel_id=1, source_target_pairs={{0,32},{4,36},{8,40},{12,44},{16,48},{20,52},{24,56},{28,60},{32,6... | collective-permute-start | bytes 786440 | tf_op jit(solution)/shard_map/ppermute | solution.py:30
  73.7 8.7 %collective-permute-start.23 = (bf16[128,1024]{1,0:T(8,128)(2,1)S(1)}, bf16[128,1024]{1,0:T(8,128)(2,1)S(1)}, u32[]{:S(2)}, u32[]{:S(2)}) collective-permute-start(bf16[128,1024]{1,0:T(8,128)(2,1)S(1)} %get-tuple-element.52), channel_id=1, source_target_pairs={{0,96},{4,100},{8,104},{12,108},{16,112},{20,116},{24,120},{28,124... | collective-permute-start | bytes 786440 | tf_op jit(solution)/shard_map/ppermute | solution.py:30
  77.5 10.6 %collective-permute-start.20 = (bf16[128,1024]{1,0:T(8,128)(2,1)S(1)}, bf16[128,1024]{1,0:T(8,128)(2,1)S(1)}, u32[]{:S(2)}, u32[]{:S(2)}) collective-permute-start(bf16[128,1024]{1,0:T(8,128)(2,1)S(1)} %get-tuple-element.48), channel_id=1, source_target_pairs={{0,32},{4,36},{8,40},{12,44},{16,48},{20,52},{24,56},{28,60},{32,6... | collective-permute-start | bytes 786440 | tf_op jit(solution)/shard_map/ppermute | solution.py:30
  77.6 10.5 %collective-permute-start.21 = (bf16[128,1024]{1,0:T(8,128)(2,1)S(1)}, bf16[128,1024]{1,0:T(8,128)(2,1)S(1)}, u32[]{:S(2)}, u32[]{:S(2)}) collective-permute-start(bf16[128,1024]{1,0:T(8,128)(2,1)S(1)} %get-tuple-element.49), channel_id=1, source_target_pairs={{0,96},{4,100},{8,104},{12,108},{16,112},{20,116},{24,120},{28,124... | collective-permute-start | bytes 786440 | tf_op jit(solution)/shard_map/ppermute | solution.py:30
  82.6 11.1 %collective-permute-start.24 = (bf16[128,1024]{1,0:T(8,128)(2,1)S(1)}, bf16[128,1024]{1,0:T(8,128)(2,1)S(1)}, u32[]{:S(2)}, u32[]{:S(2)}) collective-permute-start(bf16[128,1024]{1,0:T(8,128)(2,1)S(1)} %get-tuple-element.53), channel_id=1, source_target_pairs={{0,32},{4,36},{8,40},{12,44},{16,48},{20,52},{24,56},{28,60},{32,6... | collective-permute-start | bytes 786440 | tf_op jit(solution)/shard_map/ppermute | solution.py:30
  82.6 11.0 %collective-permute-start.25 = (bf16[128,1024]{1,0:T(8,128)(2,1)S(1)}, bf16[128,1024]{1,0:T(8,128)(2,1)S(1)}, u32[]{:S(2)}, u32[]{:S(2)}) collective-permute-start(bf16[128,1024]{1,0:T(8,128)(2,1)S(1)} %get-tuple-element.54), channel_id=1, source_target_pairs={{0,96},{4,100},{8,104},{12,108},{16,112},{20,116},{24,120},{28,124... | collective-permute-start | bytes 786440 | tf_op jit(solution)/shard_map/ppermute | solution.py:30

commit v6 on v5

--- a/solution.py
+++ b/solution.py
@@ -12,8 +12,8 @@
 NZ = LZ * HZ
 F32 = jnp.float32
 BF16 = jnp.bfloat16
-STEPS = (2, 1, 3, 0)
-GROUPS = ((0, 1), (2, 3))
+STEPS = (1, 3, 2, 0)
+GROUPS = ((0,), (1,), (2,), (3,))
 DELTA_US, SUM_US, OWN_US = 0.0, 10.0, 10.0
 
 
@@ -72,7 +72,7 @@
 def delta_kernel(rates, keys, values, gate, up, down, *refs):
     groups = len(GROUPS)
     mine, other, old = refs[:groups], refs[groups : 2 * groups], refs[2 * groups]
-    old_turned, k_ref, v_ref, columns, turned, sems = refs[2 * groups + 1 :]
+    r_ref, old_turned, k_ref, v_ref, columns, turned, sems = refs[2 * groups + 1 :]
     x, zl, core = coordinates()
     units = gate.shape[2] // NX
     half = units // NC
@@ -85,6 +85,7 @@
         pltpu.make_async_copy(keys.at[early:], k_ref.at[early:], sems.at[3]),
         pltpu.make_async_copy(values, v_ref, sems.at[4]),
         pltpu.make_async_copy(down.at[0], columns.at[2], sems.at[5]),
+        pltpu.make_async_copy(rates, r_ref, sems.at[6]),
     ]
     for copy in copies:
         copy.start()
@@ -100,7 +101,8 @@
     )
     copies[4].wait()
     copies[5].wait()
-    k, v, r = k_ref[...], v_ref[...], rates[...]
+    copies[6].wait()
+    k, v, r = k_ref[...], v_ref[...], r_ref[...]
     back = contract(columns[2], v, 0, 1)
     s = jax.nn.sigmoid(gate_in)
     act = gate_in * s
@@ -135,16 +137,17 @@
     return pl.pallas_call(
         delta_kernel,
         name="deltas",
-        in_specs=[vmem] + [pl.BlockSpec(memory_space=pl.ANY)] * len(arrays),
+        in_specs=[pl.BlockSpec(memory_space=pltpu.HBM)] + [pl.BlockSpec(memory_space=pl.ANY)] * len(arrays),
         out_specs=[vmem] * len(out_shape),
         out_shape=out_shape,
         scratch_shapes=[
+            pltpu.VMEM((1, count), F32),
             pltpu.VMEM((units, width), F32),
             pltpu.VMEM((count, width), BF16),
             pltpu.VMEM((count, width), BF16),
             pltpu.VMEM((3, width, n), BF16),
             pltpu.VMEM((3, n, count), BF16),
-            pltpu.SemaphoreType.DMA((6,)),
+            pltpu.SemaphoreType.DMA((7,)),
         ],
         compiler_params=params(50),
         cost_estimate=cost(DELTA_US),
@@ -261,7 +264,8 @@
 
 def local(input_keys, input_values, token_rates, gate_weight, up_weight, down_weight, queries):
     arrays = (input_keys, input_values, gate_weight, up_weight, down_weight)
-    *parts, old = deltas(token_rates, arrays)
+    rates = pltpu.with_memory_space_constraint(token_rates, pltpu.HBM)
+    *parts, old = deltas(rates, arrays)
     chips = []
     for mine, other in zip(parts, parts[len(GROUPS) :]):
         chips += add_cores(mine, swap_core(other))

time: 94.7 us -> 92.9 us (0.981)
  waiting for transfers between devices: 28.6 us -> 26 us
  starting transfers between devices: 48.3 us -> 49.8 us
    ppermute x26 -> x28, waiting for transfers between devices: 28.6 us -> 26 us  [move(): return lax.ppermute(array, AXES, pairs)]
    ppermute x26 -> x28, starting transfers between devices: 48.3 us -> 49.8 us  [move(): return lax.ppermute(array, AXES, pairs)]
    pallas_call x14 -> x16, Pallas kernels: 7.04 us -> 7.05 us  [call(): pl.pallas_call(kernel, name=name, in_specs=[vmem] * len(operands), out_sp...]
  transfers between devices with their start and end apart: 26 -> 28, of which waited for: 12 -> 12; matrix products, arithmetic and copies ran while one was open for 0% -> 0% of each run, Pallas kernels for 6% -> 6%
where the time goes in v6:
time: 92.9 us; the launch traced here: 92.8 us
  starting transfers between devices  49.8 us (54%)
  waiting for transfers between devices  26 us (28%)
  Pallas kernels  16.8 us (18%)
    ppermute x28, starting transfers between devices, move(): return lax.ppermute(array, AXES, pairs)  49.8 us
    ppermute x28, waiting for transfers between devices, move(): return lax.ppermute(array, AXES, pairs)  26 us
    pallas_call x1, Pallas kernels, deltas(): pl.pallas_call(delta_kernel, name='deltas', in_specs=[pl.BlockSpec(memory...  9.78 us
    pallas_call x16, Pallas kernels, call(): pl.pallas_call(kernel, name=name, in_specs=[vmem] * len(operands), out_sp...  7.05 us
  transfers between devices with their start and end apart: 28, of which 12 were waited for; matrix products, arithmetic and copies ran while one was open for 0% of the time, Pallas kernels for 6%

profile of v6, /device:TPU:1, one launch (start us, length us, event | category | flops | bytes accessed | tf_op | source)
XLA Modules:
  0.0 92.8 jit_solution(4787392049355469536)
XLA Ops:
  0.0 9.8 %deltas.1 = (bf16[1,3,64,1024]{3,2,1,0:T(8,128)(2,1)S(1)}, bf16[1,3,64,1024]{3,2,1,0:T(8,128)(2,1)S(1)}, bf16[1,3,64,1024]{3,2,1,0:T(8,128)(2,1)S(1)}, bf16[1,3,...) custom-call(f32[1,1024]{1,0:T(1,128)} %rates.1, ...), custom_call_target="tpu_custom_call" | custom-call | flops 1 | bytes 1 | tf_op jit(solution)/shard_map/deltas/pallas_call | solution.py:137
  9.8 3.3 %collective-permute-start = (bf16[1,3,64,1024]{3,2,1,0:T(8,128)(2,1)S(1)}, bf16[1,3,64,1024]{3,2,1,0:T(8,128)(2,1)S(1)}, u32[]{:S(2)}, u32[]{:S(2)}) collective-permute-start(bf16[1,3,64,1024]{3,2,1,0:T(8,128)(2,1)S(1)} %get-tuple-element.31), channel_id=1, source_target_pairs={{0,16},{4,20},{8,24},{12,28},{16,0},{20,4},{24,8},{28,12},{32,48},... | collective-permute-start | bytes 1179656 | tf_op jit(solution)/shard_map/ppermute | solution.py:30
  13.1 0.1 collective-permute-start.2
  13.2 0.4 collective-permute-start.4
  13.6 0.1 collective-permute-start.6
  13.7 0.7 collective-permute-done.other
  14.5 0.1 add_cores.4
  14.6 1.2 %collective-permute-start.1 = (bf16[3,64,1024]{2,1,0:T(8,128)(2,1)S(1)}, bf16[3,64,1024]{2,1,0:T(8,128)(2,1)S(1)}, u32[]{:S(2)}, u32[]{:S(2)}) collective-permute-start(bf16[3,64,1024]{2,1,0:T(8,128)(2,1)S(1)} %add_cores.4), channel_id=1, source_target_pairs={{0,32},{4,36},{8,40},{12,44},{16,160},{20,164},{24,168},{28,172},{... | collective-permute-start | bytes 1179656 | tf_op jit(solution)/shard_map/ppermute | solution.py:30
  15.7 0.1 add_cores.5
  15.8 2.8 %collective-permute-start.3 = (bf16[3,64,1024]{2,1,0:T(8,128)(2,1)S(1)}, bf16[3,64,1024]{2,1,0:T(8,128)(2,1)S(1)}, u32[]{:S(2)}, u32[]{:S(2)}) collective-permute-start(bf16[3,64,1024]{2,1,0:T(8,128)(2,1)S(1)} %add_cores.5), channel_id=1, source_target_pairs={{0,96},{4,100},{8,104},{12,108},{16,224},{20,228},{24,232},{28,236... | collective-permute-start | bytes 1179656 | tf_op jit(solution)/shard_map/ppermute | solution.py:30
  18.7 0.0 collective-permute-done.4.other
  18.7 0.1 add_cores.6
  18.8 1.5 %collective-permute-start.5 = (bf16[3,64,1024]{2,1,0:T(8,128)(2,1)S(1)}, bf16[3,64,1024]{2,1,0:T(8,128)(2,1)S(1)}, u32[]{:S(2)}, u32[]{:S(2)}) collective-permute-start(bf16[3,64,1024]{2,1,0:T(8,128)(2,1)S(1)} %add_cores.6), channel_id=1, source_target_pairs={{0,64},{4,68},{8,72},{12,76},{16,192},{20,196},{24,200},{28,204},{... | collective-permute-start | bytes 1179656 | tf_op jit(solution)/shard_map/ppermute | solution.py:30
  20.3 0.0 collective-permute-done.6.other
  20.3 0.1 add_cores.7
  20.4 0.0 copy-start
  20.4 2.1 %collective-permute-start.7 = (bf16[3,64,1024]{2,1,0:T(8,128)(2,1)S(1)}, bf16[3,64,1024]{2,1,0:T(8,128)(2,1)S(1)}, u32[]{:S(2)}, u32[]{:S(2)}) collective-permute-start(bf16[3,64,1024]{2,1,0:T(8,128)(2,1)S(1)} %add_cores.7), channel_id=1, source_target_pairs={{0,0},{4,4},{8,8},{12,12},{16,128},{20,132},{24,136},{28,140},{32,... | collective-permute-start | bytes 1179656 | tf_op jit(solution)/shard_map/ppermute | solution.py:30
  22.4 1.6 %collective-permute-done.1.refs_0_ = bf16[3,64,1024]{2,1,0:T(8,128)(2,1)S(1)} collective-permute-done((bf16[3,64,1024]{2,1,0:T(8,128)(2,1)S(1)}, bf16[3,64,1024]{2,1,0:T(8,128)(2,1)S(1)}, u32[]{:S(2)}, u32[]{:S(2)}) %collective-permute-start.1) | collective-permute-done | bytes 393248 | tf_op jit(solution)/shard_map/ppermute | solution.py:30
  24.1 2.5 %collective-permute-done.3.refs_1_ = bf16[3,64,1024]{2,1,0:T(8,128)(2,1)S(1)} collective-permute-done((bf16[3,64,1024]{2,1,0:T(8,128)(2,1)S(1)}, bf16[3,64,1024]{2,1,0:T(8,128)(2,1)S(1)}, u32[]{:S(2)}, u32[]{:S(2)}) %collective-permute-start.3) | collective-permute-done | bytes 393248 | tf_op jit(solution)/shard_map/ppermute | solution.py:30
  26.5 5.9 %collective-permute-done.5.refs_2_ = bf16[3,64,1024]{2,1,0:T(8,128)(2,1)S(1)} collective-permute-done((bf16[3,64,1024]{2,1,0:T(8,128)(2,1)S(1)}, bf16[3,64,1024]{2,1,0:T(8,128)(2,1)S(1)}, u32[]{:S(2)}, u32[]{:S(2)}) %collective-permute-start.5) | collective-permute-done | bytes 393248 | tf_op jit(solution)/shard_map/ppermute | solution.py:30
  32.5 1.6 %collective-permute-done.7.refs_3_ = bf16[3,64,1024]{2,1,0:T(8,128)(2,1)S(1)} collective-permute-done((bf16[3,64,1024]{2,1,0:T(8,128)(2,1)S(1)}, bf16[3,64,1024]{2,1,0:T(8,128)(2,1)S(1)}, u32[]{:S(2)}, u32[]{:S(2)}) %collective-permute-start.7) | collective-permute-done | bytes 393248 | tf_op jit(solution)/shard_map/ppermute | solution.py:30
  34.1 0.2 sum_chips.1.mine
  34.3 2.8 %collective-permute-start.8 = (bf16[3,64,1024]{2,1,0:T(8,128)(2,1)S(1)}, bf16[3,64,1024]{2,1,0:T(8,128)(2,1)S(1)}, u32[]{:S(2)}, u32[]{:S(2)}) collective-permute-start(bf16[3,64,1024]{2,1,0:T(8,128)(2,1)S(1)} %sum_chips.1.mine), channel_id=1, source_target_pairs={{0,16},{4,20},{8,24},{12,28},{16,0},{20,4},{24,8},{28,12},{32,48},... | collective-permute-start | bytes 1179656 | tf_op jit(solution)/shard_map/ppermute | solution.py:30
  37.1 0.8 collective-permute-start.17
  37.9 2.4 %collective-permute-start.15 = (bf16[256,1024]{1,0:T(8,128)(2,1)S(1)}, bf16[256,1024]{1,0:T(8,128)(2,1)S(1)}, u32[]{:S(2)}, u32[]{:S(2)}) collective-permute-start(bf16[256,1024]{1,0:T(8,128)(2,1)S(1)} %copy-done), channel_id=1, source_target_pairs={{0,96},{4,100},{8,104},{12,108},{16,112},{20,116},{24,120},{28,124... | collective-permute-start | bytes 1572872 | tf_op jit(solution)/shard_map/ppermute | solution.py:30
  40.3 0.4 renorm.1
  40.6 3.6 %collective-permute-start.9 = (bf16[3,32,1024]{2,1,0:T(8,128)(2,1)S(1)}, bf16[3,32,1024]{2,1,0:T(8,128)(2,1)S(1)}, u32[]{:S(2)}, u32[]{:S(2)}) collective-permute-start(bf16[3,32,1024]{2,1,0:T(8,128)(2,1)S(1)} %get-tuple-element.42.refs_2_.refs_1_), channel_id=1, source_target_pairs={{0,128},{4,132},{8,136},{12,140},{16,156},{20,144},{24,148},{28,15... | collective-permute-start | bytes 589832 | tf_op jit(solution)/shard_map/ppermute | solution.py:30
  44.2 1.6 %collective-permute-start.10 = (bf16[3,32,1024]{2,1,0:T(8,128)(2,1)S(1)}, bf16[3,32,1024]{2,1,0:T(8,128)(2,1)S(1)}, u32[]{:S(2)}, u32[]{:S(2)}) collective-permute-start(bf16[3,32,1024]{2,1,0:T(8,128)(2,1)S(1)} %get-tuple-element.43.refs_3_.refs_2_), channel_id=1, source_target_pairs={{0,128},{4,132},{8,136},{12,140},{16,156},{20,144},{24,148},{28,15... | collective-permute-start | bytes 589832 | tf_op jit(solution)/shard_map/ppermute | solution.py:30
  45.8 1.1 %collective-permute-done.9.refs_0_ = bf16[3,32,1024]{2,1,0:T(8,128)(2,1)S(1)} collective-permute-done((bf16[3,32,1024]{2,1,0:T(8,128)(2,1)S(1)}, bf16[3,32,1024]{2,1,0:T(8,128)(2,1)S(1)}, u32[]{:S(2)}, u32[]{:S(2)}) %collective-permute-start.9) | collective-permute-done | bytes 196640 | tf_op jit(solution)/shard_map/ppermute | solution.py:30
  46.9 3.4 %collective-permute-start.11 = (bf16[3,32,1024]{2,1,0:T(8,128)(2,1)S(1)}, bf16[3,32,1024]{2,1,0:T(8,128)(2,1)S(1)}, u32[]{:S(2)}, u32[]{:S(2)}) collective-permute-start(bf16[3,32,1024]{2,1,0:T(8,128)(2,1)S(1)} %collective-permute-done.9.refs_0_), channel_id=1, source_target_pairs={{0,128},{4,132},{8,136},{12,140},{16,156},{20,144},{24,148},{28,15... | collective-permute-start | bytes 589832 | tf_op jit(solution)/shard_map/ppermute | solution.py:30
  50.3 0.0 collective-permute-done.10.refs_1_
  50.3 2.1 %collective-permute-start.12 = (bf16[3,32,1024]{2,1,0:T(8,128)(2,1)S(1)}, bf16[3,32,1024]{2,1,0:T(8,128)(2,1)S(1)}, u32[]{:S(2)}, u32[]{:S(2)}) collective-permute-start(bf16[3,32,1024]{2,1,0:T(8,128)(2,1)S(1)} %collective-permute-done.10.refs_1_), channel_id=1, source_target_pairs={{0,128},{4,132},{8,136},{12,140},{16,156},{20,144},{24,148},{28,15... | collective-permute-start | bytes 589832 | tf_op jit(solution)/shard_map/ppermute | solution.py:30
  52.4 0.5 collective-permute-done.11.refs_2_
  52.9 3.4 %collective-permute-start.13 = (bf16[3,32,1024]{2,1,0:T(8,128)(2,1)S(1)}, bf16[3,32,1024]{2,1,0:T(8,128)(2,1)S(1)}, u32[]{:S(2)}, u32[]{:S(2)}) collective-permute-start(bf16[3,32,1024]{2,1,0:T(8,128)(2,1)S(1)} %collective-permute-done.11.refs_2_), channel_id=1, source_target_pairs={{0,128},{4,132},{8,136},{12,140},{16,156},{20,144},{24,148},{28,15... | collective-permute-start | bytes 589832 | tf_op jit(solution)/shard_map/ppermute | solution.py:30
  56.3 0.0 collective-permute-done.17.refs_1_
  56.3 0.1 collective-permute-start.18
  56.4 0.0 collective-permute-done.15.refs_0_
  56.4 2.7 %collective-permute-start.16 = (bf16[128,1024]{1,0:T(8,128)(2,1)S(1)}, bf16[128,1024]{1,0:T(8,128)(2,1)S(1)}, u32[]{:S(2)}, u32[]{:S(2)}) collective-permute-start(bf16[128,1024]{1,0:T(8,128)(2,1)S(1)} %slice.8), channel_id=1, source_target_pairs={{0,96},{4,100},{8,104},{12,108},{16,112},{20,116},{24,120},{28,124... | collective-permute-start | bytes 786440 | tf_op jit(solution)/shard_map/ppermute | solution.py:30
  59.2 0.0 collective-permute-start.14
  59.2 2.8 %collective-permute-start.19 = (bf16[3,32,1024]{2,1,0:T(8,128)(2,1)S(1)}, bf16[3,32,1024]{2,1,0:T(8,128)(2,1)S(1)}, u32[]{:S(2)}, u32[]{:S(2)}) collective-permute-start(bf16[3,32,1024]{2,1,0:T(8,128)(2,1)S(1)} %collective-permute-done.13.refs_0_), channel_id=1, source_target_pairs={{0,128},{4,132},{8,136},{12,140},{16,156},{20,144},{24,148},{28,15... | collective-permute-start | bytes 589832 | tf_op jit(solution)/shard_map/ppermute | solution.py:30
  62.0 0.1 join.2.refs_4_.refs_3_
  62.1 0.7 collective-permute-start.20
  62.7 3.0 %collective-permute-done.18.refs_1_ = bf16[128,1024]{1,0:T(8,128)(2,1)S(1)} collective-permute-done((bf16[128,1024]{1,0:T(8,128)(2,1)S(1)}, bf16[128,1024]{1,0:T(8,128)(2,1)S(1)}, u32[]{:S(2)}, u32[]{:S(2)}) %collective-permute-start.18) | collective-permute-done | bytes 262176 | tf_op jit(solution)/shard_map/ppermute | solution.py:30
  65.7 0.0 collective-permute-done.16.refs_0_
  65.7 0.1 collective-permute-done.19.refs_2_
  65.8 3.8 %collective-permute-start.21 = (bf16[3,96,1024]{2,1,0:T(8,128)(2,1)S(1)}, bf16[3,96,1024]{2,1,0:T(8,128)(2,1)S(1)}, u32[]{:S(2)}, u32[]{:S(2)}) collective-permute-start(bf16[3,96,1024]{2,1,0:T(8,128)(2,1)S(1)} %join.3.refs_5_.refs_4_), channel_id=1, source_target_pairs={{0,16},{4,20},{8,24},{12,28},{16,0},{20,4},{24,8},{28,12},{32,48},... | collective-permute-start | bytes 1769480 | tf_op jit(solution)/shard_map/ppermute | solution.py:30
  69.6 1.0 %render_rows.5.refs_4_ = f32[256,1024]{1,0:T(8,128)S(1)} custom-call(bf16[128,1024]{1,0:T(8,128)(2,1)S(1)} %collective-permute-done.16.refs_0_, bf16[128,1024]{1,0:T(8,128)(2,1)S(1)} %collective-permute-done.18.refs_1_, bf16[3,32,1024]{2,1,0:T(8,128)(2,1)S(1)} %get-tuple-element.42.refs_2_.refs_1_, ...), custom_call_target="tpu_custom_call" | custom-call | flops 1 | bytes 1 | tf_op jit(solution)/shard_map/render_rows/pallas_call | solution.py:159
  70.6 0.6 collective-permute-done.21.refs_6_.refs_7_.refs_3_
  71.2 0.7 render_rows.9
  71.9 0.1 collective-permute-start.24
  72.0 2.7 %collective-permute-start.25 = (bf16[128,1024]{1,0:T(8,128)(2,1)S(1)}, bf16[128,1024]{1,0:T(8,128)(2,1)S(1)}, u32[]{:S(2)}, u32[]{:S(2)}) collective-permute-start(bf16[128,1024]{1,0:T(8,128)(2,1)S(1)} %get-tuple-element.52), channel_id=1, source_target_pairs={{0,96},{4,100},{8,104},{12,108},{16,112},{20,116},{24,120},{28,124... | collective-permute-start | bytes 786440 | tf_op jit(solution)/shard_map/ppermute | solution.py:30
  74.7 1.1 %render_rows.7 = (bf16[128,1024]{1,0:T(8,128)(2,1)S(1)}, bf16[128,1024]{1,0:T(8,128)(2,1)S(1)}) custom-call(bf16[256,1024]{1,0:T(8,128)(2,1)S(1)} %collective-permute-done.15.refs_0_, bf16[256,1024]{1,0:T(8,128)(2,1)S(1)} %collective-permute-done.17.refs_1_, bf16[3,32,1024]{2,1,0:T(8,128)(2,1)S(1)} %get-tuple-element.42.refs_2_.refs_1_, ...), custom_call_target="tpu_custom_call" | custom-call | flops 1 | bytes 1 | tf_op jit(solution)/shard_map/render_rows/pallas_call | solution.py:159
  75.8 0.1 collective-permute-start.22
  75.8 2.7 %collective-permute-start.23 = (bf16[128,1024]{1,0:T(8,128)(2,1)S(1)}, bf16[128,1024]{1,0:T(8,128)(2,1)S(1)}, u32[]{:S(2)}, u32[]{:S(2)}) collective-permute-start(bf16[128,1024]{1,0:T(8,128)(2,1)S(1)} %get-tuple-element.49), channel_id=1, source_target_pairs={{0,96},{4,100},{8,104},{12,108},{16,112},{20,116},{24,120},{28,124... | collective-permute-start | bytes 786440 | tf_op jit(solution)/shard_map/ppermute | solution.py:30
  78.5 1.1 %render_rows.8.mid = f32[256,1024]{1,0:T(8,128)S(1)} custom-call(bf16[256,1024]{1,0:T(8,128)(2,1)S(1)} %collective-permute-done.15.refs_0_, bf16[256,1024]{1,0:T(8,128)(2,1)S(1)} %collective-permute-done.17.refs_1_, bf16[3,32,1024]{2,1,0:T(8,128)(2,1)S(1)} %get-tuple-element.42.refs_2_.refs_1_, bf16[3,32,1024]{2,1,0:T(8,128)(2,1)S(1)} %get-tuple-element.43.refs_3_.refs_2_, ...), custom_call_target="tpu_custom_call" | custom-call | flops 1 | bytes 1 | tf_op jit(solution)/shard_map/render_rows/pallas_call | solution.py:159
  79.6 1.1 %render_rows.6.own = f32[256,1024]{1,0:T(8,128)S(1)} custom-call(bf16[256,1024]{1,0:T(8,128)(2,1)S(1)} %copy-done, bf16[3,32,1024]{2,1,0:T(8,128)(2,1)S(1)} %get-tuple-element.42.refs_2_.refs_1_, bf16[3,32,1024]{2,1,0:T(8,128)(2,1)S(1)} %get-tuple-element.43.refs_3_.refs_2_, bf16[3,128,1024]{2,1,0:T(8,128)(2,1)S(1)} %join.2.refs_4_.refs_3_, ...), custom_call_target="tpu_custom_call" | custom-call | flops 1 | bytes 1 | tf_op jit(solution)/shard_map/render_rows/pallas_call | solution.py:159
  80.7 0.0 collective-permute-done.24.relay_left
  80.7 0.1 merge.1
  80.8 0.1 collective-permute-start.26
  80.9 2.7 %collective-permute-start.27 = (bf16[128,1024]{1,0:T(8,128)(2,1)S(1)}, bf16[128,1024]{1,0:T(8,128)(2,1)S(1)}, u32[]{:S(2)}, u32[]{:S(2)}) collective-permute-start(bf16[128,1024]{1,0:T(8,128)(2,1)S(1)} %get-tuple-element.54), channel_id=1, source_target_pairs={{0,96},{4,100},{8,104},{12,108},{16,112},{20,116},{24,120},{28,124... | collective-permute-start | bytes 786440 | tf_op jit(solution)/shard_map/ppermute | solution.py:30
  83.6 2.8 %collective-permute-done.22.from_left = bf16[128,1024]{1,0:T(8,128)(2,1)S(1)} collective-permute-done((bf16[128,1024]{1,0:T(8,128)(2,1)S(1)}, bf16[128,1024]{1,0:T(8,128)(2,1)S(1)}, u32[]{:S(2)}, u32[]{:S(2)}) %collective-permute-start.22) | collective-permute-done | bytes 262176 | tf_op jit(solution)/shard_map/ppermute | solution.py:30
  86.3 0.1 own.1
  86.4 5.5 %collective-permute-done.26.last_left = bf16[128,1024]{1,0:T(8,128)(2,1)S(1)} collective-permute-done((bf16[128,1024]{1,0:T(8,128)(2,1)S(1)}, bf16[128,1024]{1,0:T(8,128)(2,1)S(1)}, u32[]{:S(2)}, u32[]{:S(2)}) %collective-permute-start.26) | collective-permute-done | bytes 262176 | tf_op jit(solution)/shard_map/ppermute | solution.py:30
  92.0 0.9 total.1
  (13 shorter events, 0.1 us)
Async XLA Ops:
  9.8 4.7 %collective-permute-start = (bf16[1,3,64,1024]{3,2,1,0:T(8,128)(2,1)S(1)}, bf16[1,3,64,1024]{3,2,1,0:T(8,128)(2,1)S(1)}, u32[]{:S(2)}, u32[]{:S(2)}) collective-permute-start(bf16[1,3,64,1024]{3,2,1,0:T(8,128)(2,1)S(1)} %get-tuple-element.31), channel_id=1, source_target_pairs={{0,16},{4,20},{8,24},{12,28},{16,0},{20,4},{24,8},{28,12},{32,48},... | collective-permute-start | bytes 1179656 | tf_op jit(solution)/shard_map/ppermute | solution.py:30
  13.1 2.6 %collective-permute-start.2 = (bf16[1,3,64,1024]{3,2,1,0:T(8,128)(2,1)S(1)}, bf16[1,3,64,1024]{3,2,1,0:T(8,128)(2,1)S(1)}, u32[]{:S(2)}, u32[]{:S(2)}) collective-permute-start(bf16[1,3,64,1024]{3,2,1,0:T(8,128)(2,1)S(1)} %get-tuple-element.33), channel_id=1, source_target_pairs={{0,16},{4,20},{8,24},{12,28},{16,0},{20,4},{24,8},{28,12},{32,48},... | collective-permute-start | bytes 1179656 | tf_op jit(solution)/shard_map/ppermute | solution.py:30
  13.2 5.5 %collective-permute-start.4 = (bf16[1,3,64,1024]{3,2,1,0:T(8,128)(2,1)S(1)}, bf16[1,3,64,1024]{3,2,1,0:T(8,128)(2,1)S(1)}, u32[]{:S(2)}, u32[]{:S(2)}) collective-permute-start(bf16[1,3,64,1024]{3,2,1,0:T(8,128)(2,1)S(1)} %get-tuple-element.39), channel_id=1, source_target_pairs={{0,16},{4,20},{8,24},{12,28},{16,0},{20,4},{24,8},{28,12},{32,48},... | collective-permute-start | bytes 1179656 | tf_op jit(solution)/shard_map/ppermute | solution.py:30
  13.6 6.6 %collective-permute-start.6 = (bf16[1,3,64,1024]{3,2,1,0:T(8,128)(2,1)S(1)}, bf16[1,3,64,1024]{3,2,1,0:T(8,128)(2,1)S(1)}, u32[]{:S(2)}, u32[]{:S(2)}) collective-permute-start(bf16[1,3,64,1024]{3,2,1,0:T(8,128)(2,1)S(1)} %get-tuple-element.41), channel_id=1, source_target_pairs={{0,16},{4,20},{8,24},{12,28},{16,0},{20,4},{24,8},{28,12},{32,48},... | collective-permute-start | bytes 1179656 | tf_op jit(solution)/shard_map/ppermute | solution.py:30
  14.6 9.5 %collective-permute-start.1 = (bf16[3,64,1024]{2,1,0:T(8,128)(2,1)S(1)}, bf16[3,64,1024]{2,1,0:T(8,128)(2,1)S(1)}, u32[]{:S(2)}, u32[]{:S(2)}) collective-permute-start(bf16[3,64,1024]{2,1,0:T(8,128)(2,1)S(1)} %add_cores.4), channel_id=1, source_target_pairs={{0,32},{4,36},{8,40},{12,44},{16,160},{20,164},{24,168},{28,172},{... | collective-permute-start | bytes 1179656 | tf_op jit(solution)/shard_map/ppermute | solution.py:30
  15.8 10.7 %collective-permute-start.3 = (bf16[3,64,1024]{2,1,0:T(8,128)(2,1)S(1)}, bf16[3,64,1024]{2,1,0:T(8,128)(2,1)S(1)}, u32[]{:S(2)}, u32[]{:S(2)}) collective-permute-start(bf16[3,64,1024]{2,1,0:T(8,128)(2,1)S(1)} %add_cores.5), channel_id=1, source_target_pairs={{0,96},{4,100},{8,104},{12,108},{16,224},{20,228},{24,232},{28,236... | collective-permute-start | bytes 1179656 | tf_op jit(solution)/shard_map/ppermute | solution.py:30
  18.8 13.7 %collective-permute-start.5 = (bf16[3,64,1024]{2,1,0:T(8,128)(2,1)S(1)}, bf16[3,64,1024]{2,1,0:T(8,128)(2,1)S(1)}, u32[]{:S(2)}, u32[]{:S(2)}) collective-permute-start(bf16[3,64,1024]{2,1,0:T(8,128)(2,1)S(1)} %add_cores.6), channel_id=1, source_target_pairs={{0,64},{4,68},{8,72},{12,76},{16,192},{20,196},{24,200},{28,204},{... | collective-permute-start | bytes 1179656 | tf_op jit(solution)/shard_map/ppermute | solution.py:30
  20.4 16.8 %copy-start = (bf16[256,1024]{1,0:T(8,128)(2,1)S(1)}, bf16[256,1024]{1,0:T(8,128)(2,1)}, u32[]{:S(2)}) copy-start(bf16[256,1024]{1,0:T(8,128)(2,1)} %refs_0_) | copy-start | bytes 1572868
  20.4 13.7 %collective-permute-start.7 = (bf16[3,64,1024]{2,1,0:T(8,128)(2,1)S(1)}, bf16[3,64,1024]{2,1,0:T(8,128)(2,1)S(1)}, u32[]{:S(2)}, u32[]{:S(2)}) collective-permute-start(bf16[3,64,1024]{2,1,0:T(8,128)(2,1)S(1)} %add_cores.7), channel_id=1, source_target_pairs={{0,0},{4,4},{8,8},{12,12},{16,128},{20,132},{24,136},{28,140},{32,... | collective-permute-start | bytes 1179656 | tf_op jit(solution)/shard_map/ppermute | solution.py:30
  34.3 5.9 %collective-permute-start.8 = (bf16[3,64,1024]{2,1,0:T(8,128)(2,1)S(1)}, bf16[3,64,1024]{2,1,0:T(8,128)(2,1)S(1)}, u32[]{:S(2)}, u32[]{:S(2)}) collective-permute-start(bf16[3,64,1024]{2,1,0:T(8,128)(2,1)S(1)} %sum_chips.1.mine), channel_id=1, source_target_pairs={{0,16},{4,20},{8,24},{12,28},{16,0},{20,4},{24,8},{28,12},{32,48},... | collective-permute-start | bytes 1179656 | tf_op jit(solution)/shard_map/ppermute | solution.py:30
  37.1 19.1 %collective-permute-start.17 = (bf16[256,1024]{1,0:T(8,128)(2,1)S(1)}, bf16[256,1024]{1,0:T(8,128)(2,1)S(1)}, u32[]{:S(2)}, u32[]{:S(2)}) collective-permute-start(bf16[256,1024]{1,0:T(8,128)(2,1)S(1)} %copy-done), channel_id=1, source_target_pairs={{0,32},{4,36},{8,40},{12,44},{16,48},{20,52},{24,56},{28,60},{32,6... | collective-permute-start | bytes 1572872 | tf_op jit(solution)/shard_map/ppermute | solution.py:30
  37.9 18.5 %collective-permute-start.15 = (bf16[256,1024]{1,0:T(8,128)(2,1)S(1)}, bf16[256,1024]{1,0:T(8,128)(2,1)S(1)}, u32[]{:S(2)}, u32[]{:S(2)}) collective-permute-start(bf16[256,1024]{1,0:T(8,128)(2,1)S(1)} %copy-done), channel_id=1, source_target_pairs={{0,96},{4,100},{8,104},{12,108},{16,112},{20,116},{24,120},{28,124... | collective-permute-start | bytes 1572872 | tf_op jit(solution)/shard_map/ppermute | solution.py:30
  40.6 6.2 %collective-permute-start.9 = (bf16[3,32,1024]{2,1,0:T(8,128)(2,1)S(1)}, bf16[3,32,1024]{2,1,0:T(8,128)(2,1)S(1)}, u32[]{:S(2)}, u32[]{:S(2)}) collective-permute-start(bf16[3,32,1024]{2,1,0:T(8,128)(2,1)S(1)} %get-tuple-element.42.refs_2_.refs_1_), channel_id=1, source_target_pairs={{0,128},{4,132},{8,136},{12,140},{16,156},{20,144},{24,148},{28,15... | collective-permute-start | bytes 589832 | tf_op jit(solution)/shard_map/ppermute | solution.py:30
  44.2 6.0 %collective-permute-start.10 = (bf16[3,32,1024]{2,1,0:T(8,128)(2,1)S(1)}, bf16[3,32,1024]{2,1,0:T(8,128)(2,1)S(1)}, u32[]{:S(2)}, u32[]{:S(2)}) collective-permute-start(bf16[3,32,1024]{2,1,0:T(8,128)(2,1)S(1)} %get-tuple-element.43.refs_3_.refs_2_), channel_id=1, source_target_pairs={{0,128},{4,132},{8,136},{12,140},{16,156},{20,144},{24,148},{28,15... | collective-permute-start | bytes 589832 | tf_op jit(solution)/shard_map/ppermute | solution.py:30
  46.9 6.0 %collective-permute-start.11 = (bf16[3,32,1024]{2,1,0:T(8,128)(2,1)S(1)}, bf16[3,32,1024]{2,1,0:T(8,128)(2,1)S(1)}, u32[]{:S(2)}, u32[]{:S(2)}) collective-permute-start(bf16[3,32,1024]{2,1,0:T(8,128)(2,1)S(1)} %collective-permute-done.9.refs_0_), channel_id=1, source_target_pairs={{0,128},{4,132},{8,136},{12,140},{16,156},{20,144},{24,148},{28,15... | collective-permute-start | bytes 589832 | tf_op jit(solution)/shard_map/ppermute | solution.py:30
  50.3 8.9 %collective-permute-start.12 = (bf16[3,32,1024]{2,1,0:T(8,128)(2,1)S(1)}, bf16[3,32,1024]{2,1,0:T(8,128)(2,1)S(1)}, u32[]{:S(2)}, u32[]{:S(2)}) collective-permute-start(bf16[3,32,1024]{2,1,0:T(8,128)(2,1)S(1)} %collective-permute-done.10.refs_1_), channel_id=1, source_target_pairs={{0,128},{4,132},{8,136},{12,140},{16,156},{20,144},{24,148},{28,15... | collective-permute-start | bytes 589832 | tf_op jit(solution)/shard_map/ppermute | solution.py:30
  52.9 6.3 %collective-permute-start.13 = (bf16[3,32,1024]{2,1,0:T(8,128)(2,1)S(1)}, bf16[3,32,1024]{2,1,0:T(8,128)(2,1)S(1)}, u32[]{:S(2)}, u32[]{:S(2)}) collective-permute-start(bf16[3,32,1024]{2,1,0:T(8,128)(2,1)S(1)} %collective-permute-done.11.refs_2_), channel_id=1, source_target_pairs={{0,128},{4,132},{8,136},{12,140},{16,156},{20,144},{24,148},{28,15... | collective-permute-start | bytes 589832 | tf_op jit(solution)/shard_map/ppermute | solution.py:30
  56.3 9.4 %collective-permute-start.18 = (bf16[128,1024]{1,0:T(8,128)(2,1)S(1)}, bf16[128,1024]{1,0:T(8,128)(2,1)S(1)}, u32[]{:S(2)}, u32[]{:S(2)}) collective-permute-start(bf16[128,1024]{1,0:T(8,128)(2,1)S(1)} %slice.9), channel_id=1, source_target_pairs={{0,32},{4,36},{8,40},{12,44},{16,48},{20,52},{24,56},{28,60},{32,6... | collective-permute-start | bytes 786440 | tf_op jit(solution)/shard_map/ppermute | solution.py:30
  56.4 9.3 %collective-permute-start.16 = (bf16[128,1024]{1,0:T(8,128)(2,1)S(1)}, bf16[128,1024]{1,0:T(8,128)(2,1)S(1)}, u32[]{:S(2)}, u32[]{:S(2)}) collective-permute-start(bf16[128,1024]{1,0:T(8,128)(2,1)S(1)} %slice.8), channel_id=1, source_target_pairs={{0,96},{4,100},{8,104},{12,108},{16,112},{20,116},{24,120},{28,124... | collective-permute-start | bytes 786440 | tf_op jit(solution)/shard_map/ppermute | solution.py:30
  59.2 6.5 %collective-permute-start.14 = (bf16[3,32,1024]{2,1,0:T(8,128)(2,1)S(1)}, bf16[3,32,1024]{2,1,0:T(8,128)(2,1)S(1)}, u32[]{:S(2)}, u32[]{:S(2)}) collective-permute-start(bf16[3,32,1024]{2,1,0:T(8,128)(2,1)S(1)} %collective-permute-done.12.refs_3_), channel_id=1, source_target_pairs={{0,128},{4,132},{8,136},{12,140},{16,156},{20,144},{24,148},{28,15... | collective-permute-start | bytes 589832 | tf_op jit(solution)/shard_map/ppermute | solution.py:30
  59.2 6.6 %collective-permute-start.19 = (bf16[3,32,1024]{2,1,0:T(8,128)(2,1)S(1)}, bf16[3,32,1024]{2,1,0:T(8,128)(2,1)S(1)}, u32[]{:S(2)}, u32[]{:S(2)}) collective-permute-start(bf16[3,32,1024]{2,1,0:T(8,128)(2,1)S(1)} %collective-permute-done.13.refs_0_), channel_id=1, source_target_pairs={{0,128},{4,132},{8,136},{12,140},{16,156},{20,144},{24,148},{28,15... | collective-permute-start | bytes 589832 | tf_op jit(solution)/shard_map/ppermute | solution.py:30
  62.1 9.2 %collective-permute-start.20 = (bf16[3,128,1024]{2,1,0:T(8,128)(2,1)S(1)}, bf16[3,128,1024]{2,1,0:T(8,128)(2,1)S(1)}, u32[]{:S(2)}, u32[]{:S(2)}) collective-permute-start(bf16[3,128,1024]{2,1,0:T(8,128)(2,1)S(1)} %join.2.refs_4_.refs_3_), channel_id=1, source_target_pairs={{0,16},{4,20},{8,24},{12,28},{16,0},{20,4},{24,8},{28,12},{32,48},... | collective-permute-start | bytes 2359304 | tf_op jit(solution)/shard_map/ppermute | solution.py:30
  65.8 5.4 %collective-permute-start.21 = (bf16[3,96,1024]{2,1,0:T(8,128)(2,1)S(1)}, bf16[3,96,1024]{2,1,0:T(8,128)(2,1)S(1)}, u32[]{:S(2)}, u32[]{:S(2)}) collective-permute-start(bf16[3,96,1024]{2,1,0:T(8,128)(2,1)S(1)} %join.3.refs_5_.refs_4_), channel_id=1, source_target_pairs={{0,16},{4,20},{8,24},{12,28},{16,0},{20,4},{24,8},{28,12},{32,48},... | collective-permute-start | bytes 1769480 | tf_op jit(solution)/shard_map/ppermute | solution.py:30
  71.9 8.8 %collective-permute-start.24 = (bf16[128,1024]{1,0:T(8,128)(2,1)S(1)}, bf16[128,1024]{1,0:T(8,128)(2,1)S(1)}, u32[]{:S(2)}, u32[]{:S(2)}) collective-permute-start(bf16[128,1024]{1,0:T(8,128)(2,1)S(1)} %get-tuple-element.51), channel_id=1, source_target_pairs={{0,32},{4,36},{8,40},{12,44},{16,48},{20,52},{24,56},{28,60},{32,6... | collective-permute-start | bytes 786440 | tf_op jit(solution)/shard_map/ppermute | solution.py:30
  72.0 8.7 %collective-permute-start.25 = (bf16[128,1024]{1,0:T(8,128)(2,1)S(1)}, bf16[128,1024]{1,0:T(8,128)(2,1)S(1)}, u32[]{:S(2)}, u32[]{:S(2)}) collective-permute-start(bf16[128,1024]{1,0:T(8,128)(2,1)S(1)} %get-tuple-element.52), channel_id=1, source_target_pairs={{0,96},{4,100},{8,104},{12,108},{16,112},{20,116},{24,120},{28,124... | collective-permute-start | bytes 786440 | tf_op jit(solution)/shard_map/ppermute | solution.py:30
  75.8 10.6 %collective-permute-start.22 = (bf16[128,1024]{1,0:T(8,128)(2,1)S(1)}, bf16[128,1024]{1,0:T(8,128)(2,1)S(1)}, u32[]{:S(2)}, u32[]{:S(2)}) collective-permute-start(bf16[128,1024]{1,0:T(8,128)(2,1)S(1)} %get-tuple-element.48), channel_id=1, source_target_pairs={{0,32},{4,36},{8,40},{12,44},{16,48},{20,52},{24,56},{28,60},{32,6... | collective-permute-start | bytes 786440 | tf_op jit(solution)/shard_map/ppermute | solution.py:30
  75.8 10.5 %collective-permute-start.23 = (bf16[128,1024]{1,0:T(8,128)(2,1)S(1)}, bf16[128,1024]{1,0:T(8,128)(2,1)S(1)}, u32[]{:S(2)}, u32[]{:S(2)}) collective-permute-start(bf16[128,1024]{1,0:T(8,128)(2,1)S(1)} %get-tuple-element.49), channel_id=1, source_target_pairs={{0,96},{4,100},{8,104},{12,108},{16,112},{20,116},{24,120},{28,124... | collective-permute-start | bytes 786440 | tf_op jit(solution)/shard_map/ppermute | solution.py:30
  80.8 11.1 %collective-permute-start.26 = (bf16[128,1024]{1,0:T(8,128)(2,1)S(1)}, bf16[128,1024]{1,0:T(8,128)(2,1)S(1)}, u32[]{:S(2)}, u32[]{:S(2)}) collective-permute-start(bf16[128,1024]{1,0:T(8,128)(2,1)S(1)} %get-tuple-element.53), channel_id=1, source_target_pairs={{0,32},{4,36},{8,40},{12,44},{16,48},{20,52},{24,56},{28,60},{32,6... | collective-permute-start | bytes 786440 | tf_op jit(solution)/shard_map/ppermute | solution.py:30
  80.9 11.0 %collective-permute-start.27 = (bf16[128,1024]{1,0:T(8,128)(2,1)S(1)}, bf16[128,1024]{1,0:T(8,128)(2,1)S(1)}, u32[]{:S(2)}, u32[]{:S(2)}) collective-permute-start(bf16[128,1024]{1,0:T(8,128)(2,1)S(1)} %get-tuple-element.54), channel_id=1, source_target_pairs={{0,96},{4,100},{8,104},{12,108},{16,112},{20,116},{24,120},{28,124... | collective-permute-start | bytes 786440 | tf_op jit(solution)/shard_map/ppermute | solution.py:30

commit v7 on v6

--- a/solution.py
+++ b/solution.py
@@ -87,13 +87,15 @@
         pltpu.make_async_copy(down.at[0], columns.at[2], sems.at[5]),
         pltpu.make_async_copy(rates, r_ref, sems.at[6]),
     ]
-    for copy in copies:
+    for copy in copies[:3]:
         copy.start()
     copies[0].wait()
-    parts = []
-    for m in range(2):
-        copies[1 + m].wait()
-        parts.append(contract(columns[m], k_ref[:early], 0, 1))
+    copies[1].wait()
+    for copy in copies[3:]:
+        copy.start()
+    parts = [contract(columns[0], k_ref[:early], 0, 1)]
+    copies[2].wait()
+    parts.append(contract(columns[1], k_ref[:early], 0, 1))
     copies[3].wait()
     gate_in, up_in = (
         jnp.concatenate([part, contract(columns[m], k_ref[early:], 0, 1)], 1)
@@ -244,10 +246,8 @@
     return call(kernel, "render_rows", outs, *operands)
 
 
-def merge_kernel(mid, relay_left, relay_right, to_right, to_left):
-    half = to_right.shape[0]
-    to_right[...] = (mid[:half] + relay_left[...].astype(F32)).astype(BF16)
-    to_left[...] = (mid[half:] + relay_right[...].astype(F32)).astype(BF16)
+def merge_kernel(start, mid, relay, out):
+    out[...] = (mid[start : start + out.shape[0]] + relay[...].astype(F32)).astype(BF16)
 
 
 def own_kernel(own, from_left, from_right, out):
@@ -301,7 +301,8 @@
     direct, (mid,), (own,) = (render(rows, early + late, outs) for rows, outs in sets[1:])
     relay_left, relay_right = along_x(to_right, 1), along_x(to_left, -1)
     from_left_x, from_right_x = along_x(direct[0], 1), along_x(direct[1], -1)
-    to_right, to_left = call(merge_kernel, "merge", [part] * 2, mid, relay_left, relay_right)
+    to_right = call(functools.partial(merge_kernel, 0), "merge", part, mid, relay_left)
+    to_left = call(functools.partial(merge_kernel, half), "merge", part, mid, relay_right)
     last_left, last_right = along_x(to_right, 1), along_x(to_left, -1)
     own = call(own_kernel, "own", wide, own, from_left_x, from_right_x, us=OWN_US)
     out = jax.ShapeDtypeStruct(own.shape, BF16)

time: 92.9 us -> 92.9 us (level)
    pallas_call x16 -> x17, Pallas kernels: 7.05 us -> 7.04 us  [call(): pl.pallas_call(kernel, name=name, in_specs=[vmem] * len(operands), out_sp...]
where the time goes in v7:
time: 92.9 us; the launch traced here: 92.8 us
  starting transfers between devices  49.9 us (54%)
  waiting for transfers between devices  25.9 us (28%)
  Pallas kernels  16.8 us (18%)
    ppermute x28, starting transfers between devices, move(): return lax.ppermute(array, AXES, pairs)  49.9 us
    ppermute x28, waiting for transfers between devices, move(): return lax.ppermute(array, AXES, pairs)  25.9 us
    pallas_call x1, Pallas kernels, deltas(): pl.pallas_call(delta_kernel, name='deltas', in_specs=[pl.BlockSpec(memory...  9.79 us
    pallas_call x17, Pallas kernels, call(): pl.pallas_call(kernel, name=name, in_specs=[vmem] * len(operands), out_sp...  7.04 us
  transfers between devices with their start and end apart: 28, of which 12 were waited for; matrix products, arithmetic and copies ran while one was open for 0% of the time, Pallas kernels for 6%

profile of v7, /device:TPU:1, one launch (start us, length us, event | category | flops | bytes accessed | tf_op | source)
XLA Modules:
  0.0 92.8 jit_solution(13020063469380222392)
XLA Ops:
  0.0 9.8 %deltas.1 = (bf16[1,3,64,1024]{3,2,1,0:T(8,128)(2,1)S(1)}, bf16[1,3,64,1024]{3,2,1,0:T(8,128)(2,1)S(1)}, bf16[1,3,64,1024]{3,2,1,0:T(8,128)(2,1)S(1)}, bf16[1,3,...) custom-call(f32[1,1024]{1,0:T(1,128)} %rates.1, ...), custom_call_target="tpu_custom_call" | custom-call | flops 1 | bytes 1 | tf_op jit(solution)/shard_map/deltas/pallas_call | solution.py:139
  9.8 3.3 %collective-permute-start = (bf16[1,3,64,1024]{3,2,1,0:T(8,128)(2,1)S(1)}, bf16[1,3,64,1024]{3,2,1,0:T(8,128)(2,1)S(1)}, u32[]{:S(2)}, u32[]{:S(2)}) collective-permute-start(bf16[1,3,64,1024]{3,2,1,0:T(8,128)(2,1)S(1)} %get-tuple-element.29), channel_id=1, source_target_pairs={{0,16},{4,20},{8,24},{12,28},{16,0},{20,4},{24,8},{28,12},{32,48},... | collective-permute-start | bytes 1179656 | tf_op jit(solution)/shard_map/ppermute | solution.py:30
  13.1 0.1 collective-permute-start.2
  13.2 0.4 collective-permute-start.4
  13.6 0.1 collective-permute-start.6
  13.7 0.7 collective-permute-done.other
  14.5 0.1 add_cores.4
  14.6 1.2 %collective-permute-start.1 = (bf16[3,64,1024]{2,1,0:T(8,128)(2,1)S(1)}, bf16[3,64,1024]{2,1,0:T(8,128)(2,1)S(1)}, u32[]{:S(2)}, u32[]{:S(2)}) collective-permute-start(bf16[3,64,1024]{2,1,0:T(8,128)(2,1)S(1)} %add_cores.4), channel_id=1, source_target_pairs={{0,32},{4,36},{8,40},{12,44},{16,160},{20,164},{24,168},{28,172},{... | collective-permute-start | bytes 1179656 | tf_op jit(solution)/shard_map/ppermute | solution.py:30
  15.7 0.0 collective-permute-done.2.other
  15.7 0.1 add_cores.5
  15.8 2.8 %collective-permute-start.3 = (bf16[3,64,1024]{2,1,0:T(8,128)(2,1)S(1)}, bf16[3,64,1024]{2,1,0:T(8,128)(2,1)S(1)}, u32[]{:S(2)}, u32[]{:S(2)}) collective-permute-start(bf16[3,64,1024]{2,1,0:T(8,128)(2,1)S(1)} %add_cores.5), channel_id=1, source_target_pairs={{0,96},{4,100},{8,104},{12,108},{16,224},{20,228},{24,232},{28,236... | collective-permute-start | bytes 1179656 | tf_op jit(solution)/shard_map/ppermute | solution.py:30
  18.7 0.0 collective-permute-done.4.other
  18.7 0.1 add_cores.6
  18.8 1.5 %collective-permute-start.5 = (bf16[3,64,1024]{2,1,0:T(8,128)(2,1)S(1)}, bf16[3,64,1024]{2,1,0:T(8,128)(2,1)S(1)}, u32[]{:S(2)}, u32[]{:S(2)}) collective-permute-start(bf16[3,64,1024]{2,1,0:T(8,128)(2,1)S(1)} %add_cores.6), channel_id=1, source_target_pairs={{0,64},{4,68},{8,72},{12,76},{16,192},{20,196},{24,200},{28,204},{... | collective-permute-start | bytes 1179656 | tf_op jit(solution)/shard_map/ppermute | solution.py:30
  20.3 0.1 add_cores.7
  20.4 0.0 copy-start
  20.4 2.1 %collective-permute-start.7 = (bf16[3,64,1024]{2,1,0:T(8,128)(2,1)S(1)}, bf16[3,64,1024]{2,1,0:T(8,128)(2,1)S(1)}, u32[]{:S(2)}, u32[]{:S(2)}) collective-permute-start(bf16[3,64,1024]{2,1,0:T(8,128)(2,1)S(1)} %add_cores.7), channel_id=1, source_target_pairs={{0,0},{4,4},{8,8},{12,12},{16,128},{20,132},{24,136},{28,140},{32,... | collective-permute-start | bytes 1179656 | tf_op jit(solution)/shard_map/ppermute | solution.py:30
  22.4 1.6 %collective-permute-done.1.refs_0_ = bf16[3,64,1024]{2,1,0:T(8,128)(2,1)S(1)} collective-permute-done((bf16[3,64,1024]{2,1,0:T(8,128)(2,1)S(1)}, bf16[3,64,1024]{2,1,0:T(8,128)(2,1)S(1)}, u32[]{:S(2)}, u32[]{:S(2)}) %collective-permute-start.1) | collective-permute-done | bytes 393248 | tf_op jit(solution)/shard_map/ppermute | solution.py:30
  24.1 2.5 %collective-permute-done.3.refs_1_ = bf16[3,64,1024]{2,1,0:T(8,128)(2,1)S(1)} collective-permute-done((bf16[3,64,1024]{2,1,0:T(8,128)(2,1)S(1)}, bf16[3,64,1024]{2,1,0:T(8,128)(2,1)S(1)}, u32[]{:S(2)}, u32[]{:S(2)}) %collective-permute-start.3) | collective-permute-done | bytes 393248 | tf_op jit(solution)/shard_map/ppermute | solution.py:30
  26.6 5.9 %collective-permute-done.5.refs_2_ = bf16[3,64,1024]{2,1,0:T(8,128)(2,1)S(1)} collective-permute-done((bf16[3,64,1024]{2,1,0:T(8,128)(2,1)S(1)}, bf16[3,64,1024]{2,1,0:T(8,128)(2,1)S(1)}, u32[]{:S(2)}, u32[]{:S(2)}) %collective-permute-start.5) | collective-permute-done | bytes 393248 | tf_op jit(solution)/shard_map/ppermute | solution.py:30
  32.5 1.6 %collective-permute-done.7.refs_3_ = bf16[3,64,1024]{2,1,0:T(8,128)(2,1)S(1)} collective-permute-done((bf16[3,64,1024]{2,1,0:T(8,128)(2,1)S(1)}, bf16[3,64,1024]{2,1,0:T(8,128)(2,1)S(1)}, u32[]{:S(2)}, u32[]{:S(2)}) %collective-permute-start.7) | collective-permute-done | bytes 393248 | tf_op jit(solution)/shard_map/ppermute | solution.py:30
  34.1 0.2 sum_chips.1.mine
  34.3 2.8 %collective-permute-start.8 = (bf16[3,64,1024]{2,1,0:T(8,128)(2,1)S(1)}, bf16[3,64,1024]{2,1,0:T(8,128)(2,1)S(1)}, u32[]{:S(2)}, u32[]{:S(2)}) collective-permute-start(bf16[3,64,1024]{2,1,0:T(8,128)(2,1)S(1)} %sum_chips.1.mine), channel_id=1, source_target_pairs={{0,16},{4,20},{8,24},{12,28},{16,0},{20,4},{24,8},{28,12},{32,48},... | collective-permute-start | bytes 1179656 | tf_op jit(solution)/shard_map/ppermute | solution.py:30
  37.1 0.8 collective-permute-start.17
  37.9 2.4 %collective-permute-start.15 = (bf16[256,1024]{1,0:T(8,128)(2,1)S(1)}, bf16[256,1024]{1,0:T(8,128)(2,1)S(1)}, u32[]{:S(2)}, u32[]{:S(2)}) collective-permute-start(bf16[256,1024]{1,0:T(8,128)(2,1)S(1)} %copy-done), channel_id=1, source_target_pairs={{0,96},{4,100},{8,104},{12,108},{16,112},{20,116},{24,120},{28,124... | collective-permute-start | bytes 1572872 | tf_op jit(solution)/shard_map/ppermute | solution.py:30
  40.3 0.0 collective-permute-done.8.other
  40.3 0.4 renorm.1
  40.6 3.6 %collective-permute-start.9 = (bf16[3,32,1024]{2,1,0:T(8,128)(2,1)S(1)}, bf16[3,32,1024]{2,1,0:T(8,128)(2,1)S(1)}, u32[]{:S(2)}, u32[]{:S(2)}) collective-permute-start(bf16[3,32,1024]{2,1,0:T(8,128)(2,1)S(1)} %get-tuple-element.40.refs_2_.refs_1_), channel_id=1, source_target_pairs={{0,128},{4,132},{8,136},{12,140},{16,156},{20,144},{24,148},{28,15... | collective-permute-start | bytes 589832 | tf_op jit(solution)/shard_map/ppermute | solution.py:30
  44.2 1.6 %collective-permute-start.10 = (bf16[3,32,1024]{2,1,0:T(8,128)(2,1)S(1)}, bf16[3,32,1024]{2,1,0:T(8,128)(2,1)S(1)}, u32[]{:S(2)}, u32[]{:S(2)}) collective-permute-start(bf16[3,32,1024]{2,1,0:T(8,128)(2,1)S(1)} %get-tuple-element.41.refs_3_.refs_2_), channel_id=1, source_target_pairs={{0,128},{4,132},{8,136},{12,140},{16,156},{20,144},{24,148},{28,15... | collective-permute-start | bytes 589832 | tf_op jit(solution)/shard_map/ppermute | solution.py:30
  45.8 1.1 %collective-permute-done.9.refs_0_ = bf16[3,32,1024]{2,1,0:T(8,128)(2,1)S(1)} collective-permute-done((bf16[3,32,1024]{2,1,0:T(8,128)(2,1)S(1)}, bf16[3,32,1024]{2,1,0:T(8,128)(2,1)S(1)}, u32[]{:S(2)}, u32[]{:S(2)}) %collective-permute-start.9) | collective-permute-done | bytes 196640 | tf_op jit(solution)/shard_map/ppermute | solution.py:30
  46.9 3.4 %collective-permute-start.11 = (bf16[3,32,1024]{2,1,0:T(8,128)(2,1)S(1)}, bf16[3,32,1024]{2,1,0:T(8,128)(2,1)S(1)}, u32[]{:S(2)}, u32[]{:S(2)}) collective-permute-start(bf16[3,32,1024]{2,1,0:T(8,128)(2,1)S(1)} %collective-permute-done.9.refs_0_), channel_id=1, source_target_pairs={{0,128},{4,132},{8,136},{12,140},{16,156},{20,144},{24,148},{28,15... | collective-permute-start | bytes 589832 | tf_op jit(solution)/shard_map/ppermute | solution.py:30
  50.3 2.1 %collective-permute-start.12 = (bf16[3,32,1024]{2,1,0:T(8,128)(2,1)S(1)}, bf16[3,32,1024]{2,1,0:T(8,128)(2,1)S(1)}, u32[]{:S(2)}, u32[]{:S(2)}) collective-permute-start(bf16[3,32,1024]{2,1,0:T(8,128)(2,1)S(1)} %collective-permute-done.10.refs_1_), channel_id=1, source_target_pairs={{0,128},{4,132},{8,136},{12,140},{16,156},{20,144},{24,148},{28,15... | collective-permute-start | bytes 589832 | tf_op jit(solution)/shard_map/ppermute | solution.py:30
  52.4 0.5 collective-permute-done.11.refs_2_
  52.9 3.4 %collective-permute-start.13 = (bf16[3,32,1024]{2,1,0:T(8,128)(2,1)S(1)}, bf16[3,32,1024]{2,1,0:T(8,128)(2,1)S(1)}, u32[]{:S(2)}, u32[]{:S(2)}) collective-permute-start(bf16[3,32,1024]{2,1,0:T(8,128)(2,1)S(1)} %collective-permute-done.11.refs_2_), channel_id=1, source_target_pairs={{0,128},{4,132},{8,136},{12,140},{16,156},{20,144},{24,148},{28,15... | collective-permute-start | bytes 589832 | tf_op jit(solution)/shard_map/ppermute | solution.py:30
  56.3 0.1 collective-permute-start.18
  56.4 0.0 collective-permute-done.15.refs_0_
  56.4 2.7 %collective-permute-start.16 = (bf16[128,1024]{1,0:T(8,128)(2,1)S(1)}, bf16[128,1024]{1,0:T(8,128)(2,1)S(1)}, u32[]{:S(2)}, u32[]{:S(2)}) collective-permute-start(bf16[128,1024]{1,0:T(8,128)(2,1)S(1)} %slice.8), channel_id=1, source_target_pairs={{0,96},{4,100},{8,104},{12,108},{16,112},{20,116},{24,120},{28,124... | collective-permute-start | bytes 786440 | tf_op jit(solution)/shard_map/ppermute | solution.py:30
  59.2 0.0 collective-permute-done.12.refs_3_
  59.2 0.0 collective-permute-start.14
  59.2 0.0 collective-permute-done.13.refs_0_
  59.2 2.8 %collective-permute-start.19 = (bf16[3,32,1024]{2,1,0:T(8,128)(2,1)S(1)}, bf16[3,32,1024]{2,1,0:T(8,128)(2,1)S(1)}, u32[]{:S(2)}, u32[]{:S(2)}) collective-permute-start(bf16[3,32,1024]{2,1,0:T(8,128)(2,1)S(1)} %collective-permute-done.13.refs_0_), channel_id=1, source_target_pairs={{0,128},{4,132},{8,136},{12,140},{16,156},{20,144},{24,148},{28,15... | collective-permute-start | bytes 589832 | tf_op jit(solution)/shard_map/ppermute | solution.py:30
  62.0 0.1 join.2.refs_4_.refs_3_
  62.1 0.7 collective-permute-start.20
  62.7 3.0 %collective-permute-done.18.refs_1_ = bf16[128,1024]{1,0:T(8,128)(2,1)S(1)} collective-permute-done((bf16[128,1024]{1,0:T(8,128)(2,1)S(1)}, bf16[128,1024]{1,0:T(8,128)(2,1)S(1)}, u32[]{:S(2)}, u32[]{:S(2)}) %collective-permute-start.18) | collective-permute-done | bytes 262176 | tf_op jit(solution)/shard_map/ppermute | solution.py:30
  65.7 0.1 collective-permute-done.19.refs_2_
  65.8 3.8 %collective-permute-start.21 = (bf16[3,96,1024]{2,1,0:T(8,128)(2,1)S(1)}, bf16[3,96,1024]{2,1,0:T(8,128)(2,1)S(1)}, u32[]{:S(2)}, u32[]{:S(2)}) collective-permute-start(bf16[3,96,1024]{2,1,0:T(8,128)(2,1)S(1)} %join.3.refs_5_.refs_4_), channel_id=1, source_target_pairs={{0,16},{4,20},{8,24},{12,28},{16,0},{20,4},{24,8},{28,12},{32,48},... | collective-permute-start | bytes 1769480 | tf_op jit(solution)/shard_map/ppermute | solution.py:30
  69.6 1.0 %render_rows.5.refs_4_ = f32[256,1024]{1,0:T(8,128)S(1)} custom-call(bf16[128,1024]{1,0:T(8,128)(2,1)S(1)} %collective-permute-done.16.refs_0_, bf16[128,1024]{1,0:T(8,128)(2,1)S(1)} %collective-permute-done.18.refs_1_, bf16[3,32,1024]{2,1,0:T(8,128)(2,1)S(1)} %get-tuple-element.40.refs_2_.refs_1_, ...), custom_call_target="tpu_custom_call" | custom-call | flops 1 | bytes 1 | tf_op jit(solution)/shard_map/render_rows/pallas_call | solution.py:161
  70.6 0.6 collective-permute-done.21.refs_6_.refs_7_.refs_3_
  71.2 0.0 collective-permute-done.20.refs_5_.refs_6_.refs_2_
  71.2 0.7 render_rows.9
  71.9 0.1 collective-permute-start.24
  72.0 2.7 %collective-permute-start.26 = (bf16[128,1024]{1,0:T(8,128)(2,1)S(1)}, bf16[128,1024]{1,0:T(8,128)(2,1)S(1)}, u32[]{:S(2)}, u32[]{:S(2)}) collective-permute-start(bf16[128,1024]{1,0:T(8,128)(2,1)S(1)} %get-tuple-element.50), channel_id=1, source_target_pairs={{0,96},{4,100},{8,104},{12,108},{16,112},{20,116},{24,120},{28,124... | collective-permute-start | bytes 786440 | tf_op jit(solution)/shard_map/ppermute | solution.py:30
  74.7 1.1 %render_rows.7 = (bf16[128,1024]{1,0:T(8,128)(2,1)S(1)}, bf16[128,1024]{1,0:T(8,128)(2,1)S(1)}) custom-call(bf16[256,1024]{1,0:T(8,128)(2,1)S(1)} %collective-permute-done.15.refs_0_, bf16[256,1024]{1,0:T(8,128)(2,1)S(1)} %collective-permute-done.17.refs_1_, bf16[3,32,1024]{2,1,0:T(8,128)(2,1)S(1)} %get-tuple-element.40.refs_2_.refs_1_, ...), custom_call_target="tpu_custom_call" | custom-call | flops 1 | bytes 1 | tf_op jit(solution)/shard_map/render_rows/pallas_call | solution.py:161
  75.8 0.1 collective-permute-start.22
  75.8 2.7 %collective-permute-start.23 = (bf16[128,1024]{1,0:T(8,128)(2,1)S(1)}, bf16[128,1024]{1,0:T(8,128)(2,1)S(1)}, u32[]{:S(2)}, u32[]{:S(2)}) collective-permute-start(bf16[128,1024]{1,0:T(8,128)(2,1)S(1)} %get-tuple-element.47), channel_id=1, source_target_pairs={{0,96},{4,100},{8,104},{12,108},{16,112},{20,116},{24,120},{28,124... | collective-permute-start | bytes 786440 | tf_op jit(solution)/shard_map/ppermute | solution.py:30
  78.5 1.1 %render_rows.8.mid = f32[256,1024]{1,0:T(8,128)S(1)} custom-call(bf16[256,1024]{1,0:T(8,128)(2,1)S(1)} %collective-permute-done.15.refs_0_, bf16[256,1024]{1,0:T(8,128)(2,1)S(1)} %collective-permute-done.17.refs_1_, bf16[3,32,1024]{2,1,0:T(8,128)(2,1)S(1)} %get-tuple-element.40.refs_2_.refs_1_, bf16[3,32,1024]{2,1,0:T(8,128)(2,1)S(1)} %get-tuple-element.41.refs_3_.refs_2_, ...), custom_call_target="tpu_custom_call" | custom-call | flops 1 | bytes 1 | tf_op jit(solution)/shard_map/render_rows/pallas_call | solution.py:161
  79.6 1.1 %render_rows.6.own = f32[256,1024]{1,0:T(8,128)S(1)} custom-call(bf16[256,1024]{1,0:T(8,128)(2,1)S(1)} %copy-done, bf16[3,32,1024]{2,1,0:T(8,128)(2,1)S(1)} %get-tuple-element.40.refs_2_.refs_1_, bf16[3,32,1024]{2,1,0:T(8,128)(2,1)S(1)} %get-tuple-element.41.refs_3_.refs_2_, bf16[3,128,1024]{2,1,0:T(8,128)(2,1)S(1)} %join.2.refs_4_.refs_3_, ...), custom_call_target="tpu_custom_call" | custom-call | flops 1 | bytes 1 | tf_op jit(solution)/shard_map/render_rows/pallas_call | solution.py:161
  80.7 0.0 collective-permute-done.24.relay
  80.8 0.1 collective-permute-start.25
  80.9 2.7 %collective-permute-start.27 = (bf16[128,1024]{1,0:T(8,128)(2,1)S(1)}, bf16[128,1024]{1,0:T(8,128)(2,1)S(1)}, u32[]{:S(2)}, u32[]{:S(2)}) collective-permute-start(bf16[128,1024]{1,0:T(8,128)(2,1)S(1)} %merge.3), channel_id=1, source_target_pairs={{0,96},{4,100},{8,104},{12,108},{16,112},{20,116},{24,120},{28,124... | collective-permute-start | bytes 786440 | tf_op jit(solution)/shard_map/ppermute | solution.py:30
  83.7 2.7 %collective-permute-done.22.from_left = bf16[128,1024]{1,0:T(8,128)(2,1)S(1)} collective-permute-done((bf16[128,1024]{1,0:T(8,128)(2,1)S(1)}, bf16[128,1024]{1,0:T(8,128)(2,1)S(1)}, u32[]{:S(2)}, u32[]{:S(2)}) %collective-permute-start.22) | collective-permute-done | bytes 262176 | tf_op jit(solution)/shard_map/ppermute | solution.py:30
  86.3 0.1 own.1
  86.4 5.5 %collective-permute-done.25.last_left = bf16[128,1024]{1,0:T(8,128)(2,1)S(1)} collective-permute-done((bf16[128,1024]{1,0:T(8,128)(2,1)S(1)}, bf16[128,1024]{1,0:T(8,128)(2,1)S(1)}, u32[]{:S(2)}, u32[]{:S(2)}) %collective-permute-start.25) | collective-permute-done | bytes 262176 | tf_op jit(solution)/shard_map/ppermute | solution.py:30
  91.9 0.9 total.1
  (14 shorter events, 0.2 us)
Async XLA Ops:
  9.8 4.7 %collective-permute-start = (bf16[1,3,64,1024]{3,2,1,0:T(8,128)(2,1)S(1)}, bf16[1,3,64,1024]{3,2,1,0:T(8,128)(2,1)S(1)}, u32[]{:S(2)}, u32[]{:S(2)}) collective-permute-start(bf16[1,3,64,1024]{3,2,1,0:T(8,128)(2,1)S(1)} %get-tuple-element.29), channel_id=1, source_target_pairs={{0,16},{4,20},{8,24},{12,28},{16,0},{20,4},{24,8},{28,12},{32,48},... | collective-permute-start | bytes 1179656 | tf_op jit(solution)/shard_map/ppermute | solution.py:30
  13.1 2.6 %collective-permute-start.2 = (bf16[1,3,64,1024]{3,2,1,0:T(8,128)(2,1)S(1)}, bf16[1,3,64,1024]{3,2,1,0:T(8,128)(2,1)S(1)}, u32[]{:S(2)}, u32[]{:S(2)}) collective-permute-start(bf16[1,3,64,1024]{3,2,1,0:T(8,128)(2,1)S(1)} %get-tuple-element.31), channel_id=1, source_target_pairs={{0,16},{4,20},{8,24},{12,28},{16,0},{20,4},{24,8},{28,12},{32,48},... | collective-permute-start | bytes 1179656 | tf_op jit(solution)/shard_map/ppermute | solution.py:30
  13.2 5.5 %collective-permute-start.4 = (bf16[1,3,64,1024]{3,2,1,0:T(8,128)(2,1)S(1)}, bf16[1,3,64,1024]{3,2,1,0:T(8,128)(2,1)S(1)}, u32[]{:S(2)}, u32[]{:S(2)}) collective-permute-start(bf16[1,3,64,1024]{3,2,1,0:T(8,128)(2,1)S(1)} %get-tuple-element.37), channel_id=1, source_target_pairs={{0,16},{4,20},{8,24},{12,28},{16,0},{20,4},{24,8},{28,12},{32,48},... | collective-permute-start | bytes 1179656 | tf_op jit(solution)/shard_map/ppermute | solution.py:30
  13.6 6.6 %collective-permute-start.6 = (bf16[1,3,64,1024]{3,2,1,0:T(8,128)(2,1)S(1)}, bf16[1,3,64,1024]{3,2,1,0:T(8,128)(2,1)S(1)}, u32[]{:S(2)}, u32[]{:S(2)}) collective-permute-start(bf16[1,3,64,1024]{3,2,1,0:T(8,128)(2,1)S(1)} %get-tuple-element.39), channel_id=1, source_target_pairs={{0,16},{4,20},{8,24},{12,28},{16,0},{20,4},{24,8},{28,12},{32,48},... | collective-permute-start | bytes 1179656 | tf_op jit(solution)/shard_map/ppermute | solution.py:30
  14.6 9.5 %collective-permute-start.1 = (bf16[3,64,1024]{2,1,0:T(8,128)(2,1)S(1)}, bf16[3,64,1024]{2,1,0:T(8,128)(2,1)S(1)}, u32[]{:S(2)}, u32[]{:S(2)}) collective-permute-start(bf16[3,64,1024]{2,1,0:T(8,128)(2,1)S(1)} %add_cores.4), channel_id=1, source_target_pairs={{0,32},{4,36},{8,40},{12,44},{16,160},{20,164},{24,168},{28,172},{... | collective-permute-start | bytes 1179656 | tf_op jit(solution)/shard_map/ppermute | solution.py:30
  15.8 10.7 %collective-permute-start.3 = (bf16[3,64,1024]{2,1,0:T(8,128)(2,1)S(1)}, bf16[3,64,1024]{2,1,0:T(8,128)(2,1)S(1)}, u32[]{:S(2)}, u32[]{:S(2)}) collective-permute-start(bf16[3,64,1024]{2,1,0:T(8,128)(2,1)S(1)} %add_cores.5), channel_id=1, source_target_pairs={{0,96},{4,100},{8,104},{12,108},{16,224},{20,228},{24,232},{28,236... | collective-permute-start | bytes 1179656 | tf_op jit(solution)/shard_map/ppermute | solution.py:30
  18.8 13.7 %collective-permute-start.5 = (bf16[3,64,1024]{2,1,0:T(8,128)(2,1)S(1)}, bf16[3,64,1024]{2,1,0:T(8,128)(2,1)S(1)}, u32[]{:S(2)}, u32[]{:S(2)}) collective-permute-start(bf16[3,64,1024]{2,1,0:T(8,128)(2,1)S(1)} %add_cores.6), channel_id=1, source_target_pairs={{0,64},{4,68},{8,72},{12,76},{16,192},{20,196},{24,200},{28,204},{... | collective-permute-start | bytes 1179656 | tf_op jit(solution)/shard_map/ppermute | solution.py:30
  20.4 16.8 %copy-start = (bf16[256,1024]{1,0:T(8,128)(2,1)S(1)}, bf16[256,1024]{1,0:T(8,128)(2,1)}, u32[]{:S(2)}) copy-start(bf16[256,1024]{1,0:T(8,128)(2,1)} %refs_0_) | copy-start | bytes 1572868
  20.4 13.7 %collective-permute-start.7 = (bf16[3,64,1024]{2,1,0:T(8,128)(2,1)S(1)}, bf16[3,64,1024]{2,1,0:T(8,128)(2,1)S(1)}, u32[]{:S(2)}, u32[]{:S(2)}) collective-permute-start(bf16[3,64,1024]{2,1,0:T(8,128)(2,1)S(1)} %add_cores.7), channel_id=1, source_target_pairs={{0,0},{4,4},{8,8},{12,12},{16,128},{20,132},{24,136},{28,140},{32,... | collective-permute-start | bytes 1179656 | tf_op jit(solution)/shard_map/ppermute | solution.py:30
  34.3 6.0 %collective-permute-start.8 = (bf16[3,64,1024]{2,1,0:T(8,128)(2,1)S(1)}, bf16[3,64,1024]{2,1,0:T(8,128)(2,1)S(1)}, u32[]{:S(2)}, u32[]{:S(2)}) collective-permute-start(bf16[3,64,1024]{2,1,0:T(8,128)(2,1)S(1)} %sum_chips.1.mine), channel_id=1, source_target_pairs={{0,16},{4,20},{8,24},{12,28},{16,0},{20,4},{24,8},{28,12},{32,48},... | collective-permute-start | bytes 1179656 | tf_op jit(solution)/shard_map/ppermute | solution.py:30
  37.1 19.1 %collective-permute-start.17 = (bf16[256,1024]{1,0:T(8,128)(2,1)S(1)}, bf16[256,1024]{1,0:T(8,128)(2,1)S(1)}, u32[]{:S(2)}, u32[]{:S(2)}) collective-permute-start(bf16[256,1024]{1,0:T(8,128)(2,1)S(1)} %copy-done), channel_id=1, source_target_pairs={{0,32},{4,36},{8,40},{12,44},{16,48},{20,52},{24,56},{28,60},{32,6... | collective-permute-start | bytes 1572872 | tf_op jit(solution)/shard_map/ppermute | solution.py:30
  37.9 18.5 %collective-permute-start.15 = (bf16[256,1024]{1,0:T(8,128)(2,1)S(1)}, bf16[256,1024]{1,0:T(8,128)(2,1)S(1)}, u32[]{:S(2)}, u32[]{:S(2)}) collective-permute-start(bf16[256,1024]{1,0:T(8,128)(2,1)S(1)} %copy-done), channel_id=1, source_target_pairs={{0,96},{4,100},{8,104},{12,108},{16,112},{20,116},{24,120},{28,124... | collective-permute-start | bytes 1572872 | tf_op jit(solution)/shard_map/ppermute | solution.py:30
  40.6 6.2 %collective-permute-start.9 = (bf16[3,32,1024]{2,1,0:T(8,128)(2,1)S(1)}, bf16[3,32,1024]{2,1,0:T(8,128)(2,1)S(1)}, u32[]{:S(2)}, u32[]{:S(2)}) collective-permute-start(bf16[3,32,1024]{2,1,0:T(8,128)(2,1)S(1)} %get-tuple-element.40.refs_2_.refs_1_), channel_id=1, source_target_pairs={{0,128},{4,132},{8,136},{12,140},{16,156},{20,144},{24,148},{28,15... | collective-permute-start | bytes 589832 | tf_op jit(solution)/shard_map/ppermute | solution.py:30
  44.2 6.0 %collective-permute-start.10 = (bf16[3,32,1024]{2,1,0:T(8,128)(2,1)S(1)}, bf16[3,32,1024]{2,1,0:T(8,128)(2,1)S(1)}, u32[]{:S(2)}, u32[]{:S(2)}) collective-permute-start(bf16[3,32,1024]{2,1,0:T(8,128)(2,1)S(1)} %get-tuple-element.41.refs_3_.refs_2_), channel_id=1, source_target_pairs={{0,128},{4,132},{8,136},{12,140},{16,156},{20,144},{24,148},{28,15... | collective-permute-start | bytes 589832 | tf_op jit(solution)/shard_map/ppermute | solution.py:30
  46.9 6.0 %collective-permute-start.11 = (bf16[3,32,1024]{2,1,0:T(8,128)(2,1)S(1)}, bf16[3,32,1024]{2,1,0:T(8,128)(2,1)S(1)}, u32[]{:S(2)}, u32[]{:S(2)}) collective-permute-start(bf16[3,32,1024]{2,1,0:T(8,128)(2,1)S(1)} %collective-permute-done.9.refs_0_), channel_id=1, source_target_pairs={{0,128},{4,132},{8,136},{12,140},{16,156},{20,144},{24,148},{28,15... | collective-permute-start | bytes 589832 | tf_op jit(solution)/shard_map/ppermute | solution.py:30
  50.3 8.9 %collective-permute-start.12 = (bf16[3,32,1024]{2,1,0:T(8,128)(2,1)S(1)}, bf16[3,32,1024]{2,1,0:T(8,128)(2,1)S(1)}, u32[]{:S(2)}, u32[]{:S(2)}) collective-permute-start(bf16[3,32,1024]{2,1,0:T(8,128)(2,1)S(1)} %collective-permute-done.10.refs_1_), channel_id=1, source_target_pairs={{0,128},{4,132},{8,136},{12,140},{16,156},{20,144},{24,148},{28,15... | collective-permute-start | bytes 589832 | tf_op jit(solution)/shard_map/ppermute | solution.py:30
  52.9 6.3 %collective-permute-start.13 = (bf16[3,32,1024]{2,1,0:T(8,128)(2,1)S(1)}, bf16[3,32,1024]{2,1,0:T(8,128)(2,1)S(1)}, u32[]{:S(2)}, u32[]{:S(2)}) collective-permute-start(bf16[3,32,1024]{2,1,0:T(8,128)(2,1)S(1)} %collective-permute-done.11.refs_2_), channel_id=1, source_target_pairs={{0,128},{4,132},{8,136},{12,140},{16,156},{20,144},{24,148},{28,15... | collective-permute-start | bytes 589832 | tf_op jit(solution)/shard_map/ppermute | solution.py:30
  56.3 9.4 %collective-permute-start.18 = (bf16[128,1024]{1,0:T(8,128)(2,1)S(1)}, bf16[128,1024]{1,0:T(8,128)(2,1)S(1)}, u32[]{:S(2)}, u32[]{:S(2)}) collective-permute-start(bf16[128,1024]{1,0:T(8,128)(2,1)S(1)} %slice.9), channel_id=1, source_target_pairs={{0,32},{4,36},{8,40},{12,44},{16,48},{20,52},{24,56},{28,60},{32,6... | collective-permute-start | bytes 786440 | tf_op jit(solution)/shard_map/ppermute | solution.py:30
  56.4 9.3 %collective-permute-start.16 = (bf16[128,1024]{1,0:T(8,128)(2,1)S(1)}, bf16[128,1024]{1,0:T(8,128)(2,1)S(1)}, u32[]{:S(2)}, u32[]{:S(2)}) collective-permute-start(bf16[128,1024]{1,0:T(8,128)(2,1)S(1)} %slice.8), channel_id=1, source_target_pairs={{0,96},{4,100},{8,104},{12,108},{16,112},{20,116},{24,120},{28,124... | collective-permute-start | bytes 786440 | tf_op jit(solution)/shard_map/ppermute | solution.py:30
  59.2 6.5 %collective-permute-start.14 = (bf16[3,32,1024]{2,1,0:T(8,128)(2,1)S(1)}, bf16[3,32,1024]{2,1,0:T(8,128)(2,1)S(1)}, u32[]{:S(2)}, u32[]{:S(2)}) collective-permute-start(bf16[3,32,1024]{2,1,0:T(8,128)(2,1)S(1)} %collective-permute-done.12.refs_3_), channel_id=1, source_target_pairs={{0,128},{4,132},{8,136},{12,140},{16,156},{20,144},{24,148},{28,15... | collective-permute-start | bytes 589832 | tf_op jit(solution)/shard_map/ppermute | solution.py:30
  59.2 6.6 %collective-permute-start.19 = (bf16[3,32,1024]{2,1,0:T(8,128)(2,1)S(1)}, bf16[3,32,1024]{2,1,0:T(8,128)(2,1)S(1)}, u32[]{:S(2)}, u32[]{:S(2)}) collective-permute-start(bf16[3,32,1024]{2,1,0:T(8,128)(2,1)S(1)} %collective-permute-done.13.refs_0_), channel_id=1, source_target_pairs={{0,128},{4,132},{8,136},{12,140},{16,156},{20,144},{24,148},{28,15... | collective-permute-start | bytes 589832 | tf_op jit(solution)/shard_map/ppermute | solution.py:30
  62.1 9.2 %collective-permute-start.20 = (bf16[3,128,1024]{2,1,0:T(8,128)(2,1)S(1)}, bf16[3,128,1024]{2,1,0:T(8,128)(2,1)S(1)}, u32[]{:S(2)}, u32[]{:S(2)}) collective-permute-start(bf16[3,128,1024]{2,1,0:T(8,128)(2,1)S(1)} %join.2.refs_4_.refs_3_), channel_id=1, source_target_pairs={{0,16},{4,20},{8,24},{12,28},{16,0},{20,4},{24,8},{28,12},{32,48},... | collective-permute-start | bytes 2359304 | tf_op jit(solution)/shard_map/ppermute | solution.py:30
  65.8 5.4 %collective-permute-start.21 = (bf16[3,96,1024]{2,1,0:T(8,128)(2,1)S(1)}, bf16[3,96,1024]{2,1,0:T(8,128)(2,1)S(1)}, u32[]{:S(2)}, u32[]{:S(2)}) collective-permute-start(bf16[3,96,1024]{2,1,0:T(8,128)(2,1)S(1)} %join.3.refs_5_.refs_4_), channel_id=1, source_target_pairs={{0,16},{4,20},{8,24},{12,28},{16,0},{20,4},{24,8},{28,12},{32,48},... | collective-permute-start | bytes 1769480 | tf_op jit(solution)/shard_map/ppermute | solution.py:30
  71.9 8.8 %collective-permute-start.24 = (bf16[128,1024]{1,0:T(8,128)(2,1)S(1)}, bf16[128,1024]{1,0:T(8,128)(2,1)S(1)}, u32[]{:S(2)}, u32[]{:S(2)}) collective-permute-start(bf16[128,1024]{1,0:T(8,128)(2,1)S(1)} %get-tuple-element.49), channel_id=1, source_target_pairs={{0,32},{4,36},{8,40},{12,44},{16,48},{20,52},{24,56},{28,60},{32,6... | collective-permute-start | bytes 786440 | tf_op jit(solution)/shard_map/ppermute | solution.py:30
  72.0 8.9 %collective-permute-start.26 = (bf16[128,1024]{1,0:T(8,128)(2,1)S(1)}, bf16[128,1024]{1,0:T(8,128)(2,1)S(1)}, u32[]{:S(2)}, u32[]{:S(2)}) collective-permute-start(bf16[128,1024]{1,0:T(8,128)(2,1)S(1)} %get-tuple-element.50), channel_id=1, source_target_pairs={{0,96},{4,100},{8,104},{12,108},{16,112},{20,116},{24,120},{28,124... | collective-permute-start | bytes 786440 | tf_op jit(solution)/shard_map/ppermute | solution.py:30
  75.8 10.6 %collective-permute-start.22 = (bf16[128,1024]{1,0:T(8,128)(2,1)S(1)}, bf16[128,1024]{1,0:T(8,128)(2,1)S(1)}, u32[]{:S(2)}, u32[]{:S(2)}) collective-permute-start(bf16[128,1024]{1,0:T(8,128)(2,1)S(1)} %get-tuple-element.46), channel_id=1, source_target_pairs={{0,32},{4,36},{8,40},{12,44},{16,48},{20,52},{24,56},{28,60},{32,6... | collective-permute-start | bytes 786440 | tf_op jit(solution)/shard_map/ppermute | solution.py:30
  75.8 10.5 %collective-permute-start.23 = (bf16[128,1024]{1,0:T(8,128)(2,1)S(1)}, bf16[128,1024]{1,0:T(8,128)(2,1)S(1)}, u32[]{:S(2)}, u32[]{:S(2)}) collective-permute-start(bf16[128,1024]{1,0:T(8,128)(2,1)S(1)} %get-tuple-element.47), channel_id=1, source_target_pairs={{0,96},{4,100},{8,104},{12,108},{16,112},{20,116},{24,120},{28,124... | collective-permute-start | bytes 786440 | tf_op jit(solution)/shard_map/ppermute | solution.py:30
  80.8 11.2 %collective-permute-start.25 = (bf16[128,1024]{1,0:T(8,128)(2,1)S(1)}, bf16[128,1024]{1,0:T(8,128)(2,1)S(1)}, u32[]{:S(2)}, u32[]{:S(2)}) collective-permute-start(bf16[128,1024]{1,0:T(8,128)(2,1)S(1)} %merge.2), channel_id=1, source_target_pairs={{0,32},{4,36},{8,40},{12,44},{16,48},{20,52},{24,56},{28,60},{32,6... | collective-permute-start | bytes 786440 | tf_op jit(solution)/shard_map/ppermute | solution.py:30
  80.9 11.0 %collective-permute-start.27 = (bf16[128,1024]{1,0:T(8,128)(2,1)S(1)}, bf16[128,1024]{1,0:T(8,128)(2,1)S(1)}, u32[]{:S(2)}, u32[]{:S(2)}) collective-permute-start(bf16[128,1024]{1,0:T(8,128)(2,1)S(1)} %merge.3), channel_id=1, source_target_pairs={{0,96},{4,100},{8,104},{12,108},{16,112},{20,116},{24,120},{28,124... | collective-permute-start | bytes 786440 | tf_op jit(solution)/shard_map/ppermute | solution.py:30

commit v8 on v6

--- a/solution.py
+++ b/solution.py
@@ -12,7 +12,7 @@
 NZ = LZ * HZ
 F32 = jnp.float32
 BF16 = jnp.bfloat16
-STEPS = (1, 3, 2, 0)
+STEPS = (3, 1, 2, 0)
 GROUPS = ((0,), (1,), (2,), (3,))
 DELTA_US, SUM_US, OWN_US = 0.0, 10.0, 10.0
 

time: 92.9 us -> 94.3 us (1.015)
  starting transfers between devices: 49.8 us -> 52 us
    ppermute x28, starting transfers between devices: 49.8 us -> 52 us  [move(): return lax.ppermute(array, AXES, pairs)]
where the time goes in v8:
time: 94.3 us; the launch traced here: 94.2 us
  starting transfers between devices  52 us (55%)
  waiting for transfers between devices  25.1 us (27%)
  Pallas kernels  16.8 us (18%)
    ppermute x28, starting transfers between devices, move(): return lax.ppermute(array, AXES, pairs)  52 us
    ppermute x28, waiting for transfers between devices, move(): return lax.ppermute(array, AXES, pairs)  25.1 us
    pallas_call x1, Pallas kernels, deltas(): pl.pallas_call(delta_kernel, name='deltas', in_specs=[pl.BlockSpec(memory...  9.78 us
    pallas_call x16, Pallas kernels, call(): pl.pallas_call(kernel, name=name, in_specs=[vmem] * len(operands), out_sp...  7.04 us
  transfers between devices with their start and end apart: 28, of which 12 were waited for; matrix products, arithmetic and copies ran while one was open for 0% of the time, Pallas kernels for 6%

profile of v8, /device:TPU:1, one launch (start us, length us, event | category | flops | bytes accessed | tf_op | source)
XLA Modules:
  0.0 94.2 jit_solution(14819542872685155585)
XLA Ops:
  0.0 9.8 %deltas.1 = (bf16[1,3,64,1024]{3,2,1,0:T(8,128)(2,1)S(1)}, bf16[1,3,64,1024]{3,2,1,0:T(8,128)(2,1)S(1)}, bf16[1,3,64,1024]{3,2,1,0:T(8,128)(2,1)S(1)}, bf16[1,3,...) custom-call(f32[1,1024]{1,0:T(1,128)} %rates.1, ...), custom_call_target="tpu_custom_call" | custom-call | flops 1 | bytes 1 | tf_op jit(solution)/shard_map/deltas/pallas_call | solution.py:137
  9.8 3.3 %collective-permute-start = (bf16[1,3,64,1024]{3,2,1,0:T(8,128)(2,1)S(1)}, bf16[1,3,64,1024]{3,2,1,0:T(8,128)(2,1)S(1)}, u32[]{:S(2)}, u32[]{:S(2)}) collective-permute-start(bf16[1,3,64,1024]{3,2,1,0:T(8,128)(2,1)S(1)} %get-tuple-element.31), channel_id=1, source_target_pairs={{0,16},{4,20},{8,24},{12,28},{16,0},{20,4},{24,8},{28,12},{32,48},... | collective-permute-start | bytes 1179656 | tf_op jit(solution)/shard_map/ppermute | solution.py:30
  13.1 0.1 collective-permute-start.2
  13.2 0.4 collective-permute-start.4
  13.6 0.1 collective-permute-start.6
  13.7 0.7 collective-permute-done.other
  14.5 0.1 add_cores.4
  14.6 2.4 %collective-permute-start.1 = (bf16[3,64,1024]{2,1,0:T(8,128)(2,1)S(1)}, bf16[3,64,1024]{2,1,0:T(8,128)(2,1)S(1)}, u32[]{:S(2)}, u32[]{:S(2)}) collective-permute-start(bf16[3,64,1024]{2,1,0:T(8,128)(2,1)S(1)} %add_cores.4), channel_id=1, source_target_pairs={{0,96},{4,100},{8,104},{12,108},{16,224},{20,228},{24,232},{28,236... | collective-permute-start | bytes 1179656 | tf_op jit(solution)/shard_map/ppermute | solution.py:30
  17.0 0.0 collective-permute-done.2.other
  17.0 0.1 add_cores.5
  17.1 0.4 collective-permute-start.3
  17.5 0.0 collective-permute-done.4.other
  17.5 0.1 add_cores.6
  17.6 2.7 %collective-permute-start.5 = (bf16[3,64,1024]{2,1,0:T(8,128)(2,1)S(1)}, bf16[3,64,1024]{2,1,0:T(8,128)(2,1)S(1)}, u32[]{:S(2)}, u32[]{:S(2)}) collective-permute-start(bf16[3,64,1024]{2,1,0:T(8,128)(2,1)S(1)} %add_cores.6), channel_id=1, source_target_pairs={{0,64},{4,68},{8,72},{12,76},{16,192},{20,196},{24,200},{28,204},{... | collective-permute-start | bytes 1179656 | tf_op jit(solution)/shard_map/ppermute | solution.py:30
  20.3 0.1 add_cores.7
  20.4 0.0 copy-start
  20.4 2.2 %collective-permute-start.7 = (bf16[3,64,1024]{2,1,0:T(8,128)(2,1)S(1)}, bf16[3,64,1024]{2,1,0:T(8,128)(2,1)S(1)}, u32[]{:S(2)}, u32[]{:S(2)}) collective-permute-start(bf16[3,64,1024]{2,1,0:T(8,128)(2,1)S(1)} %add_cores.7), channel_id=1, source_target_pairs={{0,0},{4,4},{8,8},{12,12},{16,128},{20,132},{24,136},{28,140},{32,... | collective-permute-start | bytes 1179656 | tf_op jit(solution)/shard_map/ppermute | solution.py:30
  22.5 0.5 collective-permute-done.1.refs_0_
  23.1 3.8 %collective-permute-done.3.refs_1_ = bf16[3,64,1024]{2,1,0:T(8,128)(2,1)S(1)} collective-permute-done((bf16[3,64,1024]{2,1,0:T(8,128)(2,1)S(1)}, bf16[3,64,1024]{2,1,0:T(8,128)(2,1)S(1)}, u32[]{:S(2)}, u32[]{:S(2)}) %collective-permute-start.3) | collective-permute-done | bytes 393248 | tf_op jit(solution)/shard_map/ppermute | solution.py:30
  26.9 4.4 %collective-permute-done.5.refs_2_ = bf16[3,64,1024]{2,1,0:T(8,128)(2,1)S(1)} collective-permute-done((bf16[3,64,1024]{2,1,0:T(8,128)(2,1)S(1)}, bf16[3,64,1024]{2,1,0:T(8,128)(2,1)S(1)}, u32[]{:S(2)}, u32[]{:S(2)}) %collective-permute-start.5) | collective-permute-done | bytes 393248 | tf_op jit(solution)/shard_map/ppermute | solution.py:30
  31.3 4.0 %collective-permute-done.7.refs_3_ = bf16[3,64,1024]{2,1,0:T(8,128)(2,1)S(1)} collective-permute-done((bf16[3,64,1024]{2,1,0:T(8,128)(2,1)S(1)}, bf16[3,64,1024]{2,1,0:T(8,128)(2,1)S(1)}, u32[]{:S(2)}, u32[]{:S(2)}) %collective-permute-start.7) | collective-permute-done | bytes 393248 | tf_op jit(solution)/shard_map/ppermute | solution.py:30
  35.3 0.2 sum_chips.1.mine
  35.5 2.8 %collective-permute-start.8 = (bf16[3,64,1024]{2,1,0:T(8,128)(2,1)S(1)}, bf16[3,64,1024]{2,1,0:T(8,128)(2,1)S(1)}, u32[]{:S(2)}, u32[]{:S(2)}) collective-permute-start(bf16[3,64,1024]{2,1,0:T(8,128)(2,1)S(1)} %sum_chips.1.mine), channel_id=1, source_target_pairs={{0,16},{4,20},{8,24},{12,28},{16,0},{20,4},{24,8},{28,12},{32,48},... | collective-permute-start | bytes 1179656 | tf_op jit(solution)/shard_map/ppermute | solution.py:30
  38.3 2.7 %collective-permute-start.15 = (bf16[256,1024]{1,0:T(8,128)(2,1)S(1)}, bf16[256,1024]{1,0:T(8,128)(2,1)S(1)}, u32[]{:S(2)}, u32[]{:S(2)}) collective-permute-start(bf16[256,1024]{1,0:T(8,128)(2,1)S(1)} %copy-done), channel_id=1, source_target_pairs={{0,96},{4,100},{8,104},{12,108},{16,112},{20,116},{24,120},{28,124... | collective-permute-start | bytes 1572872 | tf_op jit(solution)/shard_map/ppermute | solution.py:30
  41.0 0.0 collective-permute-done.8.other
  41.0 0.4 renorm.1
  41.4 3.9 %collective-permute-start.9 = (bf16[3,32,1024]{2,1,0:T(8,128)(2,1)S(1)}, bf16[3,32,1024]{2,1,0:T(8,128)(2,1)S(1)}, u32[]{:S(2)}, u32[]{:S(2)}) collective-permute-start(bf16[3,32,1024]{2,1,0:T(8,128)(2,1)S(1)} %get-tuple-element.42.refs_2_.refs_1_), channel_id=1, source_target_pairs={{0,128},{4,132},{8,136},{12,140},{16,156},{20,144},{24,148},{28,15... | collective-permute-start | bytes 589832 | tf_op jit(solution)/shard_map/ppermute | solution.py:30
  45.3 2.4 %collective-permute-start.10 = (bf16[3,32,1024]{2,1,0:T(8,128)(2,1)S(1)}, bf16[3,32,1024]{2,1,0:T(8,128)(2,1)S(1)}, u32[]{:S(2)}, u32[]{:S(2)}) collective-permute-start(bf16[3,32,1024]{2,1,0:T(8,128)(2,1)S(1)} %get-tuple-element.43.refs_3_.refs_2_), channel_id=1, source_target_pairs={{0,128},{4,132},{8,136},{12,140},{16,156},{20,144},{24,148},{28,15... | collective-permute-start | bytes 589832 | tf_op jit(solution)/shard_map/ppermute | solution.py:30
  47.7 0.2 collective-permute-done.9.refs_0_
  47.9 3.4 %collective-permute-start.11 = (bf16[3,32,1024]{2,1,0:T(8,128)(2,1)S(1)}, bf16[3,32,1024]{2,1,0:T(8,128)(2,1)S(1)}, u32[]{:S(2)}, u32[]{:S(2)}) collective-permute-start(bf16[3,32,1024]{2,1,0:T(8,128)(2,1)S(1)} %collective-permute-done.9.refs_0_), channel_id=1, source_target_pairs={{0,128},{4,132},{8,136},{12,140},{16,156},{20,144},{24,148},{28,15... | collective-permute-start | bytes 589832 | tf_op jit(solution)/shard_map/ppermute | solution.py:30
  51.3 2.4 %collective-permute-start.12 = (bf16[3,32,1024]{2,1,0:T(8,128)(2,1)S(1)}, bf16[3,32,1024]{2,1,0:T(8,128)(2,1)S(1)}, u32[]{:S(2)}, u32[]{:S(2)}) collective-permute-start(bf16[3,32,1024]{2,1,0:T(8,128)(2,1)S(1)} %collective-permute-done.10.refs_1_), channel_id=1, source_target_pairs={{0,128},{4,132},{8,136},{12,140},{16,156},{20,144},{24,148},{28,15... | collective-permute-start | bytes 589832 | tf_op jit(solution)/shard_map/ppermute | solution.py:30
  53.8 0.2 collective-permute-done.11.refs_2_
  53.9 3.4 %collective-permute-start.13 = (bf16[3,32,1024]{2,1,0:T(8,128)(2,1)S(1)}, bf16[3,32,1024]{2,1,0:T(8,128)(2,1)S(1)}, u32[]{:S(2)}, u32[]{:S(2)}) collective-permute-start(bf16[3,32,1024]{2,1,0:T(8,128)(2,1)S(1)} %collective-permute-done.11.refs_2_), channel_id=1, source_target_pairs={{0,128},{4,132},{8,136},{12,140},{16,156},{20,144},{24,148},{28,15... | collective-permute-start | bytes 589832 | tf_op jit(solution)/shard_map/ppermute | solution.py:30
  57.4 0.1 collective-permute-start.18
  57.4 0.0 collective-permute-done.15.refs_0_
  57.5 2.7 %collective-permute-start.16 = (bf16[128,1024]{1,0:T(8,128)(2,1)S(1)}, bf16[128,1024]{1,0:T(8,128)(2,1)S(1)}, u32[]{:S(2)}, u32[]{:S(2)}) collective-permute-start(bf16[128,1024]{1,0:T(8,128)(2,1)S(1)} %slice.8), channel_id=1, source_target_pairs={{0,96},{4,100},{8,104},{12,108},{16,112},{20,116},{24,120},{28,124... | collective-permute-start | bytes 786440 | tf_op jit(solution)/shard_map/ppermute | solution.py:30
  60.2 0.0 collective-permute-done.12.refs_3_
  60.2 0.0 collective-permute-start.14
  60.3 0.0 collective-permute-done.13.refs_0_
  60.3 2.8 %collective-permute-start.19 = (bf16[3,32,1024]{2,1,0:T(8,128)(2,1)S(1)}, bf16[3,32,1024]{2,1,0:T(8,128)(2,1)S(1)}, u32[]{:S(2)}, u32[]{:S(2)}) collective-permute-start(bf16[3,32,1024]{2,1,0:T(8,128)(2,1)S(1)} %collective-permute-done.13.refs_0_), channel_id=1, source_target_pairs={{0,128},{4,132},{8,136},{12,140},{16,156},{20,144},{24,148},{28,15... | collective-permute-start | bytes 589832 | tf_op jit(solution)/shard_map/ppermute | solution.py:30
  63.1 0.1 join.2.refs_4_.refs_3_
  63.1 1.5 %collective-permute-start.20 = (bf16[3,128,1024]{2,1,0:T(8,128)(2,1)S(1)}, bf16[3,128,1024]{2,1,0:T(8,128)(2,1)S(1)}, u32[]{:S(2)}, u32[]{:S(2)}) collective-permute-start(bf16[3,128,1024]{2,1,0:T(8,128)(2,1)S(1)} %join.2.refs_4_.refs_3_), channel_id=1, source_target_pairs={{0,16},{4,20},{8,24},{12,28},{16,0},{20,4},{24,8},{28,12},{32,48},... | collective-permute-start | bytes 2359304 | tf_op jit(solution)/shard_map/ppermute | solution.py:30
  64.6 2.1 %collective-permute-done.18.refs_1_ = bf16[128,1024]{1,0:T(8,128)(2,1)S(1)} collective-permute-done((bf16[128,1024]{1,0:T(8,128)(2,1)S(1)}, bf16[128,1024]{1,0:T(8,128)(2,1)S(1)}, u32[]{:S(2)}, u32[]{:S(2)}) %collective-permute-start.18) | collective-permute-done | bytes 262176 | tf_op jit(solution)/shard_map/ppermute | solution.py:30
  66.8 0.3 collective-permute-done.19.refs_2_
  67.1 3.9 %collective-permute-start.21 = (bf16[3,96,1024]{2,1,0:T(8,128)(2,1)S(1)}, bf16[3,96,1024]{2,1,0:T(8,128)(2,1)S(1)}, u32[]{:S(2)}, u32[]{:S(2)}) collective-permute-start(bf16[3,96,1024]{2,1,0:T(8,128)(2,1)S(1)} %join.3.refs_5_.refs_4_), channel_id=1, source_target_pairs={{0,16},{4,20},{8,24},{12,28},{16,0},{20,4},{24,8},{28,12},{32,48},... | collective-permute-start | bytes 1769480 | tf_op jit(solution)/shard_map/ppermute | solution.py:30
  71.0 1.0 %render_rows.5.refs_4_ = f32[256,1024]{1,0:T(8,128)S(1)} custom-call(bf16[128,1024]{1,0:T(8,128)(2,1)S(1)} %collective-permute-done.16.refs_0_, bf16[128,1024]{1,0:T(8,128)(2,1)S(1)} %collective-permute-done.18.refs_1_, bf16[3,32,1024]{2,1,0:T(8,128)(2,1)S(1)} %get-tuple-element.42.refs_2_.refs_1_, ...), custom_call_target="tpu_custom_call" | custom-call | flops 1 | bytes 1 | tf_op jit(solution)/shard_map/render_rows/pallas_call | solution.py:159
  72.0 0.6 collective-permute-done.21.refs_6_.refs_7_.refs_3_
  72.6 0.0 collective-permute-done.20.refs_5_.refs_6_.refs_2_
  72.6 0.7 render_rows.9
  73.3 0.1 collective-permute-start.24
  73.4 2.7 %collective-permute-start.25 = (bf16[128,1024]{1,0:T(8,128)(2,1)S(1)}, bf16[128,1024]{1,0:T(8,128)(2,1)S(1)}, u32[]{:S(2)}, u32[]{:S(2)}) collective-permute-start(bf16[128,1024]{1,0:T(8,128)(2,1)S(1)} %get-tuple-element.52), channel_id=1, source_target_pairs={{0,96},{4,100},{8,104},{12,108},{16,112},{20,116},{24,120},{28,124... | collective-permute-start | bytes 786440 | tf_op jit(solution)/shard_map/ppermute | solution.py:30
  76.1 1.1 %render_rows.7 = (bf16[128,1024]{1,0:T(8,128)(2,1)S(1)}, bf16[128,1024]{1,0:T(8,128)(2,1)S(1)}) custom-call(bf16[256,1024]{1,0:T(8,128)(2,1)S(1)} %collective-permute-done.15.refs_0_, bf16[256,1024]{1,0:T(8,128)(2,1)S(1)} %collective-permute-done.17.refs_1_, bf16[3,32,1024]{2,1,0:T(8,128)(2,1)S(1)} %get-tuple-element.42.refs_2_.refs_1_, ...), custom_call_target="tpu_custom_call" | custom-call | flops 1 | bytes 1 | tf_op jit(solution)/shard_map/render_rows/pallas_call | solution.py:159
  77.1 0.1 collective-permute-start.22
  77.2 2.7 %collective-permute-start.23 = (bf16[128,1024]{1,0:T(8,128)(2,1)S(1)}, bf16[128,1024]{1,0:T(8,128)(2,1)S(1)}, u32[]{:S(2)}, u32[]{:S(2)}) collective-permute-start(bf16[128,1024]{1,0:T(8,128)(2,1)S(1)} %get-tuple-element.49), channel_id=1, source_target_pairs={{0,96},{4,100},{8,104},{12,108},{16,112},{20,116},{24,120},{28,124... | collective-permute-start | bytes 786440 | tf_op jit(solution)/shard_map/ppermute | solution.py:30
  79.9 1.1 %render_rows.8.mid = f32[256,1024]{1,0:T(8,128)S(1)} custom-call(bf16[256,1024]{1,0:T(8,128)(2,1)S(1)} %collective-permute-done.15.refs_0_, bf16[256,1024]{1,0:T(8,128)(2,1)S(1)} %collective-permute-done.17.refs_1_, bf16[3,32,1024]{2,1,0:T(8,128)(2,1)S(1)} %get-tuple-element.42.refs_2_.refs_1_, bf16[3,32,1024]{2,1,0:T(8,128)(2,1)S(1)} %get-tuple-element.43.refs_3_.refs_2_, ...), custom_call_target="tpu_custom_call" | custom-call | flops 1 | bytes 1 | tf_op jit(solution)/shard_map/render_rows/pallas_call | solution.py:159
  81.0 1.1 %render_rows.6.own = f32[256,1024]{1,0:T(8,128)S(1)} custom-call(bf16[256,1024]{1,0:T(8,128)(2,1)S(1)} %copy-done, bf16[3,32,1024]{2,1,0:T(8,128)(2,1)S(1)} %get-tuple-element.42.refs_2_.refs_1_, bf16[3,32,1024]{2,1,0:T(8,128)(2,1)S(1)} %get-tuple-element.43.refs_3_.refs_2_, bf16[3,128,1024]{2,1,0:T(8,128)(2,1)S(1)} %join.2.refs_4_.refs_3_, ...), custom_call_target="tpu_custom_call" | custom-call | flops 1 | bytes 1 | tf_op jit(solution)/shard_map/render_rows/pallas_call | solution.py:159
  82.1 0.0 collective-permute-done.24.relay_left
  82.1 0.1 merge.1
  82.2 0.1 collective-permute-start.26
  82.3 2.7 %collective-permute-start.27 = (bf16[128,1024]{1,0:T(8,128)(2,1)S(1)}, bf16[128,1024]{1,0:T(8,128)(2,1)S(1)}, u32[]{:S(2)}, u32[]{:S(2)}) collective-permute-start(bf16[128,1024]{1,0:T(8,128)(2,1)S(1)} %get-tuple-element.54), channel_id=1, source_target_pairs={{0,96},{4,100},{8,104},{12,108},{16,112},{20,116},{24,120},{28,124... | collective-permute-start | bytes 786440 | tf_op jit(solution)/shard_map/ppermute | solution.py:30
  85.0 2.8 %collective-permute-done.22.from_left = bf16[128,1024]{1,0:T(8,128)(2,1)S(1)} collective-permute-done((bf16[128,1024]{1,0:T(8,128)(2,1)S(1)}, bf16[128,1024]{1,0:T(8,128)(2,1)S(1)}, u32[]{:S(2)}, u32[]{:S(2)}) %collective-permute-start.22) | collective-permute-done | bytes 262176 | tf_op jit(solution)/shard_map/ppermute | solution.py:30
  87.7 0.1 own.1
  87.8 5.5 %collective-permute-done.26.last_left = bf16[128,1024]{1,0:T(8,128)(2,1)S(1)} collective-permute-done((bf16[128,1024]{1,0:T(8,128)(2,1)S(1)}, bf16[128,1024]{1,0:T(8,128)(2,1)S(1)}, u32[]{:S(2)}, u32[]{:S(2)}) %collective-permute-start.26) | collective-permute-done | bytes 262176 | tf_op jit(solution)/shard_map/ppermute | solution.py:30
  93.3 0.9 total.1
  (13 shorter events, 0.1 us)
Async XLA Ops:
  9.8 4.7 %collective-permute-start = (bf16[1,3,64,1024]{3,2,1,0:T(8,128)(2,1)S(1)}, bf16[1,3,64,1024]{3,2,1,0:T(8,128)(2,1)S(1)}, u32[]{:S(2)}, u32[]{:S(2)}) collective-permute-start(bf16[1,3,64,1024]{3,2,1,0:T(8,128)(2,1)S(1)} %get-tuple-element.31), channel_id=1, source_target_pairs={{0,16},{4,20},{8,24},{12,28},{16,0},{20,4},{24,8},{28,12},{32,48},... | collective-permute-start | bytes 1179656 | tf_op jit(solution)/shard_map/ppermute | solution.py:30
  13.1 3.9 %collective-permute-start.2 = (bf16[1,3,64,1024]{3,2,1,0:T(8,128)(2,1)S(1)}, bf16[1,3,64,1024]{3,2,1,0:T(8,128)(2,1)S(1)}, u32[]{:S(2)}, u32[]{:S(2)}) collective-permute-start(bf16[1,3,64,1024]{3,2,1,0:T(8,128)(2,1)S(1)} %get-tuple-element.33), channel_id=1, source_target_pairs={{0,16},{4,20},{8,24},{12,28},{16,0},{20,4},{24,8},{28,12},{32,48},... | collective-permute-start | bytes 1179656 | tf_op jit(solution)/shard_map/ppermute | solution.py:30
  13.2 4.2 %collective-permute-start.4 = (bf16[1,3,64,1024]{3,2,1,0:T(8,128)(2,1)S(1)}, bf16[1,3,64,1024]{3,2,1,0:T(8,128)(2,1)S(1)}, u32[]{:S(2)}, u32[]{:S(2)}) collective-permute-start(bf16[1,3,64,1024]{3,2,1,0:T(8,128)(2,1)S(1)} %get-tuple-element.39), channel_id=1, source_target_pairs={{0,16},{4,20},{8,24},{12,28},{16,0},{20,4},{24,8},{28,12},{32,48},... | collective-permute-start | bytes 1179656 | tf_op jit(solution)/shard_map/ppermute | solution.py:30
  13.6 6.6 %collective-permute-start.6 = (bf16[1,3,64,1024]{3,2,1,0:T(8,128)(2,1)S(1)}, bf16[1,3,64,1024]{3,2,1,0:T(8,128)(2,1)S(1)}, u32[]{:S(2)}, u32[]{:S(2)}) collective-permute-start(bf16[1,3,64,1024]{3,2,1,0:T(8,128)(2,1)S(1)} %get-tuple-element.41), channel_id=1, source_target_pairs={{0,16},{4,20},{8,24},{12,28},{16,0},{20,4},{24,8},{28,12},{32,48},... | collective-permute-start | bytes 1179656 | tf_op jit(solution)/shard_map/ppermute | solution.py:30
  14.6 8.5 %collective-permute-start.1 = (bf16[3,64,1024]{2,1,0:T(8,128)(2,1)S(1)}, bf16[3,64,1024]{2,1,0:T(8,128)(2,1)S(1)}, u32[]{:S(2)}, u32[]{:S(2)}) collective-permute-start(bf16[3,64,1024]{2,1,0:T(8,128)(2,1)S(1)} %add_cores.4), channel_id=1, source_target_pairs={{0,96},{4,100},{8,104},{12,108},{16,224},{20,228},{24,232},{28,236... | collective-permute-start | bytes 1179656 | tf_op jit(solution)/shard_map/ppermute | solution.py:30
  17.1 9.8 %collective-permute-start.3 = (bf16[3,64,1024]{2,1,0:T(8,128)(2,1)S(1)}, bf16[3,64,1024]{2,1,0:T(8,128)(2,1)S(1)}, u32[]{:S(2)}, u32[]{:S(2)}) collective-permute-start(bf16[3,64,1024]{2,1,0:T(8,128)(2,1)S(1)} %add_cores.5), channel_id=1, source_target_pairs={{0,32},{4,36},{8,40},{12,44},{16,160},{20,164},{24,168},{28,172},{... | collective-permute-start | bytes 1179656 | tf_op jit(solution)/shard_map/ppermute | solution.py:30
  17.6 13.8 %collective-permute-start.5 = (bf16[3,64,1024]{2,1,0:T(8,128)(2,1)S(1)}, bf16[3,64,1024]{2,1,0:T(8,128)(2,1)S(1)}, u32[]{:S(2)}, u32[]{:S(2)}) collective-permute-start(bf16[3,64,1024]{2,1,0:T(8,128)(2,1)S(1)} %add_cores.6), channel_id=1, source_target_pairs={{0,64},{4,68},{8,72},{12,76},{16,192},{20,196},{24,200},{28,204},{... | collective-permute-start | bytes 1179656 | tf_op jit(solution)/shard_map/ppermute | solution.py:30
  20.4 17.9 %copy-start = (bf16[256,1024]{1,0:T(8,128)(2,1)S(1)}, bf16[256,1024]{1,0:T(8,128)(2,1)}, u32[]{:S(2)}) copy-start(bf16[256,1024]{1,0:T(8,128)(2,1)} %refs_0_) | copy-start | bytes 1572868
  20.4 14.9 %collective-permute-start.7 = (bf16[3,64,1024]{2,1,0:T(8,128)(2,1)S(1)}, bf16[3,64,1024]{2,1,0:T(8,128)(2,1)S(1)}, u32[]{:S(2)}, u32[]{:S(2)}) collective-permute-start(bf16[3,64,1024]{2,1,0:T(8,128)(2,1)S(1)} %add_cores.7), channel_id=1, source_target_pairs={{0,0},{4,4},{8,8},{12,12},{16,128},{20,132},{24,136},{28,140},{32,... | collective-permute-start | bytes 1179656 | tf_op jit(solution)/shard_map/ppermute | solution.py:30
  35.5 5.5 %collective-permute-start.8 = (bf16[3,64,1024]{2,1,0:T(8,128)(2,1)S(1)}, bf16[3,64,1024]{2,1,0:T(8,128)(2,1)S(1)}, u32[]{:S(2)}, u32[]{:S(2)}) collective-permute-start(bf16[3,64,1024]{2,1,0:T(8,128)(2,1)S(1)} %sum_chips.1.mine), channel_id=1, source_target_pairs={{0,16},{4,20},{8,24},{12,28},{16,0},{20,4},{24,8},{28,12},{32,48},... | collective-permute-start | bytes 1179656 | tf_op jit(solution)/shard_map/ppermute | solution.py:30
  38.3 19.0 %collective-permute-start.17 = (bf16[256,1024]{1,0:T(8,128)(2,1)S(1)}, bf16[256,1024]{1,0:T(8,128)(2,1)S(1)}, u32[]{:S(2)}, u32[]{:S(2)}) collective-permute-start(bf16[256,1024]{1,0:T(8,128)(2,1)S(1)} %copy-done), channel_id=1, source_target_pairs={{0,32},{4,36},{8,40},{12,44},{16,48},{20,52},{24,56},{28,60},{32,6... | collective-permute-start | bytes 1572872 | tf_op jit(solution)/shard_map/ppermute | solution.py:30
  38.3 19.1 %collective-permute-start.15 = (bf16[256,1024]{1,0:T(8,128)(2,1)S(1)}, bf16[256,1024]{1,0:T(8,128)(2,1)S(1)}, u32[]{:S(2)}, u32[]{:S(2)}) collective-permute-start(bf16[256,1024]{1,0:T(8,128)(2,1)S(1)} %copy-done), channel_id=1, source_target_pairs={{0,96},{4,100},{8,104},{12,108},{16,112},{20,116},{24,120},{28,124... | collective-permute-start | bytes 1572872 | tf_op jit(solution)/shard_map/ppermute | solution.py:30
  41.4 6.5 %collective-permute-start.9 = (bf16[3,32,1024]{2,1,0:T(8,128)(2,1)S(1)}, bf16[3,32,1024]{2,1,0:T(8,128)(2,1)S(1)}, u32[]{:S(2)}, u32[]{:S(2)}) collective-permute-start(bf16[3,32,1024]{2,1,0:T(8,128)(2,1)S(1)} %get-tuple-element.42.refs_2_.refs_1_), channel_id=1, source_target_pairs={{0,128},{4,132},{8,136},{12,140},{16,156},{20,144},{24,148},{28,15... | collective-permute-start | bytes 589832 | tf_op jit(solution)/shard_map/ppermute | solution.py:30
  45.3 6.0 %collective-permute-start.10 = (bf16[3,32,1024]{2,1,0:T(8,128)(2,1)S(1)}, bf16[3,32,1024]{2,1,0:T(8,128)(2,1)S(1)}, u32[]{:S(2)}, u32[]{:S(2)}) collective-permute-start(bf16[3,32,1024]{2,1,0:T(8,128)(2,1)S(1)} %get-tuple-element.43.refs_3_.refs_2_), channel_id=1, source_target_pairs={{0,128},{4,132},{8,136},{12,140},{16,156},{20,144},{24,148},{28,15... | collective-permute-start | bytes 589832 | tf_op jit(solution)/shard_map/ppermute | solution.py:30
  47.9 6.0 %collective-permute-start.11 = (bf16[3,32,1024]{2,1,0:T(8,128)(2,1)S(1)}, bf16[3,32,1024]{2,1,0:T(8,128)(2,1)S(1)}, u32[]{:S(2)}, u32[]{:S(2)}) collective-permute-start(bf16[3,32,1024]{2,1,0:T(8,128)(2,1)S(1)} %collective-permute-done.9.refs_0_), channel_id=1, source_target_pairs={{0,128},{4,132},{8,136},{12,140},{16,156},{20,144},{24,148},{28,15... | collective-permute-start | bytes 589832 | tf_op jit(solution)/shard_map/ppermute | solution.py:30
  51.3 8.9 %collective-permute-start.12 = (bf16[3,32,1024]{2,1,0:T(8,128)(2,1)S(1)}, bf16[3,32,1024]{2,1,0:T(8,128)(2,1)S(1)}, u32[]{:S(2)}, u32[]{:S(2)}) collective-permute-start(bf16[3,32,1024]{2,1,0:T(8,128)(2,1)S(1)} %collective-permute-done.10.refs_1_), channel_id=1, source_target_pairs={{0,128},{4,132},{8,136},{12,140},{16,156},{20,144},{24,148},{28,15... | collective-permute-start | bytes 589832 | tf_op jit(solution)/shard_map/ppermute | solution.py:30
  53.9 6.3 %collective-permute-start.13 = (bf16[3,32,1024]{2,1,0:T(8,128)(2,1)S(1)}, bf16[3,32,1024]{2,1,0:T(8,128)(2,1)S(1)}, u32[]{:S(2)}, u32[]{:S(2)}) collective-permute-start(bf16[3,32,1024]{2,1,0:T(8,128)(2,1)S(1)} %collective-permute-done.11.refs_2_), channel_id=1, source_target_pairs={{0,128},{4,132},{8,136},{12,140},{16,156},{20,144},{24,148},{28,15... | collective-permute-start | bytes 589832 | tf_op jit(solution)/shard_map/ppermute | solution.py:30
  57.4 9.4 %collective-permute-start.18 = (bf16[128,1024]{1,0:T(8,128)(2,1)S(1)}, bf16[128,1024]{1,0:T(8,128)(2,1)S(1)}, u32[]{:S(2)}, u32[]{:S(2)}) collective-permute-start(bf16[128,1024]{1,0:T(8,128)(2,1)S(1)} %slice.9), channel_id=1, source_target_pairs={{0,32},{4,36},{8,40},{12,44},{16,48},{20,52},{24,56},{28,60},{32,6... | collective-permute-start | bytes 786440 | tf_op jit(solution)/shard_map/ppermute | solution.py:30
  57.5 9.3 %collective-permute-start.16 = (bf16[128,1024]{1,0:T(8,128)(2,1)S(1)}, bf16[128,1024]{1,0:T(8,128)(2,1)S(1)}, u32[]{:S(2)}, u32[]{:S(2)}) collective-permute-start(bf16[128,1024]{1,0:T(8,128)(2,1)S(1)} %slice.8), channel_id=1, source_target_pairs={{0,96},{4,100},{8,104},{12,108},{16,112},{20,116},{24,120},{28,124... | collective-permute-start | bytes 786440 | tf_op jit(solution)/shard_map/ppermute | solution.py:30
  60.2 6.5 %collective-permute-start.14 = (bf16[3,32,1024]{2,1,0:T(8,128)(2,1)S(1)}, bf16[3,32,1024]{2,1,0:T(8,128)(2,1)S(1)}, u32[]{:S(2)}, u32[]{:S(2)}) collective-permute-start(bf16[3,32,1024]{2,1,0:T(8,128)(2,1)S(1)} %collective-permute-done.12.refs_3_), channel_id=1, source_target_pairs={{0,128},{4,132},{8,136},{12,140},{16,156},{20,144},{24,148},{28,15... | collective-permute-start | bytes 589832 | tf_op jit(solution)/shard_map/ppermute | solution.py:30
  60.3 6.8 %collective-permute-start.19 = (bf16[3,32,1024]{2,1,0:T(8,128)(2,1)S(1)}, bf16[3,32,1024]{2,1,0:T(8,128)(2,1)S(1)}, u32[]{:S(2)}, u32[]{:S(2)}) collective-permute-start(bf16[3,32,1024]{2,1,0:T(8,128)(2,1)S(1)} %collective-permute-done.13.refs_0_), channel_id=1, source_target_pairs={{0,128},{4,132},{8,136},{12,140},{16,156},{20,144},{24,148},{28,15... | collective-permute-start | bytes 589832 | tf_op jit(solution)/shard_map/ppermute | solution.py:30
  63.1 9.5 %collective-permute-start.20 = (bf16[3,128,1024]{2,1,0:T(8,128)(2,1)S(1)}, bf16[3,128,1024]{2,1,0:T(8,128)(2,1)S(1)}, u32[]{:S(2)}, u32[]{:S(2)}) collective-permute-start(bf16[3,128,1024]{2,1,0:T(8,128)(2,1)S(1)} %join.2.refs_4_.refs_3_), channel_id=1, source_target_pairs={{0,16},{4,20},{8,24},{12,28},{16,0},{20,4},{24,8},{28,12},{32,48},... | collective-permute-start | bytes 2359304 | tf_op jit(solution)/shard_map/ppermute | solution.py:30
  67.1 5.5 %collective-permute-start.21 = (bf16[3,96,1024]{2,1,0:T(8,128)(2,1)S(1)}, bf16[3,96,1024]{2,1,0:T(8,128)(2,1)S(1)}, u32[]{:S(2)}, u32[]{:S(2)}) collective-permute-start(bf16[3,96,1024]{2,1,0:T(8,128)(2,1)S(1)} %join.3.refs_5_.refs_4_), channel_id=1, source_target_pairs={{0,16},{4,20},{8,24},{12,28},{16,0},{20,4},{24,8},{28,12},{32,48},... | collective-permute-start | bytes 1769480 | tf_op jit(solution)/shard_map/ppermute | solution.py:30
  73.3 8.8 %collective-permute-start.24 = (bf16[128,1024]{1,0:T(8,128)(2,1)S(1)}, bf16[128,1024]{1,0:T(8,128)(2,1)S(1)}, u32[]{:S(2)}, u32[]{:S(2)}) collective-permute-start(bf16[128,1024]{1,0:T(8,128)(2,1)S(1)} %get-tuple-element.51), channel_id=1, source_target_pairs={{0,32},{4,36},{8,40},{12,44},{16,48},{20,52},{24,56},{28,60},{32,6... | collective-permute-start | bytes 786440 | tf_op jit(solution)/shard_map/ppermute | solution.py:30
  73.4 8.7 %collective-permute-start.25 = (bf16[128,1024]{1,0:T(8,128)(2,1)S(1)}, bf16[128,1024]{1,0:T(8,128)(2,1)S(1)}, u32[]{:S(2)}, u32[]{:S(2)}) collective-permute-start(bf16[128,1024]{1,0:T(8,128)(2,1)S(1)} %get-tuple-element.52), channel_id=1, source_target_pairs={{0,96},{4,100},{8,104},{12,108},{16,112},{20,116},{24,120},{28,124... | collective-permute-start | bytes 786440 | tf_op jit(solution)/shard_map/ppermute | solution.py:30
  77.1 10.6 %collective-permute-start.22 = (bf16[128,1024]{1,0:T(8,128)(2,1)S(1)}, bf16[128,1024]{1,0:T(8,128)(2,1)S(1)}, u32[]{:S(2)}, u32[]{:S(2)}) collective-permute-start(bf16[128,1024]{1,0:T(8,128)(2,1)S(1)} %get-tuple-element.48), channel_id=1, source_target_pairs={{0,32},{4,36},{8,40},{12,44},{16,48},{20,52},{24,56},{28,60},{32,6... | collective-permute-start | bytes 786440 | tf_op jit(solution)/shard_map/ppermute | solution.py:30
  77.2 10.5 %collective-permute-start.23 = (bf16[128,1024]{1,0:T(8,128)(2,1)S(1)}, bf16[128,1024]{1,0:T(8,128)(2,1)S(1)}, u32[]{:S(2)}, u32[]{:S(2)}) collective-permute-start(bf16[128,1024]{1,0:T(8,128)(2,1)S(1)} %get-tuple-element.49), channel_id=1, source_target_pairs={{0,96},{4,100},{8,104},{12,108},{16,112},{20,116},{24,120},{28,124... | collective-permute-start | bytes 786440 | tf_op jit(solution)/shard_map/ppermute | solution.py:30
  82.2 11.1 %collective-permute-start.26 = (bf16[128,1024]{1,0:T(8,128)(2,1)S(1)}, bf16[128,1024]{1,0:T(8,128)(2,1)S(1)}, u32[]{:S(2)}, u32[]{:S(2)}) collective-permute-start(bf16[128,1024]{1,0:T(8,128)(2,1)S(1)} %get-tuple-element.53), channel_id=1, source_target_pairs={{0,32},{4,36},{8,40},{12,44},{16,48},{20,52},{24,56},{28,60},{32,6... | collective-permute-start | bytes 786440 | tf_op jit(solution)/shard_map/ppermute | solution.py:30
  82.3 11.0 %collective-permute-start.27 = (bf16[128,1024]{1,0:T(8,128)(2,1)S(1)}, bf16[128,1024]{1,0:T(8,128)(2,1)S(1)}, u32[]{:S(2)}, u32[]{:S(2)}) collective-permute-start(bf16[128,1024]{1,0:T(8,128)(2,1)S(1)} %get-tuple-element.54), channel_id=1, source_target_pairs={{0,96},{4,100},{8,104},{12,108},{16,112},{20,116},{24,120},{28,124... | collective-permute-start | bytes 786440 | tf_op jit(solution)/shard_map/ppermute | solution.py:30
